TPU v7x, 32 devices: a whole 2x2x4 slice. The times are simulated.
32 devices in a mesh: dp: 8 (over z, x), tensor: 4 (over y, core).
Axes of the slice: x: 2, y: 2, z: 4, core: 2. Of those that a mesh axis runs over, the one named last changes fastest.
Arguments:
- activations: bfloat16 [1024, 14336], P('dp', 'tensor'), may hold values from -6 to 6
- in_basis: bfloat16 [14336, 8192], P('tensor', 'dp'), may hold values from -0.046875 to 0.046875
- out_grads: bfloat16 [1024, 4096], P('dp', 'tensor'), may hold values from -6 to 6
- out_basis: bfloat16 [4096, 4096], P(None, 'tensor'), may hold values from -0.09375 to 0.09375
- doc_lengths: int32 [8], replicated, may hold values from 1 to 256, 1024 in all
Outputs:
- corrections: float32 [8192, 4096], P('dp', 'tensor')
Inputs may be any that keep to these rules, and one draw needn't show every extreme that they name: `doc_lengths`: 8 lengths that sum to 1024; the longest is exactly 256.
All inputs are finite; a program needn't handle non-finite values.
Results may differ from a plain program's by a relative error of at most 0.0018.
Values may be sent and summed in bfloat16 or wider, within the bound.
No kernel may reach another device: no remote copies, remote signals or barrier semaphores. Data moves between devices by JAX's collectives and lax.ppermute only.
A program may use at most 64 MiB of HBM per device.

v0:
```python
import jax
import jax.numpy as jnp
from jax import lax
from jax.sharding import PartitionSpec as P

MAXLEN = 256


def document_squares(rotated, grad_rows, doc_lengths, window, group):
    starts = jnp.cumsum(doc_lengths) - doc_lengths
    pad_in = jnp.concatenate([rotated, jnp.zeros((window, rotated.shape[1]), rotated.dtype)], 0)
    pad_out = jnp.concatenate(
        [grad_rows, jnp.zeros((window, grad_rows.shape[1]), grad_rows.dtype)], 0
    )
    offsets = jnp.arange(window, dtype=jnp.int32)

    def window_at(padded, begin):
        return lax.dynamic_slice_in_dim(padded, begin, window, 0)

    def advance(running, inputs_pair):
        begins, lengths = inputs_pair
        left_rows = jax.vmap(window_at, in_axes=(None, 0))(pad_in, begins)
        right_rows = jax.vmap(window_at, in_axes=(None, 0))(pad_out, begins)
        row_mask = (offsets[None, :] < lengths[:, None]).astype(left_rows.dtype)
        left_rows = left_rows * row_mask[:, :, None]
        blocks = jnp.einsum(
            "gtj,gtk->gjk", left_rows, right_rows, preferred_element_type=jnp.float32
        )
        return (running + jnp.sum(blocks * blocks, axis=0), None)

    initial = jnp.zeros((rotated.shape[1], grad_rows.shape[1]), jnp.float32)
    grouped = (starts.reshape(-1, group), doc_lengths.reshape(-1, group))
    summed, unused = lax.scan(advance, initial, grouped)
    return summed


def local(activations, in_basis, out_grads, out_basis, doc_lengths):
    all_rows = lax.all_gather(activations, "dp", axis=0, tiled=True)
    partial_value = jnp.dot(all_rows, in_basis, preferred_element_type=jnp.float32)
    rotated = lax.psum(partial_value, "tensor").astype(jnp.bfloat16)
    features = lax.all_gather(out_grads, "tensor", axis=1, tiled=True)
    local_grads = jnp.dot(features, out_basis, preferred_element_type=jnp.float32).astype(
        jnp.bfloat16
    )
    grad_rows = lax.all_gather(local_grads, "dp", axis=0, tiled=True)
    summed = document_squares(rotated, grad_rows, doc_lengths, MAXLEN, 4)
    return summed / jnp.float32(rotated.shape[0])


def solution(mesh):
    placed = (P("dp", "tensor"), P("tensor", "dp"), P("dp", "tensor"), P(None, "tensor"), P())
    return jax.shard_map(
        local, mesh=mesh, in_specs=placed, out_specs=P("dp", "tensor"), check_vma=False
    )
```

profile of v0, /device:TPU:0, one launch (start us, length us, event | category | flops | bytes accessed | tf_op | source)
XLA Modules:
  0.0 377.0 jit_solution(14659491513847896567)
XLA Ops:
  6.5 0.7 all-gather.6.cloned.1.call-update
  7.3 21.1 %all-gather.6.cloned.1.call-done = bf16[128,4096]{1,0:T(8,128)(2,1)} async-done(((bf16[128,1024]{1,0:T(8,128)(2,1)}), bf16[128,4096]{1,0:T(8,128)(2,1)}) %all-gather.6.cloned.1.call-update) | async-done | bytes 1048592 | tf_op jit(solution)/shard_map/all_gather | solution.py:41
  28.4 5.7 %convolution_convert_fusion = bf16[128,1024]{1,0:T(8,128)(2,1)} fusion(bf16[128,4096]{1,0:T(8,128)(2,1)} %all-gather.6.cloned.1.call-done, bf16[4096,1024]{1,0:T(8,128)(2,1)} %param.10), kind=kOutput, calls=%fused_computation.14 | convolution fusion | flops 1073872896 | bytes 9699328 | tf_op jit(solution)/shard_map/dot_general | solution.py:42
  34.1 0.7 all-gather.4.cloned.1.call-update
  35.2 48.3 %all-gather.8.cloned.1.call-done = bf16[1024,1024]{1,0:T(8,128)(2,1)} async-done(((bf16[128,1024]{1,0:T(8,128)(2,1)}), bf16[1024,1024]{1,0:T(8,128)(2,1)}) %all-gather.8.cloned.1.call-update) | async-done | bytes 2097168 | tf_op jit(solution)/shard_map/all_gather | solution.py:45
  83.5 1.9 concatenate.11
  85.4 110.8 %all-gather.4.cloned.1.call-done = bf16[1024,3584]{1,0:T(8,128)(2,1)} async-done(((bf16[128,3584]{1,0:T(8,128)(2,1)}), bf16[1024,3584]{1,0:T(8,128)(2,1)}) %all-gather.4.cloned.1.call-update) | async-done | bytes 7340048 | tf_op jit(solution)/shard_map/all_gather | solution.py:38
  196.2 13.4 %fusion.5 = f32[1024,1024]{1,0:T(8,128)} fusion(bf16[1024,3584]{1,0:T(8,128)(2,1)} %all-gather.4.cloned.1.call-done, bf16[3584,1024]{1,0:T(8,128)(2,1)} %param.8), kind=kOutput, calls=%fused_computation.16 | convolution fusion | flops 7516192768 | bytes 18874368 | tf_op jit(solution)/shard_map/dot_general | solution.py:39
  209.7 76.5 %all-reduce.4 = bf16[1024,1024]{1,0:T(8,128)(2,1)} all-reduce(f32[1024,1024]{1,0:T(8,128)} %fusion.5), channel_id=1, replica_groups=mesh['dp'=8,'tensor'=4] {'tensor'}, use_global_device_ids=true, to_apply=%region_1.0 | all-reduce | flops 1048576 | bytes 6291456 | tf_op jit(solution)/shard_map/psum | solution.py:40
  286.2 3.4 concatenate.10
  289.6 75.8 %while.19 = (s32[]{:T(128)}, f32[1024,1024]{1,0:T(8,128)}, s32[2,4]{1,0:T(2,128)S(1)}, bf16[1280,1024]{1,0:T(8,128)(2,1)}, s32[2,4]{1,0:T(2,128)S(1)}, /*index=5...) while((s32[]{:T(128)}, f32[1024,1024]{1,0:T(8,128)}, ...), condition=%wide.region_4.5_spmd.clone, body=%wide.region_2.4_spmd.clone.sunk | while | flops 2157971456 | bytes 27269656 | solution.py:33
  289.6 1.7 broadcast.93.clone
  291.3 8.2 %while.20 = (s32[]{:T(128)}, bf16[1280,1024]{1,0:T(8,128)(2,1)S(1)}, s32[4,2]{0,1:T(2,128)S(1)}, bf16[4,256,1024]{2,1,0:T(8,128)(2,1)}, s32[]{:T(128)}) while((s32[]{:T(128)}, bf16[1280,1024]{1,0:T(8,128)(2,1)S(1)}, s32[4,2]{0,1:T(2,128)S(1)}, bf16[4,256,1024]{2,1,0:T(8,128)(2,1)}, s32[]{:T(128)}) %tuple.54), condition=%wide.while_cond.1, body=%wide.while_body.1.sunk | while | flops 2 | bytes 1049689 | solution.py:18
  291.9 1.5 bitcast_dynamic-update-slice_fusion.4
  293.9 1.5 bitcast_dynamic-update-slice_fusion.4
  295.9 1.5 bitcast_dynamic-update-slice_fusion.4
  298.0 1.5 bitcast_dynamic-update-slice_fusion.4
  299.5 1.6 broadcast.93.clone.1
  301.2 12.9 %while.21 = (s32[]{:T(128)}, bf16[1280,1024]{1,0:T(8,128)(2,1)}, s32[4,2]{0,1:T(2,128)S(1)}, bf16[4,256,1024]{2,1,0:T(8,128)(2,1)}, s32[]{:T(128)}) while((s32[]{:T(128)}, bf16[1280,1024]{1,0:T(8,128)(2,1)}, s32[4,2]{0,1:T(2,128)S(1)}, bf16[4,256,1024]{2,1,0:T(8,128)(2,1)}, s32[]{:T(128)}) %tuple.69), condition=%wide.while_cond, body=%wide.while_body.sunk | while | flops 2 | bytes 1049689 | solution.py:18
  301.3 0.5 slice.25
  301.8 2.6 bitcast_dynamic-update-slice_fusion.5
  304.5 0.5 slice.25
  305.1 2.6 bitcast_dynamic-update-slice_fusion.5
  307.7 0.5 slice.25
  308.3 2.6 bitcast_dynamic-update-slice_fusion.5
  310.9 0.5 slice.25
  311.5 2.6 bitcast_dynamic-update-slice_fusion.5
  314.2 7.1 %multiply_reduce_fusion.2 = f32[1024,1024]{1,0:T(8,128)} fusion(bf16[4,256,1024]{2,1,0:T(8,128)(2,1)} %get-tuple-element.209, bf16[4,256,1024]{2,1,0:T(8,128)(2,1)} %get-tuple-element.210, bf16[4,256]{1,0:T(4,128)(2,1)S(1)} %fusion.16), kind=kOutput, calls=%fused_computation.5.clone.1 | convolution fusion | flops 2155872256 | bytes 8390656 | tf_op jit(solution)/shard_map/while/body/eval_jaxpr/gtj,gtk->gjk/dot_general | solution.py:26
  321.3 5.6 %select_add_fusion.2 = f32[1024,1024]{1,0:T(8,128)} fusion(f32[1024,1024]{1,0:T(8,128)} %multiply_reduce_fusion.2, f32[1024,1024]{1,0:T(8,128)} %get-tuple-element.262, pred[]{:T(512)S(6)} %compare.10), kind=kLoop, calls=%fused_computation.6.clone.1 | loop fusion | flops 2097152 | bytes 12582913 | tf_op jit(solution)/shard_map/while/body/eval_jaxpr/add | solution.py:29
  326.9 1.7 broadcast.93.clone
  328.6 8.2 %while.20 = (s32[]{:T(128)}, bf16[1280,1024]{1,0:T(8,128)(2,1)S(1)}, s32[4,2]{0,1:T(2,128)S(1)}, bf16[4,256,1024]{2,1,0:T(8,128)(2,1)}, s32[]{:T(128)}) while((s32[]{:T(128)}, bf16[1280,1024]{1,0:T(8,128)(2,1)S(1)}, s32[4,2]{0,1:T(2,128)S(1)}, bf16[4,256,1024]{2,1,0:T(8,128)(2,1)}, s32[]{:T(128)}) %tuple.54), condition=%wide.while_cond.1, body=%wide.while_body.1.sunk | while | flops 2 | bytes 1049689 | solution.py:18
  329.2 1.5 bitcast_dynamic-update-slice_fusion.4
  331.2 1.5 bitcast_dynamic-update-slice_fusion.4
  333.2 1.5 bitcast_dynamic-update-slice_fusion.4
  335.3 1.5 bitcast_dynamic-update-slice_fusion.4
  336.8 1.6 broadcast.93.clone.1
  338.5 12.9 %while.21 = (s32[]{:T(128)}, bf16[1280,1024]{1,0:T(8,128)(2,1)}, s32[4,2]{0,1:T(2,128)S(1)}, bf16[4,256,1024]{2,1,0:T(8,128)(2,1)}, s32[]{:T(128)}) while((s32[]{:T(128)}, bf16[1280,1024]{1,0:T(8,128)(2,1)}, s32[4,2]{0,1:T(2,128)S(1)}, bf16[4,256,1024]{2,1,0:T(8,128)(2,1)}, s32[]{:T(128)}) %tuple.69), condition=%wide.while_cond, body=%wide.while_body.sunk | while | flops 2 | bytes 1049689 | solution.py:18
  338.5 0.5 slice.25
  339.1 2.6 bitcast_dynamic-update-slice_fusion.5
  341.8 0.5 slice.25
  342.3 2.6 bitcast_dynamic-update-slice_fusion.5
  345.0 0.5 slice.25
  345.5 2.6 bitcast_dynamic-update-slice_fusion.5
  348.2 0.5 slice.25
  348.8 2.6 bitcast_dynamic-update-slice_fusion.5
  351.5 7.1 %multiply_reduce_fusion.2 = f32[1024,1024]{1,0:T(8,128)} fusion(bf16[4,256,1024]{2,1,0:T(8,128)(2,1)} %get-tuple-element.209, bf16[4,256,1024]{2,1,0:T(8,128)(2,1)} %get-tuple-element.210, bf16[4,256]{1,0:T(4,128)(2,1)S(1)} %fusion.16), kind=kOutput, calls=%fused_computation.5.clone.1 | convolution fusion | flops 2155872256 | bytes 8390656 | tf_op jit(solution)/shard_map/while/body/eval_jaxpr/gtj,gtk->gjk/dot_general | solution.py:26
  358.6 6.9 %select_add_fusion.2 = f32[1024,1024]{1,0:T(8,128)} fusion(f32[1024,1024]{1,0:T(8,128)} %multiply_reduce_fusion.2, f32[1024,1024]{1,0:T(8,128)} %get-tuple-element.262, pred[]{:T(512)S(6)} %compare.10), kind=kLoop, calls=%fused_computation.6.clone.1 | loop fusion | flops 2097152 | bytes 12582913 | tf_op jit(solution)/shard_map/while/body/eval_jaxpr/add | solution.py:29
  365.5 5.0 %broadcast_multiply_fusion = f32[1024,1024]{1,0:T(8,128)} fusion(f32[1024,1024]{1,0:T(8,128)} %get-tuple-element.42), kind=kLoop, calls=%fused_computation.13 | loop fusion | flops 1048576 | bytes 8388608 | tf_op jit(solution)/shard_map/div | solution.py:47
  (43 shorter events, 5.7 us)
Async XLA Ops:
  6.5 21.8 %all-gather.6.cloned.1.call-start = ((), (), s32[]{:S(2)}) async-start(), calls=%async_computation.1 | async-start | bytes 1310720 | tf_op jit(solution)/shard_map/all_gather | solution.py:41
  7.3 27.6 %copy-start = (s32[8]{0:T(128)S(1)}, s32[8]{0:T(128)}, u32[]{:S(2)}) copy-start(s32[8]{0:T(128)} %param.11) | copy-start | bytes 100
  7.3 76.2 %all-gather.8.cloned.1.call-start = ((), (), s32[]{:S(2)}) async-start(), calls=%async_computation.2 | async-start | bytes 2359296 | tf_op jit(solution)/shard_map/all_gather | solution.py:45
  34.1 162.2 %all-gather.4.cloned.1.call-start = ((), (), s32[]{:S(2)}) async-start(), calls=%async_computation | async-start | bytes 8257536 | tf_op jit(solution)/shard_map/all_gather | solution.py:38
Sparse Core Ops, SparseCore 0:
  8.9 19.4 all-gather.5
  34.2 49.2 all-gather.7
  85.7 110.4 all-gather.3
where the time goes:
time: 378 us; the launch traced here: 377 us
  waiting for transfers between devices  182 us (48%)
  blocking collectives  76.5 us (20%)
  local copies, waits for them, and re-layouts  54.3 us (14%)
  matrix products  33.3 us (9%)
  other arithmetic  17.9 us (5%)
  between operations  13.1 us (3%)
    all_gather x1, waiting for transfers between devices, local(): all_rows = lax.all_gather(activations, 'dp', axis=0, tiled=True)  111 us
    psum x1, blocking collectives, local(): rotated = lax.psum(partial_value, 'tensor').astype(jnp.bfloat16)  76.5 us
    all_gather x1, waiting for transfers between devices, local(): grad_rows = lax.all_gather(local_grads, 'dp', axis=0, tiled=True)  48.3 us
    gather x48, local copies, waits for them, and re-layouts  42.2 us
    all_gather x1, waiting for transfers between devices, local(): features = lax.all_gather(out_grads, 'tensor', axis=1, tiled=True)  21.1 us
    dot_general x2, matrix products, advance(): jnp.einsum('gtj,gtk->gjk', left_rows, right_rows, preferred_element_type=...  14.2 us
    dot_general x1, matrix products, local(): jnp.dot(all_rows, in_basis, preferred_element_type=jnp.float32)  13.4 us
    add x2, other arithmetic, advance(): return (running + jnp.sum(blocks * blocks, axis=0), None)  12.5 us
  transfers between devices with their start and end apart: 3, of which 3 were waited for; matrix products, arithmetic and copies ran while one was open for 1% of the time, Pallas kernels for 0%

commit v1 on v0

v1 whole, which is shorter than its diff:
```python
import functools

import jax
import jax.numpy as jnp
import numpy as np
from jax import lax
from jax.experimental import pallas as pl
from jax.experimental.pallas import tpu as pltpu
from jax.sharding import PartitionSpec as P

MAXLEN = 256
ROWS = 16
SUBS = 1


def ring_order(count):
    return list(range(0, count, 2)) + list(range(1, count, 2))[::-1]


def document_kernel(window, starts_ref, lengths_ref, rotated_ref, grads_ref, out_ref):
    tokens = rotated_ref.shape[0]
    documents = starts_ref.shape[0]

    def masked(base, size, first, last):
        row = base + lax.broadcasted_iota(jnp.int32, (size, 1), 0)
        keep = jnp.logical_and(row >= first, row < last)
        left = rotated_ref[pl.ds(base, size), :]
        left = jnp.where(keep, left, jnp.zeros_like(left))
        right = grads_ref[pl.ds(base, size), :]
        return lax.dot_general(
            left, right, (((0,), (0,)), ((), ())), preferred_element_type=jnp.float32
        )

    out_ref[...] = jnp.zeros_like(out_ref)

    def one(s, carry):
        first = starts_ref[s]
        last = first + lengths_ref[s]
        base = jnp.minimum((first // ROWS) * ROWS, tokens - window)
        base = pl.multiple_of(base, ROWS)
        fits = last <= base + window

        @pl.when(fits)
        def _():
            block = masked(base, window, first, last)
            out_ref[...] += block * block

        @pl.when(jnp.logical_not(fits))
        def _():
            block = masked(base, window, first, last)
            rest = pl.multiple_of(base + window, ROWS)
            block = block + masked(rest, ROWS, first, last)
            out_ref[...] += block * block

        return carry

    lax.fori_loop(0, documents, one, 0)
    out_ref[...] = out_ref[...] * jnp.float32(1.0 / tokens)


def document_squares(rotated, grad_rows, doc_lengths):
    tokens, width = rotated.shape
    columns = grad_rows.shape[1]
    starts = (jnp.cumsum(doc_lengths) - doc_lengths).astype(jnp.int32)
    tile = min(256, width)
    return pl.pallas_call(
        functools.partial(document_kernel, MAXLEN),
        out_shape=jax.ShapeDtypeStruct((width, columns), jnp.float32),
        grid_spec=pltpu.PrefetchScalarGridSpec(
            num_scalar_prefetch=2,
            grid=(width // tile,),
            in_specs=[
                pl.BlockSpec((tokens, tile), lambda j, *_: (0, j)),
                pl.BlockSpec((tokens, columns), lambda j, *_: (0, 0)),
            ],
            out_specs=pl.BlockSpec((tile, columns), lambda j, *_: (j, 0)),
        ),
        compiler_params=pltpu.CompilerParams(vmem_limit_bytes=32 * 1024 * 1024),
        cost_estimate=pl.CostEstimate(
            flops=2 * MAXLEN * doc_lengths.shape[0] * width * columns,
            bytes_accessed=2 * tokens * (width + columns) + 4 * width * columns,
            transcendentals=0,
        ),
    )(starts, doc_lengths.astype(jnp.int32), rotated, grad_rows)


def solution(mesh):
    n_dp, n_tensor = mesh.shape["dp"], mesh.shape["tensor"]
    order = ring_order(n_dp)
    place = np.argsort(np.array(order))
    forward = [(order[i], order[(i + 1) % n_dp]) for i in range(n_dp)]
    backward = [(d, s) for s, d in forward]
    swaps = {d: [(t, t ^ d) for t in range(n_tensor)] for d in range(1, n_tensor)}

    def sum_over_tensor(partial_value):
        me = lax.axis_index("tensor")
        rows = partial_value.shape[0] // n_tensor

        def share(t):
            return lax.dynamic_slice_in_dim(partial_value, t * rows, rows, 0)

        got = [lax.ppermute(share(me ^ d), "tensor", swaps[d]) for d in range(1, n_tensor)]
        total = share(me)
        for piece in got:
            total = total + piece
        total = total.astype(jnp.bfloat16)
        blocks = [(me, total)]
        for d in range(1, n_tensor):
            blocks.append((me ^ d, lax.ppermute(total, "tensor", swaps[d])))
        whole = jnp.zeros(partial_value.shape, jnp.bfloat16)
        for t, block in blocks:
            whole = lax.dynamic_update_slice_in_dim(whole, block, t * rows, 0)
        return whole

    def local(activations, in_basis, out_grads, out_basis, doc_lengths):
        mine = lax.axis_index("dp")
        spot = jnp.asarray(place, jnp.int32)[mine]
        shard = activations.shape[0]
        tokens = shard * n_dp
        half = shard // 2
        sub = half // SUBS

        def origin(step):
            return jnp.asarray(order, jnp.int32)[(spot + step) % n_dp]

        def start_of(source, way, k):
            return source * shard + way * half + k * sub

        def ring(block, subs):
            rows = half // subs
            moving = [
                (way, k, block[way * half + k * rows : way * half + (k + 1) * rows])
                for k in range(subs)
                for way in (0, 1)
            ]
            hops = [[(mine * shard, block)]]
            for h in range(1, n_dp):
                moving = [
                    (way, k, lax.ppermute(v, "dp", (forward, backward)[way]))
                    for way, k, v in moving
                ]
                hops.append(
                    [
                        (origin(-h if way == 0 else h) * shard + way * half + k * rows, v)
                        for way, k, v in moving
                    ]
                )
            return hops

        features = lax.all_gather(out_grads, "tensor", axis=1, tiled=True)
        own_grads = jnp.dot(features, out_basis, preferred_element_type=jnp.float32)
        own_grads = own_grads.astype(jnp.bfloat16)

        act_hops = ring(activations, SUBS)
        rotated = jnp.zeros((tokens, in_basis.shape[1]), jnp.bfloat16)
        groups = [[0, 1]] + [[h, h + 1] for h in range(2, n_dp - 2, 2)] + [[n_dp - 2], [n_dp - 1]]
        for group in groups:
            pieces = [piece for h in group for piece in act_hops[h]]
            stacked = jnp.concatenate([v for _, v in pieces], 0)
            partial_value = jnp.dot(stacked, in_basis, preferred_element_type=jnp.float32)
            done = sum_over_tensor(partial_value)
            at = 0
            for offset, v in pieces:
                rotated = lax.dynamic_update_slice_in_dim(
                    rotated, done[at : at + v.shape[0]], offset, 0
                )
                at += v.shape[0]

        grad_rows = jnp.zeros((tokens, own_grads.shape[1]), jnp.bfloat16)
        for hop in ring(own_grads, 1):
            for offset, v in hop:
                grad_rows = lax.dynamic_update_slice_in_dim(grad_rows, v, offset, 0)

        return document_squares(rotated, grad_rows, doc_lengths)

    placed = (P("dp", "tensor"), P("tensor", "dp"), P("dp", "tensor"), P(None, "tensor"), P())
    return jax.shard_map(
        local, mesh=mesh, in_specs=placed, out_specs=P("dp", "tensor"), check_vma=False
    )
```

time: 378 us -> 232 us (0.61)
  blocking collectives: 76.5 us -> 0 us
  waiting for transfers between devices: 182 us -> 108 us
  local copies, waits for them, and re-layouts: 54.3 us -> 5.96 us
  starting transfers between devices: 0.08 us -> 48.2 us
  between operations: 13.1 us -> 32.2 us
  other arithmetic: 17.9 us -> 1.55 us
  Pallas kernels: 0 us -> 14.7 us
  matrix products: 33.3 us -> 21.5 us
    all_gather x2 -> x0, waiting for transfers between devices: 159 us -> none  [the longest x1 111 us: local(): all_rows = lax.all_gather(activations, 'dp', axis=0, tiled=True)]
    ppermute x0 -> x58, waiting for transfers between devices: none -> 108 us  [the longest x28 52.1 us: ring(): lax.ppermute(v, 'dp', (forward, backward)[way])]
    psum x1 -> x0, blocking collectives: 76.5 us -> none  [local(): rotated = lax.psum(partial_value, 'tensor').astype(jnp.bfloat16)]
    ppermute x0 -> x58, starting transfers between devices: none -> 48.2 us  [the longest x28 29.4 us: ring(): lax.ppermute(v, 'dp', (forward, backward)[way])]
    gather x48 -> x0, local copies, waits for them, and re-layouts: 42.2 us -> none
    all_gather x1, waiting for transfers between devices: 21.1 us -> 0.01 us  [local(): features = lax.all_gather(out_grads, 'tensor', axis=1, tiled=True)]
    pallas_call x0 -> x1, Pallas kernels: none -> 14.7 us  [document_squares(): pl.pallas_call(functools.partial(document_kernel, MAXLEN), out_shape=jax....]
    add x2 -> x0, other arithmetic: 12.5 us -> none  [advance(): return (running + jnp.sum(blocks * blocks, axis=0), None)]
  transfers between devices with their start and end apart: 3 -> 59, of which waited for: 3 -> 31; matrix products, arithmetic and copies ran while one was open for 1% -> 8% of each run, Pallas kernels for 0% -> 0%
where the time goes in v1:
time: 232 us
  waiting for transfers between devices  108 us (47%)
  starting transfers between devices  48.2 us (21%)
  between operations  32.2 us (14%)
  matrix products  21.5 us (9%)
  Pallas kernels  14.7 us (6%)
  local copies, waits for them, and re-layouts  5.96 us (3%)
    ppermute x28, waiting for transfers between devices, ring(): lax.ppermute(v, 'dp', (forward, backward)[way])  52.1 us
    ppermute x15, waiting for transfers between devices, sum_over_tensor(): lax.ppermute(share(me ^ d), 'tensor', swaps[d])  34.2 us
    ppermute x28, starting transfers between devices, ring(): lax.ppermute(v, 'dp', (forward, backward)[way])  29.4 us
    ppermute x15, waiting for transfers between devices, sum_over_tensor(): blocks.append((me ^ d, lax.ppermute(total, 'tensor', swaps[d])))  21.7 us
    dot_general x5, matrix products, local(): jnp.dot(stacked, in_basis, preferred_element_type=jnp.float32)  16.4 us
    pallas_call x1, Pallas kernels, document_squares(): pl.pallas_call(functools.partial(document_kernel, MAXLEN), out_shape=jax....  14.7 us
    ppermute x15, starting transfers between devices, sum_over_tensor(): lax.ppermute(share(me ^ d), 'tensor', swaps[d])  9.55 us
    ppermute x15, starting transfers between devices, sum_over_tensor(): blocks.append((me ^ d, lax.ppermute(total, 'tensor', swaps[d])))  9.18 us
  transfers between devices with their start and end apart: 59, of which 31 were waited for; matrix products, arithmetic and copies ran while one was open for 8% of the time, Pallas kernels for 0%

profile of v1, /device:TPU:0, one launch (start us, length us, event | category | flops | bytes accessed | tf_op | source)
XLA Modules:
  0.0 232.0 jit_solution(2176979694659158750)
XLA Ops:
  6.5 1.2 fusion.35
  7.8 3.0 %collective-permute-start.1 = (bf16[64,3584]{1,0:T(8,128)(2,1)S(1)}, bf16[64,3584]{1,0:T(8,128)(2,1)S(1)}, u32[]{:S(2)}, u32[]{:S(2)}) collective-permute-start(bf16[64,3584]{1,0:T(8,128)(2,1)S(1)} %get-tuple-element.25), channel_id=1, source_target_pairs={{8,0},{16,8},{24,16},{28,24},{20,28},{12,20},{4,12},{0,4},{9,1},{1... | collective-permute-start | bytes 1376264 | tf_op jit(solution)/shard_map/ppermute | solution.py:139
  10.9 10.4 %collective-permute-done.1 = bf16[64,3584]{1,0:T(8,128)(2,1)S(1)} collective-permute-done((bf16[64,3584]{1,0:T(8,128)(2,1)S(1)}, bf16[64,3584]{1,0:T(8,128)(2,1)S(1)}, u32[]{:S(2)}, u32[]{:S(2)}) %collective-permute-start.1) | collective-permute-done | bytes 458784 | tf_op jit(solution)/shard_map/ppermute | solution.py:139
  21.4 1.4 collective-permute-done
  22.7 5.5 %fusion = f32[256,1024]{1,0:T(8,128)S(1)} fusion(bf16[3584,1024]{1,0:T(8,128)(2,1)} %param.35, bf16[64,3584]{1,0:T(8,128)(2,1)S(1)} %collective-permute-done.1, bf16[64,3584]{1,0:T(8,128)(2,1)S(1)} %collective-permute-done, bf16[128,3584]{1,0:T(8,128)(2,1)} %param.34), kind=kOutput, calls=%fused_computation | convolution fusion | flops 1884553216 | bytes 10223616 | tf_op jit(solution)/shard_map/dot_general | solution.py:160
  28.4 1.6 collective-permute-start.3
  33.8 3.2 %collective-permute-done.4 = f32[64,1024]{1,0:T(8,128)S(1)} collective-permute-done((f32[64,1024]{1,0:T(8,128)S(1)}, f32[64,1024]{1,0:T(8,128)S(1)}, u32[]{:S(2)}, u32[]{:S(2)}) %collective-permute-start.4) | collective-permute-done | bytes 262176 | tf_op jit(solution)/shard_map/ppermute | solution.py:102
  36.9 7.9 %collective-permute-done.3 = f32[64,1024]{1,0:T(8,128)S(1)} collective-permute-done((f32[64,1024]{1,0:T(8,128)S(1)}, f32[64,1024]{1,0:T(8,128)S(1)}, u32[]{:S(2)}, u32[]{:S(2)}) %collective-permute-start.3) | collective-permute-done | bytes 262176 | tf_op jit(solution)/shard_map/ppermute | solution.py:102
  45.1 1.9 collective-permute-start.6
  63.2 1.5 collective-permute-start.9
  65.3 5.2 %collective-permute-done.7 = bf16[64,1024]{1,0:T(8,128)(2,1)S(1)} collective-permute-done((bf16[64,1024]{1,0:T(8,128)(2,1)S(1)}, bf16[64,1024]{1,0:T(8,128)(2,1)S(1)}, u32[]{:S(2)}, u32[]{:S(2)}) %collective-permute-start.7) | collective-permute-done | bytes 131104 | tf_op jit(solution)/shard_map/ppermute | solution.py:109
  70.8 4.7 %collective-permute-done.9 = bf16[64,3584]{1,0:T(8,128)(2,1)S(1)} collective-permute-done((bf16[64,3584]{1,0:T(8,128)(2,1)S(1)}, bf16[64,3584]{1,0:T(8,128)(2,1)S(1)}, u32[]{:S(2)}, u32[]{:S(2)}) %collective-permute-start.9) | collective-permute-done | bytes 458784 | tf_op jit(solution)/shard_map/ppermute | solution.py:139
  75.4 1.4 collective-permute-start.11
  77.5 9.4 %collective-permute-done.11 = bf16[64,3584]{1,0:T(8,128)(2,1)} collective-permute-done((bf16[64,3584]{1,0:T(8,128)(2,1)S(1)}, bf16[64,3584]{1,0:T(8,128)(2,1)}, u32[]{:S(2)}, u32[]{:S(2)}) %collective-permute-start.11) | collective-permute-done | bytes 458784 | tf_op jit(solution)/shard_map/ppermute | solution.py:139
  86.9 1.2 collective-permute-done.10
  88.1 5.4 %fusion.6 = f32[256,1024]{1,0:T(8,128)S(1)} fusion(bf16[3584,1024]{1,0:T(8,128)(2,1)} %param.35, bf16[64,3584]{1,0:T(8,128)(2,1)} %collective-permute-done.11, bf16[64,3584]{1,0:T(8,128)(2,1)} %collective-permute-done.10, bf16[64,3584]{1,0:T(8,128)(2,1)S(1)} %collective-permute-done.9, bf16[64,3584]{1,0:T(8,128)(2,1)S(1)} %collective-permute-done.8), kind=kOutput, calls=%fused_computation.6 | convolution fusion | flops 1886388224 | bytes 10223616 | tf_op jit(solution)/shard_map/dot_general | solution.py:160
  94.4 1.2 collective-permute-start.13
  96.3 1.7 collective-permute-start.19
  99.5 5.1 %constant_dynamic-update-slice_fusion.14 = (bf16[1024,1024]{1,0:T(8,128)(2,1)S(1)}, bf16[128,1024]{1,0:T(8,128)(2,1)S(1)}) fusion(bf16[1024,1024]{1,0:T(8,128)(2,1)S(1)} %broadcast.23.clone.1, s32[]{:T(128)S(6)} %select_n.294, bf16[128,4096]{1,0:T(8,128)(2,1)S(1)} %copy-done.1, bf16[4096,1024]{1,0:T(8,128)(2,1)} %param.37), kind=kOutput, calls=%fused_computation.65 | convolution fusion | flops 1073872896 | bytes 9961476 | tf_op jit(solution)/shard_map/dot_general | solution.py:151
  105.3 3.1 %collective-permute-done.13 = f32[64,1024]{1,0:T(8,128)} collective-permute-done((f32[64,1024]{1,0:T(8,128)}, f32[64,1024]{1,0:T(8,128)}, u32[]{:S(2)}, u32[]{:S(2)}) %collective-permute-start.13) | collective-permute-done | bytes 262176 | tf_op jit(solution)/shard_map/ppermute | solution.py:102
  108.4 1.7 collective-permute-start.45
  111.5 1.7 collective-permute-done.44
  115.0 3.9 %collective-permute-done.16 = bf16[64,1024]{1,0:T(8,128)(2,1)S(1)} collective-permute-done((bf16[64,1024]{1,0:T(8,128)(2,1)S(1)}, bf16[64,1024]{1,0:T(8,128)(2,1)S(1)}, u32[]{:S(2)}, u32[]{:S(2)}) %collective-permute-start.16) | collective-permute-done | bytes 131104 | tf_op jit(solution)/shard_map/ppermute | solution.py:109
  118.8 1.7 collective-permute-start.47
  120.7 1.3 collective-permute-start.21
  123.8 1.7 collective-permute-start.49
  125.5 12.5 %collective-permute-done.48 = bf16[64,1024]{1,0:T(8,128)(2,1)S(1)} collective-permute-done((bf16[64,1024]{1,0:T(8,128)(2,1)S(1)}, bf16[64,1024]{1,0:T(8,128)(2,1)S(1)}, u32[]{:S(2)}, u32[]{:S(2)}) %collective-permute-start.48) | collective-permute-done | bytes 131104 | tf_op jit(solution)/shard_map/ppermute | solution.py:139
  138.3 1.6 collective-permute-start.51
  140.0 3.1 %collective-permute-done.50 = bf16[64,1024]{1,0:T(8,128)(2,1)S(1)} collective-permute-done((bf16[64,1024]{1,0:T(8,128)(2,1)S(1)}, bf16[64,1024]{1,0:T(8,128)(2,1)S(1)}, u32[]{:S(2)}, u32[]{:S(2)}) %collective-permute-start.50) | collective-permute-done | bytes 131104 | tf_op jit(solution)/shard_map/ppermute | solution.py:139
  143.4 1.7 collective-permute-start.53
  145.2 2.9 %collective-permute-done.52 = bf16[64,1024]{1,0:T(8,128)(2,1)S(1)} collective-permute-done((bf16[64,1024]{1,0:T(8,128)(2,1)S(1)}, bf16[64,1024]{1,0:T(8,128)(2,1)S(1)}, u32[]{:S(2)}, u32[]{:S(2)}) %collective-permute-start.52) | collective-permute-done | bytes 131104 | tf_op jit(solution)/shard_map/ppermute | solution.py:139
  148.4 1.7 collective-permute-start.55
  150.2 3.2 %fusion.14 = f32[256,1024]{1,0:T(8,128)S(1)} fusion(bf16[3584,1024]{1,0:T(8,128)(2,1)S(1)} %bitcast.47, bf16[64,3584]{1,0:T(8,128)(2,1)S(1)} %collective-permute-done.21, bf16[64,3584]{1,0:T(8,128)(2,1)S(1)} %collective-permute-done.20, bf16[64,3584]{1,0:T(8,128)(2,1)} %collective-permute-done.19, bf16[64,3584]{1,0:T(8,128)(2,1)} %collective-permute-done.18), kind=kOutput, calls=%fused_computation.14 | convolution fusion | flops 1886388224 | bytes 10223616 | tf_op jit(solution)/shard_map/dot_general | solution.py:160
  155.8 1.8 collective-permute-start.28
  157.6 4.5 %collective-permute-done.24 = f32[64,1024]{1,0:T(8,128)S(1)} collective-permute-done((f32[64,1024]{1,0:T(8,128)S(1)}, f32[64,1024]{1,0:T(8,128)S(1)}, u32[]{:S(2)}, u32[]{:S(2)}) %collective-permute-start.24) | collective-permute-done | bytes 262176 | tf_op jit(solution)/shard_map/ppermute | solution.py:102
  162.3 4.7 %collective-permute-done.23 = f32[64,1024]{1,0:T(8,128)S(1)} collective-permute-done((f32[64,1024]{1,0:T(8,128)S(1)}, f32[64,1024]{1,0:T(8,128)S(1)}, u32[]{:S(2)}, u32[]{:S(2)}) %collective-permute-start.23) | collective-permute-done | bytes 262176 | tf_op jit(solution)/shard_map/ppermute | solution.py:102
  168.2 3.0 %collective-permute-done.56 = bf16[64,1024]{1,0:T(8,128)(2,1)S(1)} collective-permute-done((bf16[64,1024]{1,0:T(8,128)(2,1)S(1)}, bf16[64,1024]{1,0:T(8,128)(2,1)S(1)}, u32[]{:S(2)}, u32[]{:S(2)}) %collective-permute-start.56) | collective-permute-done | bytes 131104 | tf_op jit(solution)/shard_map/ppermute | solution.py:139
  171.3 1.4 collective-permute-start.26
  173.3 3.4 %collective-permute-done.26 = bf16[64,1024]{1,0:T(8,128)(2,1)S(1)} collective-permute-done((bf16[64,1024]{1,0:T(8,128)(2,1)S(1)}, bf16[64,1024]{1,0:T(8,128)(2,1)S(1)}, u32[]{:S(2)}, u32[]{:S(2)}) %collective-permute-start.26) | collective-permute-done | bytes 131104 | tf_op jit(solution)/shard_map/ppermute | solution.py:109
  176.7 2.0 collective-permute-done.27
  182.7 1.3 collective-permute-start.36
  184.0 1.5 collective-permute-done.32
  185.5 3.1 %collective-permute-done.31 = f32[32,1024]{1,0:T(8,128)S(1)} collective-permute-done((f32[32,1024]{1,0:T(8,128)S(1)}, f32[32,1024]{1,0:T(8,128)S(1)}, u32[]{:S(2)}, u32[]{:S(2)}) %collective-permute-start.31) | collective-permute-done | bytes 131104 | tf_op jit(solution)/shard_map/ppermute | solution.py:102
  190.8 3.0 %collective-permute-done.34 = bf16[32,1024]{1,0:T(8,128)(2,1)S(1)} collective-permute-done((bf16[32,1024]{1,0:T(8,128)(2,1)S(1)}, bf16[32,1024]{1,0:T(8,128)(2,1)S(1)}, u32[]{:S(2)}, u32[]{:S(2)}) %collective-permute-start.34) | collective-permute-done | bytes 65568 | tf_op jit(solution)/shard_map/ppermute | solution.py:109
  198.5 3.9 %collective-permute-done.40 = f32[32,1024]{1,0:T(8,128)S(1)} collective-permute-done((f32[32,1024]{1,0:T(8,128)S(1)}, f32[32,1024]{1,0:T(8,128)S(1)}, u32[]{:S(2)}, u32[]{:S(2)}) %collective-permute-start.40) | collective-permute-done | bytes 131104 | tf_op jit(solution)/shard_map/ppermute | solution.py:102
  202.4 2.3 collective-permute-done.39
  206.8 3.0 %collective-permute-done.42 = bf16[32,1024]{1,0:T(8,128)(2,1)S(1)} collective-permute-done((bf16[32,1024]{1,0:T(8,128)(2,1)S(1)}, bf16[32,1024]{1,0:T(8,128)(2,1)S(1)}, u32[]{:S(2)}, u32[]{:S(2)}) %collective-permute-start.42) | collective-permute-done | bytes 65568 | tf_op jit(solution)/shard_map/ppermute | solution.py:109
  210.5 14.7 %shard_map.316 = f32[1024,1024]{1,0:T(8,128)} custom-call(s32[8]{0:T(128)S(1)} %bitcast_subtract_fusion.starts_ref, s32[8]{0:T(128)S(1)} %copy-done, bf16[1024,1024]{1,0:T(8,128)(2,1)S(1)} %slice_dynamic-update-slice_fusion.1.rotated_ref, bf16[1024,1024]{1,0:T(8,128)(2,1)S(1)} %constant_dynamic-update-slice_fusion.13.grads_ref), custom_call_target="tpu_custom_call" | custom-call | flops 4294967296 | bytes 8388608 | tf_op jit(solution)/shard_map/pallas_call | solution.py:66
  (158 shorter events, 31.7 us)
Async XLA Ops:
  6.5 91.8 %all-gather.2.cloned.1.call-start = ((), (), s32[]{:S(2)}) async-start(), calls=%async_computation | async-start | bytes 1310720 | tf_op jit(solution)/shard_map/all_gather | solution.py:150
  7.8 13.6 %collective-permute-start.1 = (bf16[64,3584]{1,0:T(8,128)(2,1)S(1)}, bf16[64,3584]{1,0:T(8,128)(2,1)S(1)}, u32[]{:S(2)}, u32[]{:S(2)}) collective-permute-start(bf16[64,3584]{1,0:T(8,128)(2,1)S(1)} %get-tuple-element.25), channel_id=1, source_target_pairs={{8,0},{16,8},{24,16},{28,24},{20,28},{12,20},{4,12},{0,4},{9,1},{1... | collective-permute-start | bytes 1376264 | tf_op jit(solution)/shard_map/ppermute | solution.py:139
  10.7 12.0 %collective-permute-start = (bf16[64,3584]{1,0:T(8,128)(2,1)S(1)}, bf16[64,3584]{1,0:T(8,128)(2,1)S(1)}, u32[]{:S(2)}, u32[]{:S(2)}) collective-permute-start(bf16[64,3584]{1,0:T(8,128)(2,1)S(1)} %get-tuple-element.24), channel_id=1, source_target_pairs={{0,8},{8,16},{16,24},{24,28},{28,20},{20,12},{12,4},{4,0},{1,9},{9... | collective-permute-start | bytes 1376264 | tf_op jit(solution)/shard_map/ppermute | solution.py:139
  28.4 8.6 %collective-permute-start.4 = (f32[64,1024]{1,0:T(8,128)S(1)}, f32[64,1024]{1,0:T(8,128)S(1)}, u32[]{:S(2)}, u32[]{:S(2)}) collective-permute-start(f32[64,1024]{1,0:T(8,128)S(1)} %get-tuple-element.22), channel_id=1, source_target_pairs={{0,3},{1,2},{2,1},{3,0},{4,7},{5,6},{6,5},{7,4},{8,11},{9,10},{10,... | collective-permute-start | bytes 786440 | tf_op jit(solution)/shard_map/ppermute | solution.py:102
  28.4 16.4 %collective-permute-start.3 = (f32[64,1024]{1,0:T(8,128)S(1)}, f32[64,1024]{1,0:T(8,128)S(1)}, u32[]{:S(2)}, u32[]{:S(2)}) collective-permute-start(f32[64,1024]{1,0:T(8,128)S(1)} %get-tuple-element.23), channel_id=1, source_target_pairs={{0,2},{1,3},{2,0},{3,1},{4,6},{5,7},{6,4},{7,5},{8,10},{9,11},{10,... | collective-permute-start | bytes 786440 | tf_op jit(solution)/shard_map/ppermute | solution.py:102
  30.0 14.8 %collective-permute-start.2 = (f32[64,1024]{1,0:T(8,128)S(1)}, f32[64,1024]{1,0:T(8,128)S(1)}, u32[]{:S(2)}, u32[]{:S(2)}) collective-permute-start(f32[64,1024]{1,0:T(8,128)S(1)} %get-tuple-element.21), channel_id=1, source_target_pairs={{0,1},{1,0},{2,3},{3,2},{4,5},{5,4},{6,7},{7,6},{8,9},{9,8},{10,11... | collective-permute-start | bytes 786440 | tf_op jit(solution)/shard_map/ppermute | solution.py:102
  45.0 20.3 %collective-permute-start.5 = (bf16[64,1024]{1,0:T(8,128)(2,1)S(1)}, bf16[64,1024]{1,0:T(8,128)(2,1)S(1)}, u32[]{:S(2)}, u32[]{:S(2)}) collective-permute-start(bf16[64,1024]{1,0:T(8,128)(2,1)S(1)} %get-tuple-element.14), channel_id=1, source_target_pairs={{0,1},{1,0},{2,3},{3,2},{4,5},{5,4},{6,7},{7,6},{8,9},{9,8},{10,11... | collective-permute-start | bytes 393224 | tf_op jit(solution)/shard_map/ppermute | solution.py:109
  45.1 20.2 %collective-permute-start.6 = (bf16[64,1024]{1,0:T(8,128)(2,1)S(1)}, bf16[64,1024]{1,0:T(8,128)(2,1)S(1)}, u32[]{:S(2)}, u32[]{:S(2)}) collective-permute-start(bf16[64,1024]{1,0:T(8,128)(2,1)S(1)} %get-tuple-element.14), channel_id=1, source_target_pairs={{0,2},{1,3},{2,0},{3,1},{4,6},{5,7},{6,4},{7,5},{8,10},{9,11},{10,... | collective-permute-start | bytes 393224 | tf_op jit(solution)/shard_map/ppermute | solution.py:109
  63.2 12.3 %collective-permute-start.9 = (bf16[64,3584]{1,0:T(8,128)(2,1)S(1)}, bf16[64,3584]{1,0:T(8,128)(2,1)S(1)}, u32[]{:S(2)}, u32[]{:S(2)}) collective-permute-start(bf16[64,3584]{1,0:T(8,128)(2,1)S(1)} %collective-permute-done.1), channel_id=1, source_target_pairs={{8,0},{16,8},{24,16},{28,24},{20,28},{12,20},{4,12},{0,4},{9,1},{1... | collective-permute-start | bytes 1376264 | tf_op jit(solution)/shard_map/ppermute | solution.py:139
  64.6 12.2 %collective-permute-start.8 = (bf16[64,3584]{1,0:T(8,128)(2,1)S(1)}, bf16[64,3584]{1,0:T(8,128)(2,1)S(1)}, u32[]{:S(2)}, u32[]{:S(2)}) collective-permute-start(bf16[64,3584]{1,0:T(8,128)(2,1)S(1)} %collective-permute-done), channel_id=1, source_target_pairs={{0,8},{8,16},{16,24},{24,28},{28,20},{20,12},{12,4},{4,0},{1,9},{9... | collective-permute-start | bytes 1376264 | tf_op jit(solution)/shard_map/ppermute | solution.py:139
  65.2 5.2 %collective-permute-start.7 = (bf16[64,1024]{1,0:T(8,128)(2,1)S(1)}, bf16[64,1024]{1,0:T(8,128)(2,1)S(1)}, u32[]{:S(2)}, u32[]{:S(2)}) collective-permute-start(bf16[64,1024]{1,0:T(8,128)(2,1)S(1)} %get-tuple-element.14), channel_id=1, source_target_pairs={{0,3},{1,2},{2,1},{3,0},{4,7},{5,6},{6,5},{7,4},{8,11},{9,10},{10,... | collective-permute-start | bytes 393224 | tf_op jit(solution)/shard_map/ppermute | solution.py:109
  75.4 11.5 %collective-permute-start.11 = (bf16[64,3584]{1,0:T(8,128)(2,1)S(1)}, bf16[64,3584]{1,0:T(8,128)(2,1)}, u32[]{:S(2)}, u32[]{:S(2)}) collective-permute-start(bf16[64,3584]{1,0:T(8,128)(2,1)S(1)} %collective-permute-done.9), channel_id=1, source_target_pairs={{8,0},{16,8},{24,16},{28,24},{20,28},{12,20},{4,12},{0,4},{9,1},{1... | collective-permute-start | bytes 1376264 | tf_op jit(solution)/shard_map/ppermute | solution.py:139
  76.9 11.2 %collective-permute-start.10 = (bf16[64,3584]{1,0:T(8,128)(2,1)S(1)}, bf16[64,3584]{1,0:T(8,128)(2,1)}, u32[]{:S(2)}, u32[]{:S(2)}) collective-permute-start(bf16[64,3584]{1,0:T(8,128)(2,1)S(1)} %collective-permute-done.8), channel_id=1, source_target_pairs={{0,8},{8,16},{16,24},{24,28},{28,20},{20,12},{12,4},{4,0},{1,9},{9... | collective-permute-start | bytes 1376264 | tf_op jit(solution)/shard_map/ppermute | solution.py:139
  94.4 10.2 %collective-permute-start.14 = (f32[64,1024]{1,0:T(8,128)}, f32[64,1024]{1,0:T(8,128)S(1)}, u32[]{:S(2)}, u32[]{:S(2)}) collective-permute-start(f32[64,1024]{1,0:T(8,128)} %get-tuple-element.19), channel_id=1, source_target_pairs={{0,3},{1,2},{2,1},{3,0},{4,7},{5,6},{6,5},{7,4},{8,11},{9,10},{10,... | collective-permute-start | bytes 786440 | tf_op jit(solution)/shard_map/ppermute | solution.py:102
  94.4 14.0 %collective-permute-start.13 = (f32[64,1024]{1,0:T(8,128)}, f32[64,1024]{1,0:T(8,128)}, u32[]{:S(2)}, u32[]{:S(2)}) collective-permute-start(f32[64,1024]{1,0:T(8,128)} %get-tuple-element.20), channel_id=1, source_target_pairs={{0,2},{1,3},{2,0},{3,1},{4,6},{5,7},{6,4},{7,5},{8,10},{9,11},{10,... | collective-permute-start | bytes 786440 | tf_op jit(solution)/shard_map/ppermute | solution.py:102
  95.6 14.5 %collective-permute-start.12 = (f32[64,1024]{1,0:T(8,128)}, f32[64,1024]{1,0:T(8,128)}, u32[]{:S(2)}, u32[]{:S(2)}) collective-permute-start(f32[64,1024]{1,0:T(8,128)} %get-tuple-element.18), channel_id=1, source_target_pairs={{0,1},{1,0},{2,3},{3,2},{4,5},{5,4},{6,7},{7,6},{8,9},{9,8},{10,11... | collective-permute-start | bytes 786440 | tf_op jit(solution)/shard_map/ppermute | solution.py:102
  96.3 24.4 %collective-permute-start.19 = (bf16[64,3584]{1,0:T(8,128)(2,1)}, bf16[64,3584]{1,0:T(8,128)(2,1)}, u32[]{:S(2)}, u32[]{:S(2)}) collective-permute-start(bf16[64,3584]{1,0:T(8,128)(2,1)} %collective-permute-done.11), channel_id=1, source_target_pairs={{8,0},{16,8},{24,16},{28,24},{20,28},{12,20},{4,12},{0,4},{9,1},{1... | collective-permute-start | bytes 1376264 | tf_op jit(solution)/shard_map/ppermute | solution.py:139
  98.0 24.0 %collective-permute-start.18 = (bf16[64,3584]{1,0:T(8,128)(2,1)}, bf16[64,3584]{1,0:T(8,128)(2,1)}, u32[]{:S(2)}, u32[]{:S(2)}) collective-permute-start(bf16[64,3584]{1,0:T(8,128)(2,1)} %collective-permute-done.10), channel_id=1, source_target_pairs={{0,8},{8,16},{16,24},{24,28},{28,20},{20,12},{12,4},{4,0},{1,9},{9... | collective-permute-start | bytes 1376264 | tf_op jit(solution)/shard_map/ppermute | solution.py:139
  104.6 8.5 %collective-permute-start.44 = (bf16[64,1024]{1,0:T(8,128)(2,1)S(1)}, bf16[64,1024]{1,0:T(8,128)(2,1)S(1)}, u32[]{:S(2)}, u32[]{:S(2)}) collective-permute-start(bf16[64,1024]{1,0:T(8,128)(2,1)S(1)} %get-tuple-element.33), channel_id=1, source_target_pairs={{0,8},{8,16},{16,24},{24,28},{28,20},{20,12},{12,4},{4,0},{1,9},{9... | collective-permute-start | bytes 393224 | tf_op jit(solution)/shard_map/ppermute | solution.py:139
  108.4 5.9 %collective-permute-start.45 = (bf16[64,1024]{1,0:T(8,128)(2,1)S(1)}, bf16[64,1024]{1,0:T(8,128)(2,1)S(1)}, u32[]{:S(2)}, u32[]{:S(2)}) collective-permute-start(bf16[64,1024]{1,0:T(8,128)(2,1)S(1)} %get-tuple-element.32), channel_id=1, source_target_pairs={{8,0},{16,8},{24,16},{28,24},{20,28},{12,20},{4,12},{0,4},{9,1},{1... | collective-permute-start | bytes 393224 | tf_op jit(solution)/shard_map/ppermute | solution.py:139
  113.1 5.7 %collective-permute-start.16 = (bf16[64,1024]{1,0:T(8,128)(2,1)S(1)}, bf16[64,1024]{1,0:T(8,128)(2,1)S(1)}, u32[]{:S(2)}, u32[]{:S(2)}) collective-permute-start(bf16[64,1024]{1,0:T(8,128)(2,1)S(1)} %get-tuple-element.12), channel_id=1, source_target_pairs={{0,2},{1,3},{2,0},{3,1},{4,6},{5,7},{6,4},{7,5},{8,10},{9,11},{10,... | collective-permute-start | bytes 393224 | tf_op jit(solution)/shard_map/ppermute | solution.py:109
  114.3 6.2 %collective-permute-start.17 = (bf16[64,1024]{1,0:T(8,128)(2,1)S(1)}, bf16[64,1024]{1,0:T(8,128)(2,1)S(1)}, u32[]{:S(2)}, u32[]{:S(2)}) collective-permute-start(bf16[64,1024]{1,0:T(8,128)(2,1)S(1)} %get-tuple-element.12), channel_id=1, source_target_pairs={{0,3},{1,2},{2,1},{3,0},{4,7},{5,6},{6,5},{7,4},{8,11},{9,10},{10,... | collective-permute-start | bytes 393224 | tf_op jit(solution)/shard_map/ppermute | solution.py:109
  114.5 8.3 %collective-permute-start.46 = (bf16[64,1024]{1,0:T(8,128)(2,1)S(1)}, bf16[64,1024]{1,0:T(8,128)(2,1)S(1)}, u32[]{:S(2)}, u32[]{:S(2)}) collective-permute-start(bf16[64,1024]{1,0:T(8,128)(2,1)S(1)} %collective-permute-done.44), channel_id=1, source_target_pairs={{0,8},{8,16},{16,24},{24,28},{28,20},{20,12},{12,4},{4,0},{1,9},{9... | collective-permute-start | bytes 393224 | tf_op jit(solution)/shard_map/ppermute | solution.py:139
  120.7 29.5 %collective-permute-start.21 = (bf16[64,3584]{1,0:T(8,128)(2,1)}, bf16[64,3584]{1,0:T(8,128)(2,1)S(1)}, u32[]{:S(2)}, u32[]{:S(2)}) collective-permute-start(bf16[64,3584]{1,0:T(8,128)(2,1)} %collective-permute-done.19), channel_id=1, source_target_pairs={{8,0},{16,8},{24,16},{28,24},{20,28},{12,20},{4,12},{0,4},{9,1},{1... | collective-permute-start | bytes 1376264 | tf_op jit(solution)/shard_map/ppermute | solution.py:139
  122.0 28.1 %collective-permute-start.20 = (bf16[64,3584]{1,0:T(8,128)(2,1)}, bf16[64,3584]{1,0:T(8,128)(2,1)S(1)}, u32[]{:S(2)}, u32[]{:S(2)}) collective-permute-start(bf16[64,3584]{1,0:T(8,128)(2,1)} %collective-permute-done.18), channel_id=1, source_target_pairs={{0,8},{8,16},{16,24},{24,28},{28,20},{20,12},{12,4},{4,0},{1,9},{9... | collective-permute-start | bytes 1376264 | tf_op jit(solution)/shard_map/ppermute | solution.py:139
  122.7 15.2 %collective-permute-start.48 = (bf16[64,1024]{1,0:T(8,128)(2,1)S(1)}, bf16[64,1024]{1,0:T(8,128)(2,1)S(1)}, u32[]{:S(2)}, u32[]{:S(2)}) collective-permute-start(bf16[64,1024]{1,0:T(8,128)(2,1)S(1)} %collective-permute-done.46), channel_id=1, source_target_pairs={{0,8},{8,16},{16,24},{24,28},{28,20},{20,12},{12,4},{4,0},{1,9},{9... | collective-permute-start | bytes 393224 | tf_op jit(solution)/shard_map/ppermute | solution.py:139
  123.8 14.5 %collective-permute-start.49 = (bf16[64,1024]{1,0:T(8,128)(2,1)S(1)}, bf16[64,1024]{1,0:T(8,128)(2,1)S(1)}, u32[]{:S(2)}, u32[]{:S(2)}) collective-permute-start(bf16[64,1024]{1,0:T(8,128)(2,1)S(1)} %collective-permute-done.47), channel_id=1, source_target_pairs={{8,0},{16,8},{24,16},{28,24},{20,28},{12,20},{4,12},{0,4},{9,1},{1... | collective-permute-start | bytes 393224 | tf_op jit(solution)/shard_map/ppermute | solution.py:139
  138.0 5.2 %collective-permute-start.50 = (bf16[64,1024]{1,0:T(8,128)(2,1)S(1)}, bf16[64,1024]{1,0:T(8,128)(2,1)S(1)}, u32[]{:S(2)}, u32[]{:S(2)}) collective-permute-start(bf16[64,1024]{1,0:T(8,128)(2,1)S(1)} %collective-permute-done.48), channel_id=1, source_target_pairs={{0,8},{8,16},{16,24},{24,28},{28,20},{20,12},{12,4},{4,0},{1,9},{9... | collective-permute-start | bytes 393224 | tf_op jit(solution)/shard_map/ppermute | solution.py:139
  148.1 7.3 %collective-permute-start.54 = (bf16[64,1024]{1,0:T(8,128)(2,1)S(1)}, bf16[64,1024]{1,0:T(8,128)(2,1)S(1)}, u32[]{:S(2)}, u32[]{:S(2)}) collective-permute-start(bf16[64,1024]{1,0:T(8,128)(2,1)S(1)} %collective-permute-done.52), channel_id=1, source_target_pairs={{0,8},{8,16},{16,24},{24,28},{28,20},{20,12},{12,4},{4,0},{1,9},{9... | collective-permute-start | bytes 393224 | tf_op jit(solution)/shard_map/ppermute | solution.py:139
  148.4 7.4 %collective-permute-start.55 = (bf16[64,1024]{1,0:T(8,128)(2,1)S(1)}, bf16[64,1024]{1,0:T(8,128)(2,1)S(1)}, u32[]{:S(2)}, u32[]{:S(2)}) collective-permute-start(bf16[64,1024]{1,0:T(8,128)(2,1)S(1)} %collective-permute-done.53), channel_id=1, source_target_pairs={{8,0},{16,8},{24,16},{28,24},{20,28},{12,20},{4,12},{0,4},{9,1},{1... | collective-permute-start | bytes 393224 | tf_op jit(solution)/shard_map/ppermute | solution.py:139
  153.5 8.6 %collective-permute-start.24 = (f32[64,1024]{1,0:T(8,128)S(1)}, f32[64,1024]{1,0:T(8,128)S(1)}, u32[]{:S(2)}, u32[]{:S(2)}) collective-permute-start(f32[64,1024]{1,0:T(8,128)S(1)} %get-tuple-element.16), channel_id=1, source_target_pairs={{0,3},{1,2},{2,1},{3,0},{4,7},{5,6},{6,5},{7,4},{8,11},{9,10},{10,... | collective-permute-start | bytes 786440 | tf_op jit(solution)/shard_map/ppermute | solution.py:102
  153.5 13.5 %collective-permute-start.23 = (f32[64,1024]{1,0:T(8,128)S(1)}, f32[64,1024]{1,0:T(8,128)S(1)}, u32[]{:S(2)}, u32[]{:S(2)}) collective-permute-start(f32[64,1024]{1,0:T(8,128)S(1)} %get-tuple-element.17), channel_id=1, source_target_pairs={{0,2},{1,3},{2,0},{3,1},{4,6},{5,7},{6,4},{7,5},{8,10},{9,11},{10,... | collective-permute-start | bytes 786440 | tf_op jit(solution)/shard_map/ppermute | solution.py:102
  154.6 13.4 %collective-permute-start.22 = (f32[64,1024]{1,0:T(8,128)S(1)}, f32[64,1024]{1,0:T(8,128)S(1)}, u32[]{:S(2)}, u32[]{:S(2)}) collective-permute-start(f32[64,1024]{1,0:T(8,128)S(1)} %get-tuple-element.15), channel_id=1, source_target_pairs={{0,1},{1,0},{2,3},{3,2},{4,5},{5,4},{6,7},{7,6},{8,9},{9,8},{10,11... | collective-permute-start | bytes 786440 | tf_op jit(solution)/shard_map/ppermute | solution.py:102
  155.4 23.4 %collective-permute-start.29 = (bf16[64,3584]{1,0:T(8,128)(2,1)S(1)}, bf16[64,3584]{1,0:T(8,128)(2,1)S(1)}, u32[]{:S(2)}, u32[]{:S(2)}) collective-permute-start(bf16[64,3584]{1,0:T(8,128)(2,1)S(1)} %collective-permute-done.21), channel_id=1, source_target_pairs={{8,0},{16,8},{24,16},{28,24},{20,28},{12,20},{4,12},{0,4},{9,1},{1... | collective-permute-start | bytes 1376264 | tf_op jit(solution)/shard_map/ppermute | solution.py:139
  155.8 23.0 %collective-permute-start.28 = (bf16[64,3584]{1,0:T(8,128)(2,1)S(1)}, bf16[64,3584]{1,0:T(8,128)(2,1)S(1)}, u32[]{:S(2)}, u32[]{:S(2)}) collective-permute-start(bf16[64,3584]{1,0:T(8,128)(2,1)S(1)} %collective-permute-done.20), channel_id=1, source_target_pairs={{0,8},{8,16},{16,24},{24,28},{28,20},{20,12},{12,4},{4,0},{1,9},{9... | collective-permute-start | bytes 1376264 | tf_op jit(solution)/shard_map/ppermute | solution.py:139
  162.0 9.2 %collective-permute-start.56 = (bf16[64,1024]{1,0:T(8,128)(2,1)S(1)}, bf16[64,1024]{1,0:T(8,128)(2,1)S(1)}, u32[]{:S(2)}, u32[]{:S(2)}) collective-permute-start(bf16[64,1024]{1,0:T(8,128)(2,1)S(1)} %collective-permute-done.54), channel_id=1, source_target_pairs={{0,8},{8,16},{16,24},{24,28},{28,20},{20,12},{12,4},{4,0},{1,9},{9... | collective-permute-start | bytes 393224 | tf_op jit(solution)/shard_map/ppermute | solution.py:139
  167.0 5.9 %collective-permute-start.57 = (bf16[64,1024]{1,0:T(8,128)(2,1)S(1)}, bf16[64,1024]{1,0:T(8,128)(2,1)S(1)}, u32[]{:S(2)}, u32[]{:S(2)}) collective-permute-start(bf16[64,1024]{1,0:T(8,128)(2,1)S(1)} %collective-permute-done.55), channel_id=1, source_target_pairs={{8,0},{16,8},{24,16},{28,24},{20,28},{12,20},{4,12},{0,4},{9,1},{1... | collective-permute-start | bytes 393224 | tf_op jit(solution)/shard_map/ppermute | solution.py:139
  168.1 5.1 %collective-permute-start.25 = (bf16[64,1024]{1,0:T(8,128)(2,1)S(1)}, bf16[64,1024]{1,0:T(8,128)(2,1)S(1)}, u32[]{:S(2)}, u32[]{:S(2)}) collective-permute-start(bf16[64,1024]{1,0:T(8,128)(2,1)S(1)} %get-tuple-element.10), channel_id=1, source_target_pairs={{0,1},{1,0},{2,3},{3,2},{4,5},{5,4},{6,7},{7,6},{8,9},{9,8},{10,11... | collective-permute-start | bytes 393224 | tf_op jit(solution)/shard_map/ppermute | solution.py:109
  171.3 5.4 %collective-permute-start.26 = (bf16[64,1024]{1,0:T(8,128)(2,1)S(1)}, bf16[64,1024]{1,0:T(8,128)(2,1)S(1)}, u32[]{:S(2)}, u32[]{:S(2)}) collective-permute-start(bf16[64,1024]{1,0:T(8,128)(2,1)S(1)} %get-tuple-element.10), channel_id=1, source_target_pairs={{0,2},{1,3},{2,0},{3,1},{4,6},{5,7},{6,4},{7,5},{8,10},{9,11},{10,... | collective-permute-start | bytes 393224 | tf_op jit(solution)/shard_map/ppermute | solution.py:109
  172.9 5.9 %collective-permute-start.27 = (bf16[64,1024]{1,0:T(8,128)(2,1)S(1)}, bf16[64,1024]{1,0:T(8,128)(2,1)S(1)}, u32[]{:S(2)}, u32[]{:S(2)}) collective-permute-start(bf16[64,1024]{1,0:T(8,128)(2,1)S(1)} %get-tuple-element.10), channel_id=1, source_target_pairs={{0,3},{1,2},{2,1},{3,0},{4,7},{5,6},{6,5},{7,4},{8,11},{9,10},{10,... | collective-permute-start | bytes 393224 | tf_op jit(solution)/shard_map/ppermute | solution.py:109
  180.0 5.6 %collective-permute-start.32 = (f32[32,1024]{1,0:T(8,128)S(1)}, f32[32,1024]{1,0:T(8,128)S(1)}, u32[]{:S(2)}, u32[]{:S(2)}) collective-permute-start(f32[32,1024]{1,0:T(8,128)S(1)} %get-tuple-element.30), channel_id=1, source_target_pairs={{0,3},{1,2},{2,1},{3,0},{4,7},{5,6},{6,5},{7,4},{8,11},{9,10},{10,... | collective-permute-start | bytes 393224 | tf_op jit(solution)/shard_map/ppermute | solution.py:102
  181.1 7.5 %collective-permute-start.31 = (f32[32,1024]{1,0:T(8,128)S(1)}, f32[32,1024]{1,0:T(8,128)S(1)}, u32[]{:S(2)}, u32[]{:S(2)}) collective-permute-start(f32[32,1024]{1,0:T(8,128)S(1)} %get-tuple-element.31), channel_id=1, source_target_pairs={{0,2},{1,3},{2,0},{3,1},{4,6},{5,7},{6,4},{7,5},{8,10},{9,11},{10,... | collective-permute-start | bytes 393224 | tf_op jit(solution)/shard_map/ppermute | solution.py:102
  181.9 6.8 %collective-permute-start.30 = (f32[32,1024]{1,0:T(8,128)S(1)}, f32[32,1024]{1,0:T(8,128)S(1)}, u32[]{:S(2)}, u32[]{:S(2)}) collective-permute-start(f32[32,1024]{1,0:T(8,128)S(1)} %get-tuple-element.29), channel_id=1, source_target_pairs={{0,1},{1,0},{2,3},{3,2},{4,5},{5,4},{6,7},{7,6},{8,9},{9,8},{10,11... | collective-permute-start | bytes 393224 | tf_op jit(solution)/shard_map/ppermute | solution.py:102
  181.9 13.0 %collective-permute-start.37 = (bf16[64,3584]{1,0:T(8,128)(2,1)S(1)}, bf16[64,3584]{1,0:T(8,128)(2,1)S(1)}, u32[]{:S(2)}, u32[]{:S(2)}) collective-permute-start(bf16[64,3584]{1,0:T(8,128)(2,1)S(1)} %collective-permute-done.29), channel_id=1, source_target_pairs={{8,0},{16,8},{24,16},{28,24},{20,28},{12,20},{4,12},{0,4},{9,1},{1... | collective-permute-start | bytes 1376264 | tf_op jit(solution)/shard_map/ppermute | solution.py:139
  182.7 12.7 %collective-permute-start.36 = (bf16[64,3584]{1,0:T(8,128)(2,1)S(1)}, bf16[64,3584]{1,0:T(8,128)(2,1)S(1)}, u32[]{:S(2)}, u32[]{:S(2)}) collective-permute-start(bf16[64,3584]{1,0:T(8,128)(2,1)S(1)} %collective-permute-done.28), channel_id=1, source_target_pairs={{0,8},{8,16},{16,24},{24,28},{28,20},{20,12},{12,4},{4,0},{1,9},{9... | collective-permute-start | bytes 1376264 | tf_op jit(solution)/shard_map/ppermute | solution.py:139
  196.6 5.9 %collective-permute-start.40 = (f32[32,1024]{1,0:T(8,128)S(1)}, f32[32,1024]{1,0:T(8,128)S(1)}, u32[]{:S(2)}, u32[]{:S(2)}) collective-permute-start(f32[32,1024]{1,0:T(8,128)S(1)} %get-tuple-element.27), channel_id=1, source_target_pairs={{0,3},{1,2},{2,1},{3,0},{4,7},{5,6},{6,5},{7,4},{8,11},{9,10},{10,... | collective-permute-start | bytes 393224 | tf_op jit(solution)/shard_map/ppermute | solution.py:102
  196.8 7.9 %collective-permute-start.39 = (f32[32,1024]{1,0:T(8,128)S(1)}, f32[32,1024]{1,0:T(8,128)S(1)}, u32[]{:S(2)}, u32[]{:S(2)}) collective-permute-start(f32[32,1024]{1,0:T(8,128)S(1)} %get-tuple-element.28), channel_id=1, source_target_pairs={{0,2},{1,3},{2,0},{3,1},{4,6},{5,7},{6,4},{7,5},{8,10},{9,11},{10,... | collective-permute-start | bytes 393224 | tf_op jit(solution)/shard_map/ppermute | solution.py:102
  197.9 6.8 %collective-permute-start.38 = (f32[32,1024]{1,0:T(8,128)S(1)}, f32[32,1024]{1,0:T(8,128)S(1)}, u32[]{:S(2)}, u32[]{:S(2)}) collective-permute-start(f32[32,1024]{1,0:T(8,128)S(1)} %get-tuple-element.26), channel_id=1, source_target_pairs={{0,1},{1,0},{2,3},{3,2},{4,5},{5,4},{6,7},{7,6},{8,9},{9,8},{10,11... | collective-permute-start | bytes 393224 | tf_op jit(solution)/shard_map/ppermute | solution.py:102
  (17 other events, 217.0 us)
Sparse Core Ops, SparseCore 0:
  30.4 19.3 all-gather.1

commit v2 on v0

v2 whole, which is shorter than its diff:
```python
import functools

import jax
import jax.numpy as jnp
from jax import lax
from jax.experimental import pallas as pl
from jax.experimental.pallas import tpu as pltpu
from jax.sharding import PartitionSpec as P

MAXLEN = 256
LAG = 3
WAIT_SHARES = 2
WAIT_SUM = 1


def ring_order(count):
    return list(range(0, count, 2)) + list(range(1, count, 2))[::-1]


def document_kernel(window, lengths_ref, rotated_ref, grads_ref, out_ref, turned_ref):
    tokens = rotated_ref.shape[0]
    documents = lengths_ref.shape[0]

    for at in range(0, tokens, window):
        turned_ref[:, at : at + window] = rotated_ref[at : at + window, :].T

    def product(block, first, last):
        base = pl.multiple_of(block * window, window)
        row = base + lax.broadcasted_iota(jnp.int32, (window, 1), 0)
        keep = jnp.logical_and(row >= first, row < last)
        right = grads_ref[pl.ds(base, window), :]
        right = jnp.where(keep, right, jnp.zeros_like(right))
        left = turned_ref[:, pl.ds(base, window)]
        return jnp.dot(left, right, preferred_element_type=jnp.float32)

    def add(s, value):
        value = value * value
        if s > 0:
            value = out_ref[...] + value
        if s == documents - 1:
            value = value * jnp.float32(1.0 / tokens)
        out_ref[...] = value

    first = jnp.int32(0)
    for s in range(documents):
        last = first + lengths_ref[s]
        low, high = first // window, (last - 1) // window

        @pl.when(low == high)
        def _(s=s, low=low, first=first, last=last):
            add(s, product(low, first, last))

        @pl.when(low != high)
        def _(s=s, low=low, high=high, first=first, last=last):
            add(s, product(low, first, last) + product(high, first, last))

        first = last


def document_squares(rotated, grad_rows, doc_lengths):
    tokens, width = rotated.shape
    columns = grad_rows.shape[1]
    return pl.pallas_call(
        functools.partial(document_kernel, MAXLEN),
        out_shape=jax.ShapeDtypeStruct((width, columns), jnp.float32),
        in_specs=[
            pl.BlockSpec(memory_space=pltpu.SMEM),
            pl.BlockSpec(memory_space=pltpu.VMEM),
            pl.BlockSpec(memory_space=pltpu.VMEM),
        ],
        out_specs=pl.BlockSpec(memory_space=pltpu.VMEM),
        scratch_shapes=[pltpu.VMEM((width, tokens), jnp.bfloat16)],
        compiler_params=pltpu.CompilerParams(vmem_limit_bytes=40 * 1024 * 1024),
        cost_estimate=pl.CostEstimate(
            flops=2 * MAXLEN * doc_lengths.shape[0] * width * columns,
            bytes_accessed=2 * tokens * (width + columns) + 4 * width * columns,
            transcendentals=0,
        ),
    )(doc_lengths.astype(jnp.int32), rotated, grad_rows)


def rotate_kernel(hidden, *refs):
    *pieces, basis_ref, out_ref = refs
    rows = [ref[:, :hidden] for ref in pieces]
    stacked = jnp.concatenate(rows, 0) if len(rows) > 1 else rows[0]
    out_ref[...] = jnp.dot(stacked, basis_ref[...], preferred_element_type=jnp.float32)


def rotate(pieces, basis):
    hidden, width = basis.shape
    rows = sum(v.shape[0] for v in pieces)
    return pl.pallas_call(
        functools.partial(rotate_kernel, hidden),
        out_shape=jax.ShapeDtypeStruct((rows, width), jnp.float32),
        in_specs=[pl.BlockSpec(memory_space=pltpu.VMEM)] * (len(pieces) + 1),
        out_specs=pl.BlockSpec(memory_space=pltpu.VMEM),
        compiler_params=pltpu.CompilerParams(vmem_limit_bytes=16 * 1024 * 1024),
        cost_estimate=pl.CostEstimate(flops=0, bytes_accessed=0, transcendentals=0),
    )(*pieces, basis)


def solution(mesh):
    n_dp, n_tensor = mesh.shape["dp"], mesh.shape["tensor"]
    order = ring_order(n_dp)
    forward = [(order[i], order[(i + 1) % n_dp]) for i in range(n_dp)]
    backward = [(d, s) for s, d in forward]
    swaps = {d: [(t, t ^ d) for t in range(n_tensor)] for d in range(1, n_tensor)}

    def local(activations, in_basis, out_grads, out_basis, doc_lengths):
        in_basis = pltpu.with_memory_space_constraint(in_basis, pltpu.VMEM)
        mine = lax.axis_index("dp")
        me = lax.axis_index("tensor")
        spot = jnp.where(mine % 2 == 0, mine // 2, n_dp - 1 - mine // 2)
        shard = activations.shape[0]
        half = shard // 2
        tokens = shard * n_dp
        columns = out_basis.shape[1]

        def offset_of(hop, way):
            step = -hop if way == 0 else hop
            at = (spot + step) % n_dp
            source = jnp.where(2 * at < n_dp, 2 * at, 2 * (n_dp - 1 - at) + 1)
            return source * shard + way * half

        def pieces_of(block):
            return [block[:half], block[half:]]

        def pass_on(pieces):
            return [lax.ppermute(v, "dp", p) for v, p in zip(pieces, (forward, backward))]

        def share(values, t):
            rows = shard // n_tensor
            own = [lax.dynamic_slice_in_dim(v, t * rows, rows, 0) for v in values]
            return jnp.concatenate(own, 0)

        def send_shares(values):
            got = [
                lax.ppermute(share(values, me ^ d), "tensor", swaps[d])
                for d in range(1, n_tensor)
            ]
            return [share(values, me)] + got

        def send_sum(parts):
            total = functools.reduce(jnp.add, parts).astype(jnp.bfloat16)
            return [total] + [lax.ppermute(total, "tensor", swaps[d]) for d in range(1, n_tensor)]

        def by_peer(blocks, axis):
            size = blocks[0].shape[axis]
            shape = list(blocks[0].shape)
            shape[axis] *= n_tensor
            value = jnp.zeros(shape, blocks[0].dtype)
            for d, block in enumerate(blocks):
                value = lax.dynamic_update_slice_in_dim(value, block, (me ^ d) * size, axis)
            return value

        hops = n_dp - 1 + LAG
        groups = [list(range(0, 3))] + [[h, h + 1] for h in range(3, n_dp - 2, 2)]
        groups += [list(range(groups[-1][-1] + 1, n_dp))]

        act = {0: pieces_of(activations)}
        grads, partials, sums = {}, {}, {}
        flight = pass_on(act[0])
        gathered = [out_grads]
        gathered += [lax.ppermute(out_grads, "tensor", swaps[d]) for d in range(1, n_tensor)]
        partials[0] = rotate(act[0], in_basis)
        due = {1: [("features", 0, gathered)], 2: []}

        def later(hop, kind, i, value):
            due.setdefault(hop, []).append((kind, i, value))

        for hop in range(1, hops + 1):
            ready = due.pop(hop, [])
            bundle = (flight, [value for _, _, value in ready])
            arrived, values = lax.optimization_barrier(bundle)
            for (kind, i, _), value in zip(ready, values):
                if kind == "features":
                    product = jnp.dot(
                        by_peer(value, 1), out_basis, preferred_element_type=jnp.float32
                    )
                    later(hop + 1, "own", 0, product.astype(jnp.bfloat16))
                elif kind == "own":
                    grads[0] = pieces_of(value)
                elif kind == "shares":
                    later(hop + WAIT_SUM, "sums", i, send_sum(value))
                elif kind == "sums":
                    sums[i] = value
                else:
                    partials[i] = value
            if hop < n_dp:
                act[hop] = arrived
            if hop > LAG:
                grads[hop - LAG] = [v[:, -columns:] for v in arrived]
            moving = arrived
            if hop == LAG:
                moving = [jnp.concatenate([v, g], 1) for v, g in zip(arrived, grads[0])]
            if hop == n_dp - 1:
                moving = grads[hop - LAG]
            if hop < hops:
                flight = pass_on(moving)
            if hop < n_dp:
                partials[hop] = rotate(act[hop], in_basis)
            for i, group in enumerate(groups):
                if group[-1] == hop:
                    parts = send_shares([partials[h] for h in group])
                    if hop < n_dp - 1:
                        later(hop + WAIT_SHARES, "shares", i, parts)
                    else:
                        sums[i] = send_sum(parts)

        for _, items in sorted(due.items()):
            for kind, i, value in items:
                sums[i] = send_sum(value) if kind == "shares" else value

        rotated = jnp.zeros((tokens, in_basis.shape[1]), jnp.bfloat16)
        rows = shard // n_tensor
        for i, group in enumerate(groups):
            for j, h in enumerate(group):
                value = by_peer([v[j * rows : (j + 1) * rows] for v in sums[i]], 0)
                for way, piece in enumerate(pieces_of(value)):
                    rotated = lax.dynamic_update_slice_in_dim(
                        rotated, piece, offset_of(h, way), 0
                    )
        grad_rows = jnp.zeros((tokens, columns), jnp.bfloat16)
        for h, pieces in grads.items():
            for way, piece in enumerate(pieces):
                grad_rows = lax.dynamic_update_slice_in_dim(
                    grad_rows, piece, offset_of(h, way), 0
                )
        return document_squares(rotated, grad_rows, doc_lengths)

    placed = (P("dp", "tensor"), P("tensor", "dp"), P("dp", "tensor"), P(None, "tensor"), P())
    return jax.shard_map(
        local, mesh=mesh, in_specs=placed, out_specs=P("dp", "tensor"), check_vma=False
    )
```

time: 378 us -> 169 us (0.45)
  waiting for transfers between devices: 182 us -> 83.9 us
  blocking collectives: 76.5 us -> 0 us
  starting transfers between devices: 0.08 us -> 38.2 us
  local copies, waits for them, and re-layouts: 54.3 us -> 16.5 us
  matrix products: 33.3 us -> 1.28 us
  Pallas kernels: 0 us -> 21.6 us
  between operations: 13.1 us -> 0.97 us
  other arithmetic: 17.9 us -> 5.78 us
    all_gather x3 -> x0, waiting for transfers between devices: 180 us -> none  [the longest x1 111 us: local(): all_rows = lax.all_gather(activations, 'dp', axis=0, tiled=True)]
    ppermute x0 -> x47, waiting for transfers between devices: none -> 83.9 us  [the longest x20 52.5 us: pass_on(): lax.ppermute(v, 'dp', p)]
    psum x1 -> x0, blocking collectives: 76.5 us -> none  [local(): rotated = lax.psum(partial_value, 'tensor').astype(jnp.bfloat16)]
    gather x48 -> x0, local copies, waits for them, and re-layouts: 42.2 us -> none
    ppermute x0 -> x47, starting transfers between devices: none -> 38.2 us  [the longest x20 21.6 us: pass_on(): lax.ppermute(v, 'dp', p)]
    dot_general x4 -> x1, matrix products: 33.3 us -> 1.28 us  [local(): jnp.dot(by_peer(value, 1), out_basis, preferred_element_type=jnp.float32)]
    pallas_call x0 -> x9, Pallas kernels: none -> 21.6 us  [the longest x1 11.1 us: document_squares(): pl.pallas_call(functools.partial(document_kernel, MAXLEN), out_shape=jax....]
    add x2 -> x0, other arithmetic: 12.5 us -> none  [advance(): return (running + jnp.sum(blocks * blocks, axis=0), None)]
  transfers between devices with their start and end apart: 3 -> 47, of which waited for: 3 -> 26; matrix products, arithmetic and copies ran while one was open for 1% -> 6% of each run, Pallas kernels for 0% -> 6%
where the time goes in v2:
time: 169 us; the launch traced here: 168 us
  waiting for transfers between devices  83.9 us (50%)
  starting transfers between devices  38.2 us (23%)
  Pallas kernels  21.6 us (13%)
  local copies, waits for them, and re-layouts  16.5 us (10%)
  other arithmetic  5.78 us (3%)
    ppermute x20, waiting for transfers between devices, pass_on(): lax.ppermute(v, 'dp', p)  52.5 us
    ppermute x20, starting transfers between devices, pass_on(): lax.ppermute(v, 'dp', p)  21.6 us
    ppermute x12, waiting for transfers between devices, send_shares(): lax.ppermute(share(values, me ^ d), 'tensor', swaps[d])  15 us
    unnamed x20, local copies, waits for them, and re-layouts  11.3 us
    pallas_call x1, Pallas kernels, document_squares(): pl.pallas_call(functools.partial(document_kernel, MAXLEN), out_shape=jax....  11.1 us
    pallas_call x8, Pallas kernels, rotate(): pl.pallas_call(functools.partial(rotate_kernel, hidden), out_shape=jax.Sh...  10.5 us
    ppermute x12, waiting for transfers between devices, send_sum(): lax.ppermute(total, 'tensor', swaps[d])  10 us
    ppermute x12, starting transfers between devices, send_sum(): lax.ppermute(total, 'tensor', swaps[d])  7.98 us
  transfers between devices with their start and end apart: 47, of which 26 were waited for; matrix products, arithmetic and copies ran while one was open for 6% of the time, Pallas kernels for 6%

profile of v2, /device:TPU:0, one launch (start us, length us, event | category | flops | bytes accessed | tf_op | source)
XLA Modules:
  0.0 168.2 jit_solution(16681867316445850958)
XLA Ops:
  0.0 1.2 fusion
  1.2 3.0 %collective-permute-start.1 = (bf16[64,3584]{1,0:T(8,128)(2,1)S(1)}, bf16[64,3584]{1,0:T(8,128)(2,1)S(1)}, u32[]{:S(2)}, u32[]{:S(2)}) collective-permute-start(bf16[64,3584]{1,0:T(8,128)(2,1)S(1)} %get-tuple-element.105.refs_1_), channel_id=1, source_target_pairs={{8,0},{16,8},{24,16},{28,24},{20,28},{12,20},{4,12},{0,4},{9,1},{1... | collective-permute-start | bytes 1376264 | tf_op jit(solution)/shard_map/ppermute | solution.py:129
  4.4 1.9 %collective-permute-start.3 = (bf16[128,1024]{1,0:T(8,128)(2,1)}, bf16[128,1024]{1,0:T(8,128)(2,1)S(1)}, u32[]{:S(2)}, u32[]{:S(2)}) collective-permute-start(bf16[128,1024]{1,0:T(8,128)(2,1)} %param.7), channel_id=1, source_target_pairs={{0,2},{1,3},{2,0},{3,1},{4,6},{5,7},{6,4},{7,5},{8,10},{9,11},{10,... | collective-permute-start | bytes 786440 | tf_op jit(solution)/shard_map/ppermute | solution.py:164
  6.5 3.1 %copy-done = bf16[3584,1024]{1,0:T(8,128)(2,1)S(1)} copy-done((bf16[3584,1024]{1,0:T(8,128)(2,1)S(1)}, bf16[3584,1024]{1,0:T(8,128)(2,1)}, u32[]{:S(2)}) %copy-start) | copy-done | bytes 7340056
  10.8 3.0 %collective-permute-done.3 = bf16[128,1024]{1,0:T(8,128)(2,1)S(1)} collective-permute-done((bf16[128,1024]{1,0:T(8,128)(2,1)}, bf16[128,1024]{1,0:T(8,128)(2,1)S(1)}, u32[]{:S(2)}, u32[]{:S(2)}) %collective-permute-start.3) | collective-permute-done | bytes 262176 | tf_op jit(solution)/shard_map/ppermute | solution.py:164
  13.8 3.4 %collective-permute-done.4 = bf16[128,1024]{1,0:T(8,128)(2,1)S(1)} collective-permute-done((bf16[128,1024]{1,0:T(8,128)(2,1)}, bf16[128,1024]{1,0:T(8,128)(2,1)S(1)}, u32[]{:S(2)}, u32[]{:S(2)}) %collective-permute-start.4) | collective-permute-done | bytes 262176 | tf_op jit(solution)/shard_map/ppermute | solution.py:164
  17.2 1.6 collective-permute-start.5
  19.2 3.1 %copy-done.1 = bf16[3584,1024]{1,0:T(8,128)(2,1)S(1)} copy-done((bf16[3584,1024]{1,0:T(8,128)(2,1)S(1)}, bf16[3584,1024]{1,0:T(8,128)(2,1)}, u32[]{:S(2)}) %copy-start.1) | copy-done | bytes 7340056
  23.6 1.2 copy-done.5
  25.8 1.3 convolution_convert_fusion
  27.1 3.1 %collective-permute-done.5.refs_0_ = bf16[64,3584]{1,0:T(8,128)(2,1)S(1)} collective-permute-done((bf16[64,3584]{1,0:T(8,128)(2,1)S(1)}, bf16[64,3584]{1,0:T(8,128)(2,1)S(1)}, u32[]{:S(2)}, u32[]{:S(2)}) %collective-permute-start.5) | collective-permute-done | bytes 458784 | tf_op jit(solution)/shard_map/ppermute | solution.py:129
  30.2 1.4 collective-permute-done.6.refs_1_
  31.6 1.6 collective-permute-start.7
  36.0 7.7 %collective-permute-done.7.refs_0_ = bf16[64,3584]{1,0:T(8,128)(2,1)S(1)} collective-permute-done((bf16[64,3584]{1,0:T(8,128)(2,1)S(1)}, bf16[64,3584]{1,0:T(8,128)(2,1)S(1)}, u32[]{:S(2)}, u32[]{:S(2)}) %collective-permute-start.7) | collective-permute-done | bytes 458784 | tf_op jit(solution)/shard_map/ppermute | solution.py:129
  43.7 1.3 collective-permute-done.8.refs_1_
  45.9 1.6 collective-permute-start.9
  49.6 1.3 collective-permute-start.12
  51.7 3.1 %copy-done.2 = bf16[3584,1024]{1,0:T(8,128)(2,1)S(1)} copy-done((bf16[3584,1024]{1,0:T(8,128)(2,1)S(1)}, bf16[3584,1024]{1,0:T(8,128)(2,1)}, u32[]{:S(2)}) %copy-start.2) | copy-done | bytes 7340056
  56.0 5.9 %collective-permute-done.12 = f32[96,1024]{1,0:T(8,128)} collective-permute-done((f32[96,1024]{1,0:T(8,128)}, f32[96,1024]{1,0:T(8,128)}, u32[]{:S(2)}, u32[]{:S(2)}) %collective-permute-start.12) | collective-permute-done | bytes 393248 | tf_op jit(solution)/shard_map/ppermute | solution.py:138
  61.9 4.7 %collective-permute-done.13 = f32[96,1024]{1,0:T(8,128)} collective-permute-done((f32[96,1024]{1,0:T(8,128)}, f32[96,1024]{1,0:T(8,128)}, u32[]{:S(2)}, u32[]{:S(2)}) %collective-permute-start.13) | collective-permute-done | bytes 393248 | tf_op jit(solution)/shard_map/ppermute | solution.py:138
  66.6 1.3 add_convert_fusion
  68.0 2.0 %collective-permute-start.18 = (bf16[96,1024]{1,0:T(8,128)(2,1)S(1)}, bf16[96,1024]{1,0:T(8,128)(2,1)S(1)}, u32[]{:S(2)}, u32[]{:S(2)}) collective-permute-start(bf16[96,1024]{1,0:T(8,128)(2,1)S(1)} %add_convert_fusion), channel_id=1, source_target_pairs={{0,3},{1,2},{2,1},{3,0},{4,7},{5,6},{6,5},{7,4},{8,11},{9,10},{10,... | collective-permute-start | bytes 589832 | tf_op jit(solution)/shard_map/ppermute | solution.py:145
  70.2 1.6 collective-permute-start.14
  71.8 2.5 %shard_map.59 = f32[128,1024]{1,0:T(8,128)S(1)} custom-call(bf16[64,4608]{1,0:T(8,128)(2,1)} %collective-permute-done.9.refs_0_, bf16[64,4608]{1,0:T(8,128)(2,1)} %collective-permute-done.10.refs_1_, bf16[3584,1024]{1,0:T(8,128)(2,1)S(1)} %copy-done.2), custom_call_target="tpu_custom_call" | custom-call | tf_op jit(solution)/shard_map/pallas_call | solution.py:92
  77.2 2.5 %collective-permute-done.17 = bf16[96,1024]{1,0:T(8,128)(2,1)S(1)} collective-permute-done((bf16[96,1024]{1,0:T(8,128)(2,1)S(1)}, bf16[96,1024]{1,0:T(8,128)(2,1)S(1)}, u32[]{:S(2)}, u32[]{:S(2)}) %collective-permute-start.17) | collective-permute-done | bytes 196640 | tf_op jit(solution)/shard_map/ppermute | solution.py:145
  80.6 5.6 %collective-permute-done.14.refs_0_ = bf16[64,4608]{1,0:T(8,128)(2,1)S(1)} collective-permute-done((bf16[64,4608]{1,0:T(8,128)(2,1)}, bf16[64,4608]{1,0:T(8,128)(2,1)S(1)}, u32[]{:S(2)}, u32[]{:S(2)}) %collective-permute-start.14) | collective-permute-done | bytes 589856 | tf_op jit(solution)/shard_map/ppermute | solution.py:129
  86.2 3.9 %collective-permute-done.15.refs_1_ = bf16[64,4608]{1,0:T(8,128)(2,1)S(1)} collective-permute-done((bf16[64,4608]{1,0:T(8,128)(2,1)}, bf16[64,4608]{1,0:T(8,128)(2,1)S(1)}, u32[]{:S(2)}, u32[]{:S(2)}) %collective-permute-start.15) | collective-permute-done | bytes 589856 | tf_op jit(solution)/shard_map/ppermute | solution.py:129
  90.2 1.5 collective-permute-start.19
  94.1 10.8 %collective-permute-done.19.refs_0_ = bf16[64,4608]{1,0:T(8,128)(2,1)S(1)} collective-permute-done((bf16[64,4608]{1,0:T(8,128)(2,1)S(1)}, bf16[64,4608]{1,0:T(8,128)(2,1)S(1)}, u32[]{:S(2)}, u32[]{:S(2)}) %collective-permute-start.19) | collective-permute-done | bytes 589856 | tf_op jit(solution)/shard_map/ppermute | solution.py:129
  104.9 1.2 collective-permute-done.20.refs_1_
  106.3 1.8 %collective-permute-start.27 = (bf16[64,1024]{1,0:T(8,128)(2,1)S(1)}, bf16[64,1024]{1,0:T(8,128)(2,1)S(1)}, u32[]{:S(2)}, u32[]{:S(2)}) collective-permute-start(bf16[64,1024]{1,0:T(8,128)(2,1)S(1)} %add_convert_fusion.2), channel_id=1, source_target_pairs={{0,2},{1,3},{2,0},{3,1},{4,6},{5,7},{6,4},{7,5},{8,10},{9,11},{10,... | collective-permute-start | bytes 393224 | tf_op jit(solution)/shard_map/ppermute | solution.py:145
  108.8 1.2 shard_map.61
  110.0 1.5 collective-permute-start.25
  112.5 2.4 %collective-permute-done.27 = bf16[64,1024]{1,0:T(8,128)(2,1)S(1)} collective-permute-done((bf16[64,1024]{1,0:T(8,128)(2,1)S(1)}, bf16[64,1024]{1,0:T(8,128)(2,1)S(1)}, u32[]{:S(2)}, u32[]{:S(2)}) %collective-permute-start.27) | collective-permute-done | bytes 131104 | tf_op jit(solution)/shard_map/ppermute | solution.py:145
  116.0 7.8 %collective-permute-done.24.refs_0_ = bf16[64,4608]{1,0:T(8,128)(2,1)S(1)} collective-permute-done((bf16[64,4608]{1,0:T(8,128)(2,1)S(1)}, bf16[64,4608]{1,0:T(8,128)(2,1)S(1)}, u32[]{:S(2)}, u32[]{:S(2)}) %collective-permute-start.24) | collective-permute-done | bytes 589856 | tf_op jit(solution)/shard_map/ppermute | solution.py:129
  123.8 1.6 collective-permute-done.25.refs_1_
  125.6 1.5 collective-permute-start.30
  129.1 1.4 collective-permute-start.41
  132.2 1.3 collective-permute-start.37
  134.4 3.9 %collective-permute-done.40 = f32[32,1024]{1,0:T(8,128)S(1)} collective-permute-done((f32[32,1024]{1,0:T(8,128)S(1)}, f32[32,1024]{1,0:T(8,128)S(1)}, u32[]{:S(2)}, u32[]{:S(2)}) %collective-permute-start.40) | collective-permute-done | bytes 131104 | tf_op jit(solution)/shard_map/ppermute | solution.py:138
  138.4 1.3 collective-permute-start.43
  139.8 1.2 collective-permute-done.42
  141.5 3.8 %collective-permute-done.43 = bf16[32,1024]{1,0:T(8,128)(2,1)S(1)} collective-permute-done((bf16[32,1024]{1,0:T(8,128)(2,1)S(1)}, bf16[32,1024]{1,0:T(8,128)(2,1)S(1)}, u32[]{:S(2)}, u32[]{:S(2)}) %collective-permute-start.43) | collective-permute-done | bytes 65568 | tf_op jit(solution)/shard_map/ppermute | solution.py:145
  145.9 1.5 collective-permute-start.35
  147.5 2.9 %collective-permute-done.34 = bf16[64,1024]{1,0:T(8,128)(2,1)S(1)} collective-permute-done((bf16[64,1024]{1,0:T(8,128)(2,1)S(1)}, bf16[64,1024]{1,0:T(8,128)(2,1)S(1)}, u32[]{:S(2)}, u32[]{:S(2)}) %collective-permute-start.34) | collective-permute-done | bytes 131104 | tf_op jit(solution)/shard_map/ppermute | solution.py:129
  152.1 1.5 collective-permute-start.46
  153.9 2.7 %collective-permute-done.45 = bf16[64,1024]{1,0:T(8,128)(2,1)S(1)} collective-permute-done((bf16[64,1024]{1,0:T(8,128)(2,1)S(1)}, bf16[64,1024]{1,0:T(8,128)(2,1)S(1)}, u32[]{:S(2)}, u32[]{:S(2)}) %collective-permute-start.45) | collective-permute-done | bytes 131104 | tf_op jit(solution)/shard_map/ppermute | solution.py:129
  157.2 11.1 %shard_map.63 = f32[1024,1024]{1,0:T(8,128)} custom-call(s32[8]{0:T(128)S(1)} %copy-done.3, bf16[1024,1024]{1,0:T(8,128)(2,1)S(1)} %slice_dynamic-update-slice_fusion.rotated_ref, bf16[1024,1024]{1,0:T(8,128)(2,1)S(1)} %constant_dynamic-update-slice_fusion.grads_ref), custom_call_target="tpu_custom_call" | custom-call | flops 4294967296 | bytes 8388608 | tf_op jit(solution)/shard_map/pallas_call | solution.py:63
  (171 shorter events, 29.5 us)
Async XLA Ops:
  1.2 16.0 %collective-permute-start.1 = (bf16[64,3584]{1,0:T(8,128)(2,1)S(1)}, bf16[64,3584]{1,0:T(8,128)(2,1)S(1)}, u32[]{:S(2)}, u32[]{:S(2)}) collective-permute-start(bf16[64,3584]{1,0:T(8,128)(2,1)S(1)} %get-tuple-element.105.refs_1_), channel_id=1, source_target_pairs={{8,0},{16,8},{24,16},{28,24},{20,28},{12,20},{4,12},{0,4},{9,1},{1... | collective-permute-start | bytes 1376264 | tf_op jit(solution)/shard_map/ppermute | solution.py:129
  4.2 13.0 %collective-permute-start = (bf16[64,3584]{1,0:T(8,128)(2,1)S(1)}, bf16[64,3584]{1,0:T(8,128)(2,1)S(1)}, u32[]{:S(2)}, u32[]{:S(2)}) collective-permute-start(bf16[64,3584]{1,0:T(8,128)(2,1)S(1)} %get-tuple-element.106.refs_0_), channel_id=1, source_target_pairs={{0,8},{8,16},{16,24},{24,28},{28,20},{20,12},{12,4},{4,0},{1,9},{9... | collective-permute-start | bytes 1376264 | tf_op jit(solution)/shard_map/ppermute | solution.py:129
  4.4 9.4 %collective-permute-start.3 = (bf16[128,1024]{1,0:T(8,128)(2,1)}, bf16[128,1024]{1,0:T(8,128)(2,1)S(1)}, u32[]{:S(2)}, u32[]{:S(2)}) collective-permute-start(bf16[128,1024]{1,0:T(8,128)(2,1)} %param.7), channel_id=1, source_target_pairs={{0,2},{1,3},{2,0},{3,1},{4,6},{5,7},{6,4},{7,5},{8,10},{9,11},{10,... | collective-permute-start | bytes 786440 | tf_op jit(solution)/shard_map/ppermute | solution.py:164
  6.3 7.5 %collective-permute-start.2 = (bf16[128,1024]{1,0:T(8,128)(2,1)}, bf16[128,1024]{1,0:T(8,128)(2,1)S(1)}, u32[]{:S(2)}, u32[]{:S(2)}) collective-permute-start(bf16[128,1024]{1,0:T(8,128)(2,1)} %param.7), channel_id=1, source_target_pairs={{0,1},{1,0},{2,3},{3,2},{4,5},{5,4},{6,7},{7,6},{8,9},{9,8},{10,11... | collective-permute-start | bytes 786440 | tf_op jit(solution)/shard_map/ppermute | solution.py:164
  6.3 10.9 %collective-permute-start.4 = (bf16[128,1024]{1,0:T(8,128)(2,1)}, bf16[128,1024]{1,0:T(8,128)(2,1)S(1)}, u32[]{:S(2)}, u32[]{:S(2)}) collective-permute-start(bf16[128,1024]{1,0:T(8,128)(2,1)} %param.7), channel_id=1, source_target_pairs={{0,3},{1,2},{2,1},{3,0},{4,7},{5,6},{6,5},{7,4},{8,11},{9,10},{10,... | collective-permute-start | bytes 786440 | tf_op jit(solution)/shard_map/ppermute | solution.py:164
  17.2 13.0 %collective-permute-start.5 = (bf16[64,3584]{1,0:T(8,128)(2,1)S(1)}, bf16[64,3584]{1,0:T(8,128)(2,1)S(1)}, u32[]{:S(2)}, u32[]{:S(2)}) collective-permute-start(bf16[64,3584]{1,0:T(8,128)(2,1)S(1)} %collective-permute-done.refs_0_), channel_id=1, source_target_pairs={{0,8},{8,16},{16,24},{24,28},{28,20},{20,12},{12,4},{4,0},{1,9},{9... | collective-permute-start | bytes 1376264 | tf_op jit(solution)/shard_map/ppermute | solution.py:129
  18.8 12.9 %collective-permute-start.6 = (bf16[64,3584]{1,0:T(8,128)(2,1)S(1)}, bf16[64,3584]{1,0:T(8,128)(2,1)S(1)}, u32[]{:S(2)}, u32[]{:S(2)}) collective-permute-start(bf16[64,3584]{1,0:T(8,128)(2,1)S(1)} %collective-permute-done.1.refs_1_), channel_id=1, source_target_pairs={{8,0},{16,8},{24,16},{28,24},{20,28},{12,20},{4,12},{0,4},{9,1},{1... | collective-permute-start | bytes 1376264 | tf_op jit(solution)/shard_map/ppermute | solution.py:129
  31.6 12.1 %collective-permute-start.7 = (bf16[64,3584]{1,0:T(8,128)(2,1)S(1)}, bf16[64,3584]{1,0:T(8,128)(2,1)S(1)}, u32[]{:S(2)}, u32[]{:S(2)}) collective-permute-start(bf16[64,3584]{1,0:T(8,128)(2,1)S(1)} %collective-permute-done.5.refs_0_), channel_id=1, source_target_pairs={{0,8},{8,16},{16,24},{24,28},{28,20},{20,12},{12,4},{4,0},{1,9},{9... | collective-permute-start | bytes 1376264 | tf_op jit(solution)/shard_map/ppermute | solution.py:129
  33.2 11.8 %collective-permute-start.8 = (bf16[64,3584]{1,0:T(8,128)(2,1)S(1)}, bf16[64,3584]{1,0:T(8,128)(2,1)S(1)}, u32[]{:S(2)}, u32[]{:S(2)}) collective-permute-start(bf16[64,3584]{1,0:T(8,128)(2,1)S(1)} %collective-permute-done.6.refs_1_), channel_id=1, source_target_pairs={{8,0},{16,8},{24,16},{28,24},{20,28},{12,20},{4,12},{0,4},{9,1},{1... | collective-permute-start | bytes 1376264 | tf_op jit(solution)/shard_map/ppermute | solution.py:129
  35.6 20.3 %collective-permute-start.11 = (f32[96,1024]{1,0:T(8,128)}, f32[96,1024]{1,0:T(8,128)}, u32[]{:S(2)}, u32[]{:S(2)}) collective-permute-start(f32[96,1024]{1,0:T(8,128)} %pad_maximum_fusion.3), channel_id=1, source_target_pairs={{0,1},{1,0},{2,3},{3,2},{4,5},{5,4},{6,7},{7,6},{8,9},{9,8},{10,11... | collective-permute-start | bytes 1179656 | tf_op jit(solution)/shard_map/ppermute | solution.py:138
  45.9 20.8 %collective-permute-start.9 = (bf16[64,4608]{1,0:T(8,128)(2,1)}, bf16[64,4608]{1,0:T(8,128)(2,1)}, u32[]{:S(2)}, u32[]{:S(2)}) collective-permute-start(bf16[64,4608]{1,0:T(8,128)(2,1)} %pad_maximum_fusion), channel_id=1, source_target_pairs={{0,8},{8,16},{16,24},{24,28},{28,20},{20,12},{12,4},{4,0},{1,9},{9... | collective-permute-start | bytes 1769480 | tf_op jit(solution)/shard_map/ppermute | solution.py:129
  48.3 18.3 %collective-permute-start.10 = (bf16[64,4608]{1,0:T(8,128)(2,1)}, bf16[64,4608]{1,0:T(8,128)(2,1)}, u32[]{:S(2)}, u32[]{:S(2)}) collective-permute-start(bf16[64,4608]{1,0:T(8,128)(2,1)} %pad_maximum_fusion.1), channel_id=1, source_target_pairs={{8,0},{16,8},{24,16},{28,24},{20,28},{12,20},{4,12},{0,4},{9,1},{1... | collective-permute-start | bytes 1769480 | tf_op jit(solution)/shard_map/ppermute | solution.py:129
  49.6 12.4 %collective-permute-start.12 = (f32[96,1024]{1,0:T(8,128)}, f32[96,1024]{1,0:T(8,128)}, u32[]{:S(2)}, u32[]{:S(2)}) collective-permute-start(f32[96,1024]{1,0:T(8,128)} %pad_maximum_fusion.4), channel_id=1, source_target_pairs={{0,2},{1,3},{2,0},{3,1},{4,6},{5,7},{6,4},{7,5},{8,10},{9,11},{10,... | collective-permute-start | bytes 1179656 | tf_op jit(solution)/shard_map/ppermute | solution.py:138
  51.7 15.0 %collective-permute-start.13 = (f32[96,1024]{1,0:T(8,128)}, f32[96,1024]{1,0:T(8,128)}, u32[]{:S(2)}, u32[]{:S(2)}) collective-permute-start(f32[96,1024]{1,0:T(8,128)} %pad_maximum_fusion.5), channel_id=1, source_target_pairs={{0,3},{1,2},{2,1},{3,0},{4,7},{5,6},{6,5},{7,4},{8,11},{9,10},{10,... | collective-permute-start | bytes 1179656 | tf_op jit(solution)/shard_map/ppermute | solution.py:138
  68.0 9.1 %collective-permute-start.18 = (bf16[96,1024]{1,0:T(8,128)(2,1)S(1)}, bf16[96,1024]{1,0:T(8,128)(2,1)S(1)}, u32[]{:S(2)}, u32[]{:S(2)}) collective-permute-start(bf16[96,1024]{1,0:T(8,128)(2,1)S(1)} %add_convert_fusion), channel_id=1, source_target_pairs={{0,3},{1,2},{2,1},{3,0},{4,7},{5,6},{6,5},{7,4},{8,11},{9,10},{10,... | collective-permute-start | bytes 589832 | tf_op jit(solution)/shard_map/ppermute | solution.py:145
  69.9 9.7 %collective-permute-start.17 = (bf16[96,1024]{1,0:T(8,128)(2,1)S(1)}, bf16[96,1024]{1,0:T(8,128)(2,1)S(1)}, u32[]{:S(2)}, u32[]{:S(2)}) collective-permute-start(bf16[96,1024]{1,0:T(8,128)(2,1)S(1)} %add_convert_fusion), channel_id=1, source_target_pairs={{0,2},{1,3},{2,0},{3,1},{4,6},{5,7},{6,4},{7,5},{8,10},{9,11},{10,... | collective-permute-start | bytes 589832 | tf_op jit(solution)/shard_map/ppermute | solution.py:145
  70.2 9.7 %collective-permute-start.16 = (bf16[96,1024]{1,0:T(8,128)(2,1)S(1)}, bf16[96,1024]{1,0:T(8,128)(2,1)S(1)}, u32[]{:S(2)}, u32[]{:S(2)}) collective-permute-start(bf16[96,1024]{1,0:T(8,128)(2,1)S(1)} %add_convert_fusion), channel_id=1, source_target_pairs={{0,1},{1,0},{2,3},{3,2},{4,5},{5,4},{6,7},{7,6},{8,9},{9,8},{10,11... | collective-permute-start | bytes 589832 | tf_op jit(solution)/shard_map/ppermute | solution.py:145
  70.2 16.0 %collective-permute-start.14 = (bf16[64,4608]{1,0:T(8,128)(2,1)}, bf16[64,4608]{1,0:T(8,128)(2,1)S(1)}, u32[]{:S(2)}, u32[]{:S(2)}) collective-permute-start(bf16[64,4608]{1,0:T(8,128)(2,1)} %collective-permute-done.9.refs_0_), channel_id=1, source_target_pairs={{0,8},{8,16},{16,24},{24,28},{28,20},{20,12},{12,4},{4,0},{1,9},{9... | collective-permute-start | bytes 1769480 | tf_op jit(solution)/shard_map/ppermute | solution.py:129
  71.8 21.0 %slice-start.2 = ((s8[7340032]{0:T(1024)(128)(4,1)}), s8[4194304]{0:T(1024)(128)(4,1)S(1)}, s32[]{:S(2)}) async-start(s8[7340032]{0:T(1024)(128)(4,1)} %bitcast.4), calls=%async_computation.2 | async-start | bytes 8388608
  74.3 15.7 %collective-permute-start.15 = (bf16[64,4608]{1,0:T(8,128)(2,1)}, bf16[64,4608]{1,0:T(8,128)(2,1)S(1)}, u32[]{:S(2)}, u32[]{:S(2)}) collective-permute-start(bf16[64,4608]{1,0:T(8,128)(2,1)} %collective-permute-done.10.refs_1_), channel_id=1, source_target_pairs={{8,0},{16,8},{24,16},{28,24},{20,28},{12,20},{4,12},{0,4},{9,1},{1... | collective-permute-start | bytes 1769480 | tf_op jit(solution)/shard_map/ppermute | solution.py:129
  77.1 17.0 %collective-permute-start.21 = (f32[64,1024]{1,0:T(8,128)S(1)}, f32[64,1024]{1,0:T(8,128)S(1)}, u32[]{:S(2)}, u32[]{:S(2)}) collective-permute-start(f32[64,1024]{1,0:T(8,128)S(1)} %pad_maximum_fusion.7), channel_id=1, source_target_pairs={{0,1},{1,0},{2,3},{3,2},{4,5},{5,4},{6,7},{7,6},{8,9},{9,8},{10,11... | collective-permute-start | bytes 786440 | tf_op jit(solution)/shard_map/ppermute | solution.py:138
  79.6 14.5 %collective-permute-start.22 = (f32[64,1024]{1,0:T(8,128)S(1)}, f32[64,1024]{1,0:T(8,128)S(1)}, u32[]{:S(2)}, u32[]{:S(2)}) collective-permute-start(f32[64,1024]{1,0:T(8,128)S(1)} %pad_maximum_fusion.8), channel_id=1, source_target_pairs={{0,2},{1,3},{2,0},{3,1},{4,6},{5,7},{6,4},{7,5},{8,10},{9,11},{10,... | collective-permute-start | bytes 786440 | tf_op jit(solution)/shard_map/ppermute | solution.py:138
  79.9 14.2 %collective-permute-start.23 = (f32[64,1024]{1,0:T(8,128)S(1)}, f32[64,1024]{1,0:T(8,128)S(1)}, u32[]{:S(2)}, u32[]{:S(2)}) collective-permute-start(f32[64,1024]{1,0:T(8,128)S(1)} %pad_maximum_fusion.9), channel_id=1, source_target_pairs={{0,3},{1,2},{2,1},{3,0},{4,7},{5,6},{6,5},{7,4},{8,11},{9,10},{10,... | collective-permute-start | bytes 786440 | tf_op jit(solution)/shard_map/ppermute | solution.py:138
  90.2 14.7 %collective-permute-start.19 = (bf16[64,4608]{1,0:T(8,128)(2,1)S(1)}, bf16[64,4608]{1,0:T(8,128)(2,1)S(1)}, u32[]{:S(2)}, u32[]{:S(2)}) collective-permute-start(bf16[64,4608]{1,0:T(8,128)(2,1)S(1)} %collective-permute-done.14.refs_0_), channel_id=1, source_target_pairs={{0,8},{8,16},{16,24},{24,28},{28,20},{20,12},{12,4},{4,0},{1,9},{9... | collective-permute-start | bytes 1769480 | tf_op jit(solution)/shard_map/ppermute | solution.py:129
  91.8 14.4 %collective-permute-start.20 = (bf16[64,4608]{1,0:T(8,128)(2,1)S(1)}, bf16[64,4608]{1,0:T(8,128)(2,1)S(1)}, u32[]{:S(2)}, u32[]{:S(2)}) collective-permute-start(bf16[64,4608]{1,0:T(8,128)(2,1)S(1)} %collective-permute-done.15.refs_1_), channel_id=1, source_target_pairs={{8,0},{16,8},{24,16},{28,24},{20,28},{12,20},{4,12},{0,4},{9,1},{1... | collective-permute-start | bytes 1769480 | tf_op jit(solution)/shard_map/ppermute | solution.py:129
  106.2 5.6 %collective-permute-start.28 = (bf16[64,1024]{1,0:T(8,128)(2,1)S(1)}, bf16[64,1024]{1,0:T(8,128)(2,1)S(1)}, u32[]{:S(2)}, u32[]{:S(2)}) collective-permute-start(bf16[64,1024]{1,0:T(8,128)(2,1)S(1)} %add_convert_fusion.2), channel_id=1, source_target_pairs={{0,3},{1,2},{2,1},{3,0},{4,7},{5,6},{6,5},{7,4},{8,11},{9,10},{10,... | collective-permute-start | bytes 393224 | tf_op jit(solution)/shard_map/ppermute | solution.py:145
  106.3 8.6 %collective-permute-start.27 = (bf16[64,1024]{1,0:T(8,128)(2,1)S(1)}, bf16[64,1024]{1,0:T(8,128)(2,1)S(1)}, u32[]{:S(2)}, u32[]{:S(2)}) collective-permute-start(bf16[64,1024]{1,0:T(8,128)(2,1)S(1)} %add_convert_fusion.2), channel_id=1, source_target_pairs={{0,2},{1,3},{2,0},{3,1},{4,6},{5,7},{6,4},{7,5},{8,10},{9,11},{10,... | collective-permute-start | bytes 393224 | tf_op jit(solution)/shard_map/ppermute | solution.py:145
  108.1 6.8 %collective-permute-start.26 = (bf16[64,1024]{1,0:T(8,128)(2,1)S(1)}, bf16[64,1024]{1,0:T(8,128)(2,1)S(1)}, u32[]{:S(2)}, u32[]{:S(2)}) collective-permute-start(bf16[64,1024]{1,0:T(8,128)(2,1)S(1)} %add_convert_fusion.2), channel_id=1, source_target_pairs={{0,1},{1,0},{2,3},{3,2},{4,5},{5,4},{6,7},{7,6},{8,9},{9,8},{10,11... | collective-permute-start | bytes 393224 | tf_op jit(solution)/shard_map/ppermute | solution.py:145
  108.1 15.7 %collective-permute-start.24 = (bf16[64,4608]{1,0:T(8,128)(2,1)S(1)}, bf16[64,4608]{1,0:T(8,128)(2,1)S(1)}, u32[]{:S(2)}, u32[]{:S(2)}) collective-permute-start(bf16[64,4608]{1,0:T(8,128)(2,1)S(1)} %collective-permute-done.19.refs_0_), channel_id=1, source_target_pairs={{0,8},{8,16},{16,24},{24,28},{28,20},{20,12},{12,4},{4,0},{1,9},{9... | collective-permute-start | bytes 1769480 | tf_op jit(solution)/shard_map/ppermute | solution.py:129
  110.0 15.4 %collective-permute-start.25 = (bf16[64,4608]{1,0:T(8,128)(2,1)S(1)}, bf16[64,4608]{1,0:T(8,128)(2,1)S(1)}, u32[]{:S(2)}, u32[]{:S(2)}) collective-permute-start(bf16[64,4608]{1,0:T(8,128)(2,1)S(1)} %collective-permute-done.20.refs_1_), channel_id=1, source_target_pairs={{8,0},{16,8},{24,16},{28,24},{20,28},{12,20},{4,12},{0,4},{9,1},{1... | collective-permute-start | bytes 1769480 | tf_op jit(solution)/shard_map/ppermute | solution.py:129
  111.8 17.3 %collective-permute-start.31 = (f32[64,1024]{1,0:T(8,128)S(1)}, f32[64,1024]{1,0:T(8,128)S(1)}, u32[]{:S(2)}, u32[]{:S(2)}) collective-permute-start(f32[64,1024]{1,0:T(8,128)S(1)} %pad_maximum_fusion.11), channel_id=1, source_target_pairs={{0,1},{1,0},{2,3},{3,2},{4,5},{5,4},{6,7},{7,6},{8,9},{9,8},{10,11... | collective-permute-start | bytes 786440 | tf_op jit(solution)/shard_map/ppermute | solution.py:138
  114.9 14.2 %collective-permute-start.32 = (f32[64,1024]{1,0:T(8,128)S(1)}, f32[64,1024]{1,0:T(8,128)S(1)}, u32[]{:S(2)}, u32[]{:S(2)}) collective-permute-start(f32[64,1024]{1,0:T(8,128)S(1)} %pad_maximum_fusion.12), channel_id=1, source_target_pairs={{0,2},{1,3},{2,0},{3,1},{4,6},{5,7},{6,4},{7,5},{8,10},{9,11},{10,... | collective-permute-start | bytes 786440 | tf_op jit(solution)/shard_map/ppermute | solution.py:138
  114.9 15.6 %collective-permute-start.33 = (f32[64,1024]{1,0:T(8,128)S(1)}, f32[64,1024]{1,0:T(8,128)S(1)}, u32[]{:S(2)}, u32[]{:S(2)}) collective-permute-start(f32[64,1024]{1,0:T(8,128)S(1)} %pad_maximum_fusion.13), channel_id=1, source_target_pairs={{0,3},{1,2},{2,1},{3,0},{4,7},{5,6},{6,5},{7,4},{8,11},{9,10},{10,... | collective-permute-start | bytes 786440 | tf_op jit(solution)/shard_map/ppermute | solution.py:138
  125.6 5.7 %collective-permute-start.30 = (bf16[64,1024]{1,0:T(8,128)(2,1)S(1)}, bf16[64,1024]{1,0:T(8,128)(2,1)S(1)}, u32[]{:S(2)}, u32[]{:S(2)}) collective-permute-start(bf16[64,1024]{1,0:T(8,128)(2,1)S(1)} %get-tuple-element.108), channel_id=1, source_target_pairs={{8,0},{16,8},{24,16},{28,24},{20,28},{12,20},{4,12},{0,4},{9,1},{1... | collective-permute-start | bytes 393224 | tf_op jit(solution)/shard_map/ppermute | solution.py:129
  127.1 5.0 %collective-permute-start.29 = (bf16[64,1024]{1,0:T(8,128)(2,1)S(1)}, bf16[64,1024]{1,0:T(8,128)(2,1)S(1)}, u32[]{:S(2)}, u32[]{:S(2)}) collective-permute-start(bf16[64,1024]{1,0:T(8,128)(2,1)S(1)} %get-tuple-element.110), channel_id=1, source_target_pairs={{0,8},{8,16},{16,24},{24,28},{28,20},{20,12},{12,4},{4,0},{1,9},{9... | collective-permute-start | bytes 393224 | tf_op jit(solution)/shard_map/ppermute | solution.py:129
  129.0 4.5 %collective-permute-start.39 = (f32[32,1024]{1,0:T(8,128)S(1)}, f32[32,1024]{1,0:T(8,128)S(1)}, u32[]{:S(2)}, u32[]{:S(2)}) collective-permute-start(f32[32,1024]{1,0:T(8,128)S(1)} %get-tuple-element.111), channel_id=1, source_target_pairs={{0,1},{1,0},{2,3},{3,2},{4,5},{5,4},{6,7},{7,6},{8,9},{9,8},{10,11... | collective-permute-start | bytes 393224 | tf_op jit(solution)/shard_map/ppermute | solution.py:138
  129.1 5.3 %collective-permute-start.41 = (f32[32,1024]{1,0:T(8,128)S(1)}, f32[32,1024]{1,0:T(8,128)S(1)}, u32[]{:S(2)}, u32[]{:S(2)}) collective-permute-start(f32[32,1024]{1,0:T(8,128)S(1)} %get-tuple-element.112), channel_id=1, source_target_pairs={{0,3},{1,2},{2,1},{3,0},{4,7},{5,6},{6,5},{7,4},{8,11},{9,10},{10,... | collective-permute-start | bytes 393224 | tf_op jit(solution)/shard_map/ppermute | solution.py:138
  130.5 7.9 %collective-permute-start.40 = (f32[32,1024]{1,0:T(8,128)S(1)}, f32[32,1024]{1,0:T(8,128)S(1)}, u32[]{:S(2)}, u32[]{:S(2)}) collective-permute-start(f32[32,1024]{1,0:T(8,128)S(1)} %get-tuple-element.113), channel_id=1, source_target_pairs={{0,2},{1,3},{2,0},{3,1},{4,6},{5,7},{6,4},{7,5},{8,10},{9,11},{10,... | collective-permute-start | bytes 393224 | tf_op jit(solution)/shard_map/ppermute | solution.py:138
  132.1 15.3 %collective-permute-start.38 = (bf16[64,1024]{1,0:T(8,128)(2,1)S(1)}, bf16[64,1024]{1,0:T(8,128)(2,1)S(1)}, u32[]{:S(2)}, u32[]{:S(2)}) collective-permute-start(bf16[64,1024]{1,0:T(8,128)(2,1)S(1)} %add_convert_fusion.1), channel_id=1, source_target_pairs={{0,3},{1,2},{2,1},{3,0},{4,7},{5,6},{6,5},{7,4},{8,11},{9,10},{10,... | collective-permute-start | bytes 393224 | tf_op jit(solution)/shard_map/ppermute | solution.py:145
  132.2 15.3 %collective-permute-start.37 = (bf16[64,1024]{1,0:T(8,128)(2,1)S(1)}, bf16[64,1024]{1,0:T(8,128)(2,1)S(1)}, u32[]{:S(2)}, u32[]{:S(2)}) collective-permute-start(bf16[64,1024]{1,0:T(8,128)(2,1)S(1)} %add_convert_fusion.1), channel_id=1, source_target_pairs={{0,2},{1,3},{2,0},{3,1},{4,6},{5,7},{6,4},{7,5},{8,10},{9,11},{10,... | collective-permute-start | bytes 393224 | tf_op jit(solution)/shard_map/ppermute | solution.py:145
  133.5 13.9 %collective-permute-start.36 = (bf16[64,1024]{1,0:T(8,128)(2,1)S(1)}, bf16[64,1024]{1,0:T(8,128)(2,1)S(1)}, u32[]{:S(2)}, u32[]{:S(2)}) collective-permute-start(bf16[64,1024]{1,0:T(8,128)(2,1)S(1)} %add_convert_fusion.1), channel_id=1, source_target_pairs={{0,1},{1,0},{2,3},{3,2},{4,5},{5,4},{6,7},{7,6},{8,9},{9,8},{10,11... | collective-permute-start | bytes 393224 | tf_op jit(solution)/shard_map/ppermute | solution.py:145
  138.4 6.9 %collective-permute-start.43 = (bf16[32,1024]{1,0:T(8,128)(2,1)S(1)}, bf16[32,1024]{1,0:T(8,128)(2,1)S(1)}, u32[]{:S(2)}, u32[]{:S(2)}) collective-permute-start(bf16[32,1024]{1,0:T(8,128)(2,1)S(1)} %get-tuple-element.104), channel_id=1, source_target_pairs={{0,2},{1,3},{2,0},{3,1},{4,6},{5,7},{6,4},{7,5},{8,10},{9,11},{10,... | collective-permute-start | bytes 196616 | tf_op jit(solution)/shard_map/ppermute | solution.py:145
  139.7 1.3 collective-permute-start.42
  141.0 4.9 %collective-permute-start.44 = (bf16[32,1024]{1,0:T(8,128)(2,1)S(1)}, bf16[32,1024]{1,0:T(8,128)(2,1)S(1)}, u32[]{:S(2)}, u32[]{:S(2)}) collective-permute-start(bf16[32,1024]{1,0:T(8,128)(2,1)S(1)} %get-tuple-element.104), channel_id=1, source_target_pairs={{0,3},{1,2},{2,1},{3,0},{4,7},{5,6},{6,5},{7,4},{8,11},{9,10},{10,... | collective-permute-start | bytes 196616 | tf_op jit(solution)/shard_map/ppermute | solution.py:145
  145.4 5.0 %collective-permute-start.34 = (bf16[64,1024]{1,0:T(8,128)(2,1)S(1)}, bf16[64,1024]{1,0:T(8,128)(2,1)S(1)}, u32[]{:S(2)}, u32[]{:S(2)}) collective-permute-start(bf16[64,1024]{1,0:T(8,128)(2,1)S(1)} %collective-permute-done.29), channel_id=1, source_target_pairs={{0,8},{8,16},{16,24},{24,28},{28,20},{20,12},{12,4},{4,0},{1,9},{9... | collective-permute-start | bytes 393224 | tf_op jit(solution)/shard_map/ppermute | solution.py:129
  145.9 5.5 %collective-permute-start.35 = (bf16[64,1024]{1,0:T(8,128)(2,1)S(1)}, bf16[64,1024]{1,0:T(8,128)(2,1)S(1)}, u32[]{:S(2)}, u32[]{:S(2)}) collective-permute-start(bf16[64,1024]{1,0:T(8,128)(2,1)S(1)} %collective-permute-done.30), channel_id=1, source_target_pairs={{8,0},{16,8},{24,16},{28,24},{20,28},{12,20},{4,12},{0,4},{9,1},{1... | collective-permute-start | bytes 393224 | tf_op jit(solution)/shard_map/ppermute | solution.py:129
  151.5 5.0 %collective-permute-start.45 = (bf16[64,1024]{1,0:T(8,128)(2,1)S(1)}, bf16[64,1024]{1,0:T(8,128)(2,1)S(1)}, u32[]{:S(2)}, u32[]{:S(2)}) collective-permute-start(bf16[64,1024]{1,0:T(8,128)(2,1)S(1)} %collective-permute-done.34), channel_id=1, source_target_pairs={{0,8},{8,16},{16,24},{24,28},{28,20},{20,12},{12,4},{4,0},{1,9},{9... | collective-permute-start | bytes 393224 | tf_op jit(solution)/shard_map/ppermute | solution.py:129
  152.1 5.0 %collective-permute-start.46 = (bf16[64,1024]{1,0:T(8,128)(2,1)S(1)}, bf16[64,1024]{1,0:T(8,128)(2,1)S(1)}, u32[]{:S(2)}, u32[]{:S(2)}) collective-permute-start(bf16[64,1024]{1,0:T(8,128)(2,1)S(1)} %collective-permute-done.35), channel_id=1, source_target_pairs={{8,0},{16,8},{24,16},{28,24},{20,28},{12,20},{4,12},{0,4},{9,1},{1... | collective-permute-start | bytes 393224 | tf_op jit(solution)/shard_map/ppermute | solution.py:129
  (9 other events, 58.9 us)

commit v3 on v0

v3 whole, which is shorter than its diff:
```python
import functools

import jax
import jax.numpy as jnp
from jax import lax
from jax.experimental import pallas as pl
from jax.experimental.pallas import tpu as pltpu
from jax.sharding import PartitionSpec as P

MAXLEN = 256
LAG = 3
TILE = 16
SMALL_VMEM = 8 * 1024 * 1024
DOCUMENT_VMEM = 20 * 1024 * 1024
FREE = pl.CostEstimate(flops=0, bytes_accessed=0, transcendentals=0)
SMEM = pl.BlockSpec(memory_space=pltpu.SMEM)
VMEM = pl.BlockSpec(memory_space=pltpu.VMEM)
ANY = pl.BlockSpec(memory_space=pl.ANY)


def ring_order(count):
    return list(range(0, count, 2)) + list(range(1, count, 2))[::-1]


def call(kernel, shapes, in_specs, *operands, scratch=()):
    return pl.pallas_call(
        kernel,
        out_shape=[jax.ShapeDtypeStruct(*shape) for shape in shapes],
        in_specs=in_specs,
        out_specs=[VMEM] * len(shapes),
        scratch_shapes=list(scratch),
        compiler_params=pltpu.CompilerParams(vmem_limit_bytes=SMALL_VMEM),
        cost_estimate=FREE,
    )(*operands)


def product_of(piece_refs, basis_ref):
    hidden = basis_ref.shape[0]
    pieces = [ref[:, :hidden] for ref in piece_refs]
    return jnp.dot(
        jnp.concatenate(pieces, 0), basis_ref[...], preferred_element_type=jnp.float32
    )


def rotate_pair_kernel(me_ref, *refs):
    *piece_refs, basis_ref, kept_ref, sent_ref = refs
    product = product_of(piece_refs, basis_ref)
    rows = product.shape[0] // 2
    low = me_ref[0] % 2 == 0
    kept_ref[...] = jnp.where(low, product[:rows], product[rows:])
    sent_ref[...] = jnp.where(low, product[rows:], product[:rows])


def rotate_pair(me, pieces, basis):
    rows = sum(v.shape[0] for v in pieces) // 2
    shape = ((rows, basis.shape[1]), jnp.float32)
    specs = [SMEM] + [VMEM] * (len(pieces) + 1)
    return call(rotate_pair_kernel, [shape] * 2, specs, me, *pieces, basis)


def rotate_shares_kernel(count, me_ref, *refs):
    piece_refs, (basis_ref, *share_refs, product_ref) = refs[:-count - 2], refs[-count - 2 :]
    product_ref[...] = product_of(piece_refs, basis_ref)
    rows = share_refs[0].shape[0]
    for d, share_ref in enumerate(share_refs):
        at = pl.multiple_of((me_ref[0] ^ d) * rows, rows)
        share_ref[...] = product_ref[pl.ds(at, rows), :]


def rotate_shares(me, pieces, basis, count):
    rows, width = sum(v.shape[0] for v in pieces), basis.shape[1]
    return call(
        functools.partial(rotate_shares_kernel, count),
        [((rows // count, width), jnp.float32)] * count,
        [SMEM] + [VMEM] * (len(pieces) + 1),
        me,
        *pieces,
        basis,
        scratch=[pltpu.VMEM((rows, width), jnp.float32)],
    )


def add_halve_kernel(j, me_ref, left_ref, right_ref, kept_ref, sent_ref):
    rows = kept_ref.shape[0]
    side = (me_ref[0] >> j) & 1
    for out_ref, at in ((kept_ref, side), (sent_ref, 1 - side)):
        span = pl.ds(pl.multiple_of(at * rows, rows), rows)
        out_ref[...] = left_ref[span, :] + right_ref[span, :]


def add_halve(me, pair, j):
    rows, width = pair[0].shape
    shape = ((rows // 2, width), jnp.float32)
    return call(functools.partial(add_halve_kernel, j), [shape] * 2, [SMEM, VMEM, VMEM], me, *pair)


def own_grads_kernel(me_ref, *refs):
    *feature_refs, basis_ref, out_ref, total_ref = refs
    d, k = pl.program_id(0), pl.program_id(1)
    block = basis_ref.shape[0]

    @pl.when(jnp.logical_and(d == 0, k == 0))
    def _():
        total_ref[...] = jnp.zeros_like(total_ref)

    for i, feature_ref in enumerate(feature_refs):

        @pl.when(d == i)
        def _(feature_ref=feature_ref):
            left = feature_ref[:, pl.ds(pl.multiple_of(k * block, block), block)]
            total_ref[...] += jnp.dot(left, basis_ref[...], preferred_element_type=jnp.float32)

    out_ref[...] = total_ref[...].astype(out_ref.dtype)


def own_grads(me, features, basis):
    rows, depth = features[0].shape
    width = basis.shape[1]
    block = next(n for n in (512, 256, 128, depth) if depth % n == 0)
    steps = depth // block
    return pl.pallas_call(
        own_grads_kernel,
        out_shape=jax.ShapeDtypeStruct((rows, width), jnp.bfloat16),
        grid_spec=pltpu.PrefetchScalarGridSpec(
            num_scalar_prefetch=1,
            grid=(len(features), steps),
            in_specs=[pl.BlockSpec((rows, depth), lambda d, k, me: (0, 0)) for _ in features]
            + [pl.BlockSpec((block, width), lambda d, k, me: ((me[0] ^ d) * steps + k, 0))],
            out_specs=pl.BlockSpec((rows, width), lambda d, k, me: (0, 0)),
            scratch_shapes=[pltpu.VMEM((rows, width), jnp.float32)],
        ),
        compiler_params=pltpu.CompilerParams(vmem_limit_bytes=SMALL_VMEM),
        cost_estimate=FREE,
    )(me, *features, basis)


def document_kernel(window, places, lengths_ref, me_ref, *refs):
    count = len(places)
    block_refs, (out_ref, rotated_ref, grads_ref, turned_ref, sems) = refs[:count], refs[count:]
    tokens, columns = grads_ref.shape
    documents = lengths_ref.shape[0]

    copies = []
    for n, (ref, (is_grads, row, rows, begin)) in enumerate(zip(block_refs, places)):
        source = ref.at[pl.ds(row, rows), :]
        if is_grads and ref.shape[1] > columns:
            source = ref.at[pl.ds(row, rows), pl.ds(ref.shape[1] - columns, columns)]
        at = pl.multiple_of(begin(me_ref[0], me_ref[1]), TILE)
        target = (grads_ref if is_grads else rotated_ref).at[pl.ds(at, rows), :]
        copies.append(pltpu.make_async_copy(source, target, sems.at[n]))
    for copy in copies:
        copy.start()
    for copy in copies:
        copy.wait()

    for at in range(0, tokens, window):
        turned_ref[:, at : at + window] = rotated_ref[at : at + window, :].T

    def product(block, first, last):
        base = pl.multiple_of(block * window, window)
        row = base + lax.broadcasted_iota(jnp.int32, (window, 1), 0)
        keep = jnp.logical_and(row >= first, row < last)
        right = grads_ref[pl.ds(base, window), :]
        right = jnp.where(keep, right, jnp.zeros_like(right))
        left = turned_ref[:, pl.ds(base, window)]
        return jnp.dot(left, right, preferred_element_type=jnp.float32)

    def add(s, value):
        value = value * value
        if s > 0:
            value = out_ref[...] + value
        if s == documents - 1:
            value = value * jnp.float32(1.0 / tokens)
        out_ref[...] = value

    first = jnp.int32(0)
    for s in range(documents):
        last = first + lengths_ref[s]
        low, high = first // window, (last - 1) // window

        @pl.when(low == high)
        def _(s=s, low=low, first=first, last=last):
            add(s, product(low, first, last))

        @pl.when(low != high)
        def _(s=s, low=low, high=high, first=first, last=last):
            add(s, product(low, first, last) + product(high, first, last))

        first = last


def document_squares(me, blocks, places, doc_lengths, tokens, width, columns):
    return pl.pallas_call(
        functools.partial(document_kernel, MAXLEN, places),
        out_shape=jax.ShapeDtypeStruct((width, columns), jnp.float32),
        in_specs=[SMEM, SMEM] + [ANY] * len(blocks),
        out_specs=VMEM,
        scratch_shapes=[
            pltpu.VMEM((tokens, width), jnp.bfloat16),
            pltpu.VMEM((tokens, columns), jnp.bfloat16),
            pltpu.VMEM((width, tokens), jnp.bfloat16),
            pltpu.SemaphoreType.DMA((len(blocks),)),
        ],
        compiler_params=pltpu.CompilerParams(vmem_limit_bytes=DOCUMENT_VMEM),
        cost_estimate=FREE,
    )(doc_lengths.astype(jnp.int32), me, *blocks)


def solution(mesh):
    n_dp, n_tensor = mesh.shape["dp"], mesh.shape["tensor"]
    order = ring_order(n_dp)
    forward = [(order[i], order[(i + 1) % n_dp]) for i in range(n_dp)]
    backward = [(d, s) for s, d in forward]
    swaps = {d: [(t, t ^ d) for t in range(n_tensor)] for d in range(1, n_tensor)}
    depth = n_tensor.bit_length() - 1

    def local(activations, in_basis, out_grads, out_basis, doc_lengths):
        shard = activations.shape[0]
        half = shard // 2
        tokens = shard * n_dp
        width, columns = in_basis.shape[1], out_basis.shape[1]
        basis = pltpu.with_memory_space_constraint(in_basis, pltpu.VMEM)

        mine = lax.axis_index("dp")
        spot = jnp.where(mine % 2 == 0, mine // 2, n_dp - 1 - mine // 2)
        me = jnp.stack([lax.axis_index("tensor"), spot]).astype(jnp.int32)
        activations, me = lax.optimization_barrier((activations, me))

        def begin_of(hops, row, owner_row):
            def begin(index, spot):
                at = row + owner_row(index)
                hop = hops[0] + at // shard if len(hops) > 1 else hops[0]
                way = (at % shard) // half
                place = lax.rem(spot + jnp.where(way == 0, n_dp - hop, hop), jnp.int32(n_dp))
                source = jnp.where(2 * place < n_dp, 2 * place, 2 * (n_dp - 1 - place) + 1)
                return source * shard + at % shard

            return begin

        def halves(block):
            return [block[:half], block[half:]]

        def pass_on(pieces):
            return [lax.ppermute(v, "dp", p) for v, p in zip(pieces, (forward, backward))]

        def swap(block, d):
            return lax.ppermute(block, "tensor", swaps[d])

        stages = [("halve", j) for j in range(1, depth)]
        stages += [("collect", j) for j in reversed(range(depth))]

        def stage(k, state):
            kind, j = stages[k]
            held, came = state
            if kind == "halve":
                kept, sent = add_halve(me, (held, came), j)
                return kept, swap(sent, 1 << j)
            if j == depth - 1:
                held = (held + came).astype(jnp.bfloat16)
            else:
                held = jnp.concatenate([held, came], 0)
            return held, swap(held, 1 << j)

        def direct_middle(parts):
            total = functools.reduce(jnp.add, parts).astype(jnp.bfloat16)
            return [total] + [swap(total, d) for d in range(1, n_tensor)]

        hops = n_dp - 1 + LAG
        groups = [[h, h + 1] for h in range(0, n_dp, 2)]
        if shard // n_tensor >= TILE:
            groups = groups[:-1] + [[n_dp - 2], [n_dp - 1]]

        act = {0: halves(activations)}
        grads, sums = {}, {}
        flight = pass_on(act[0])
        features = [out_grads] + [swap(out_grads, d) for d in range(1, n_tensor)]
        due = {2: [("features", 0, features)]}

        def later(hop, kind, i, value):
            due.setdefault(hop, []).append((kind, i, value))

        def start_shares(group):
            parts = rotate_shares(me, [v for h in group for v in act[h]], basis, n_tensor)
            return [parts[0]] + [swap(parts[d], d) for d in range(1, n_tensor)]

        for hop in range(1, hops + 1):
            ready = due.pop(hop, [])
            bundle = (flight, [value for _, _, value in ready])
            arrived, values = lax.optimization_barrier(bundle)
            got = {(kind, i): value for (kind, i, _), value in zip(ready, values)}
            if ("features", 0) in got:
                later(hop + 1, "own", 0, own_grads(me, got["features", 0], out_basis))
            if ("own", 0) in got:
                grads[0] = halves(got["own", 0])
            if hop < n_dp:
                act[hop] = arrived
            if hop > LAG:
                grads[hop - LAG] = arrived
            moving = arrived
            if hop == LAG:
                moving = [jnp.concatenate([v, g], 1) for v, g in zip(arrived, grads[0])]
            if hop == n_dp - 1:
                moving = [v[:, -columns:] for v in arrived]
            if hop < hops:
                flight = pass_on(moving)
            for (kind, i), value in got.items():
                if kind == "product":
                    later(hop + 1, 0, i, (value[0], swap(value[1], 1)))
                elif kind == "shares":
                    later(hop + 1, "total", i, direct_middle(value))
                elif kind == "total" or kind == len(stages):
                    sums[i] = value
                elif isinstance(kind, int):
                    later(hop + 1, kind + 1, i, stage(kind, value))
            for i, group in enumerate(groups):
                if group[-1] != hop:
                    continue
                if len(group) == 1 and hop == n_dp - 1:
                    sums[i] = direct_middle(start_shares(group))
                elif len(group) == 1:
                    later(hop + 1, "shares", i, start_shares(group))
                else:
                    product = rotate_pair(me, [v for h in group for v in act[h]], basis)
                    if hop < n_dp - 3:
                        later(hop + 1, "product", i, product)
                    else:
                        later(hop + 1, 0, i, (product[0], swap(product[1], 1)))

        for _, items in sorted(due.items()):
            for kind, i, value in items:
                if isinstance(kind, int):
                    for k in range(kind, len(stages)):
                        value = stage(k, value)
                sums[i] = value

        blocks, places = [], []
        for i, group in enumerate(groups):
            if len(group) == 1:
                rows = shard // n_tensor
                for d, block in enumerate(sums[i]):
                    owner_row = lambda me, d=d, rows=rows: (me ^ d) * rows
                    blocks.append(block)
                    places.append((False, 0, rows, begin_of(group, 0, owner_row)))
                continue
            rows = 2 * shard // n_tensor
            around = [0]
            for j in reversed(range(depth)):
                around = around + [d ^ (1 << j) for d in around]
            for n, d in enumerate(around):

                def owner_row(me, d=d):
                    bits = [((me ^ d) >> j) & 1 for j in range(depth)]
                    return sum(bit * (2 * shard >> (j + 1)) for j, bit in enumerate(bits))

                block = sums[i][2 * n // len(around)]
                blocks.append(block)
                row = n % (len(around) // 2) * rows
                places.append((False, row, rows, begin_of(group, 0, owner_row)))
        for h, pieces in grads.items():
            for way, piece in enumerate(pieces):
                blocks.append(piece)
                owner_row = lambda me, way=way: jnp.int32(way * half)
                places.append((True, 0, half, begin_of([h], 0, owner_row)))
        return document_squares(me, blocks, places, doc_lengths, tokens, width, columns)

    placed = (P("dp", "tensor"), P("tensor", "dp"), P("dp", "tensor"), P(None, "tensor"), P())
    return jax.shard_map(
        local, mesh=mesh, in_specs=placed, out_specs=P("dp", "tensor"), check_vma=False
    )
```

time: 378 us -> 153 us (0.40)
  waiting for transfers between devices: 182 us -> 68.7 us
  blocking collectives: 76.5 us -> 0 us
  local copies, waits for them, and re-layouts: 54.3 us -> 7.83 us
  starting transfers between devices: 0.08 us -> 41.8 us
  Pallas kernels: 0 us -> 33.8 us
  matrix products: 33.3 us -> 0 us
  other arithmetic: 17.9 us -> 0.31 us
  between operations: 13.1 us -> 0.46 us
    all_gather x3 -> x0, waiting for transfers between devices: 180 us -> none  [the longest x1 111 us: local(): all_rows = lax.all_gather(activations, 'dp', axis=0, tiled=True)]
    psum x1 -> x0, blocking collectives: 76.5 us -> none  [local(): rotated = lax.psum(partial_value, 'tensor').astype(jnp.bfloat16)]
    ppermute x0 -> x47, waiting for transfers between devices: none -> 68.7 us  [the longest x27 38.8 us: swap(): return lax.ppermute(block, 'tensor', swaps[d])]
    gather x48 -> x0, local copies, waits for them, and re-layouts: 42.2 us -> none
    ppermute x0 -> x47, starting transfers between devices: none -> 41.8 us  [the longest x20 21.6 us: pass_on(): lax.ppermute(v, 'dp', p)]
    pallas_call x0 -> x10, Pallas kernels: none -> 33.8 us  [the longest x1 16.8 us: document_squares(): pl.pallas_call(functools.partial(document_kernel, MAXLEN, places), out_sh...]
    dot_general x4 -> x0, matrix products: 33.3 us -> none  [the longest x2 14.2 us: advance(): jnp.einsum('gtj,gtk->gjk', left_rows, right_rows, preferred_element_type=...]
    add x2 -> x0, other arithmetic: 12.5 us -> none  [advance(): return (running + jnp.sum(blocks * blocks, axis=0), None)]
  transfers between devices with their start and end apart: 3 -> 47, of which waited for: 3 -> 27; matrix products, arithmetic and copies ran while one was open for 1% -> 0% of each run, Pallas kernels for 0% -> 11%
where the time goes in v3:
time: 153 us
  waiting for transfers between devices  68.7 us (45%)
  starting transfers between devices  41.8 us (27%)
  Pallas kernels  33.8 us (22%)
  local copies, waits for them, and re-layouts  7.83 us (5%)
    ppermute x27, waiting for transfers between devices, swap(): return lax.ppermute(block, 'tensor', swaps[d])  38.8 us
    ppermute x20, waiting for transfers between devices, pass_on(): lax.ppermute(v, 'dp', p)  30 us
    ppermute x20, starting transfers between devices, pass_on(): lax.ppermute(v, 'dp', p)  21.6 us
    ppermute x27, starting transfers between devices, swap(): return lax.ppermute(block, 'tensor', swaps[d])  20.1 us
    pallas_call x1, Pallas kernels, document_squares(): pl.pallas_call(functools.partial(document_kernel, MAXLEN, places), out_sh...  16.8 us
    pallas_call x8, Pallas kernels, call(): pl.pallas_call(kernel, out_shape=[jax.ShapeDtypeStruct(*shape) for shape...  13.4 us
    unnamed x15, local copies, waits for them, and re-layouts  6.51 us
    pallas_call x1, Pallas kernels, own_grads(): pl.pallas_call(own_grads_kernel, out_shape=jax.ShapeDtypeStruct((rows, wi...  3.58 us
  transfers between devices with their start and end apart: 47, of which 27 were waited for; matrix products, arithmetic and copies ran while one was open for 0% of the time, Pallas kernels for 11%

profile of v3, /device:TPU:0, one launch (start us, length us, event | category | flops | bytes accessed | tf_op | source)
XLA Modules:
  0.0 152.9 jit_solution(13153805546757628900)
XLA Ops:
  0.1 1.2 fusion
  1.3 3.0 %collective-permute-start.1 = (bf16[64,3584]{1,0:T(8,128)(2,1)S(1)}, bf16[64,3584]{1,0:T(8,128)(2,1)S(1)}, u32[]{:S(2)}, u32[]{:S(2)}) collective-permute-start(bf16[64,3584]{1,0:T(8,128)(2,1)S(1)} %get-tuple-element.171.refs_1_), channel_id=1, source_target_pairs={{8,0},{16,8},{24,16},{28,24},{20,28},{12,20},{4,12},{0,4},{9,1},{1... | collective-permute-start | bytes 1376264 | tf_op jit(solution)/shard_map/ppermute | solution.py:244
  4.5 10.5 %collective-permute-done.1.refs_3_ = bf16[64,3584]{1,0:T(8,128)(2,1)S(1)} collective-permute-done((bf16[64,3584]{1,0:T(8,128)(2,1)S(1)}, bf16[64,3584]{1,0:T(8,128)(2,1)S(1)}, u32[]{:S(2)}, u32[]{:S(2)}) %collective-permute-start.1) | collective-permute-done | bytes 458784 | tf_op jit(solution)/shard_map/ppermute | solution.py:244
  14.9 1.4 collective-permute-done.refs_2_
  16.7 1.6 %collective-permute-start.3 = (bf16[64,3584]{1,0:T(8,128)(2,1)S(1)}, bf16[64,3584]{1,0:T(8,128)(2,1)S(1)}, u32[]{:S(2)}, u32[]{:S(2)}) collective-permute-start(bf16[64,3584]{1,0:T(8,128)(2,1)S(1)} %collective-permute-done.1.refs_3_), channel_id=1, source_target_pairs={{8,0},{16,8},{24,16},{28,24},{20,28},{12,20},{4,12},{0,4},{9,1},{1... | collective-permute-start | bytes 1376264 | tf_op jit(solution)/shard_map/ppermute | solution.py:244
  18.3 1.5 collective-permute-start.5
  20.5 3.1 %copy-done = bf16[3584,1024]{1,0:T(8,128)(2,1)S(1)} copy-done((bf16[3584,1024]{1,0:T(8,128)(2,1)S(1)}, bf16[3584,1024]{1,0:T(8,128)(2,1)}, u32[]{:S(2)}) %copy-start) | copy-done | bytes 7340056
  23.6 2.6 %shard_map.55 = (f32[128,1024]{1,0:T(8,128)S(1)}, f32[128,1024]{1,0:T(8,128)S(1)}) custom-call(s32[2]{0:T(128)S(1)} %pad_add_fusion.me_ref, bf16[64,3584]{1,0:T(8,128)(2,1)S(1)} %get-tuple-element.172.refs_0_, bf16[64,3584]{1,0:T(8,128)(2,1)S(1)} %get-tuple-element.171.refs_1_, bf16[64,3584]{1,0:T(8,128)(2,1)S(1)} %collective-permute-done.refs_2_, ...), custom_call_target="tpu_custom_call" | custom-call | tf_op jit(solution)/shard_map/pallas_call | solution.py:26
  26.6 2.7 %collective-permute-done.6.refs_3_ = bf16[128,1024]{1,0:T(8,128)(2,1)S(1)} collective-permute-done((bf16[128,1024]{1,0:T(8,128)(2,1)S(1)}, bf16[128,1024]{1,0:T(8,128)(2,1)S(1)}, u32[]{:S(2)}, u32[]{:S(2)}) %collective-permute-start.6) | collective-permute-done | bytes 262176 | tf_op jit(solution)/shard_map/ppermute | solution.py:247
  30.9 1.4 collective-permute-start.8
  32.2 3.4 %copy-done.1 = bf16[4096,1024]{1,0:T(8,128)(2,1)S(1)} copy-done((bf16[4096,1024]{1,0:T(8,128)(2,1)S(1)}, bf16[4096,1024]{1,0:T(8,128)(2,1)}, u32[]{:S(2)}) %copy-start.1) | copy-done | bytes 8388632
  35.6 3.6 %shard_map.56 = bf16[128,1024]{1,0:T(8,128)(2,1)S(1)} custom-call(s32[2]{0:T(128)S(1)} %pad_add_fusion.me_ref, bf16[128,1024]{1,0:T(8,128)(2,1)S(1)} %copy-done.2, bf16[128,1024]{1,0:T(8,128)(2,1)S(1)} %collective-permute-done.4.refs_1_, bf16[128,1024]{1,0:T(8,128)(2,1)S(1)} %collective-permute-done.5.refs_2_, ...), custom_call_target="tpu_custom_call" | custom-call | tf_op jit(solution)/shard_map/pallas_call | solution.py:121
  39.2 3.5 %collective-permute-done.7.refs_2_ = bf16[64,3584]{1,0:T(8,128)(2,1)S(1)} collective-permute-done((bf16[64,3584]{1,0:T(8,128)(2,1)S(1)}, bf16[64,3584]{1,0:T(8,128)(2,1)S(1)}, u32[]{:S(2)}, u32[]{:S(2)}) %collective-permute-start.7) | collective-permute-done | bytes 458784 | tf_op jit(solution)/shard_map/ppermute | solution.py:244
  43.2 1.6 %collective-permute-start.10 = (bf16[64,4608]{1,0:T(8,128)(2,1)S(1)}, bf16[64,4608]{1,0:T(8,128)(2,1)S(1)}, u32[]{:S(2)}, u32[]{:S(2)}) collective-permute-start(bf16[64,4608]{1,0:T(8,128)(2,1)S(1)} %pad_maximum_fusion), channel_id=1, source_target_pairs={{0,8},{8,16},{16,24},{24,28},{28,20},{20,12},{12,4},{4,0},{1,9},{9... | collective-permute-start | bytes 1769480 | tf_op jit(solution)/shard_map/ppermute | solution.py:244
  46.0 1.5 collective-permute-start.12
  47.5 2.7 %shard_map.58 = (f32[128,1024]{1,0:T(8,128)S(1)}, f32[128,1024]{1,0:T(8,128)S(1)}) custom-call(s32[2]{0:T(128)S(1)} %pad_add_fusion.me_ref, bf16[64,3584]{1,0:T(8,128)(2,1)S(1)} %collective-permute-done.2.refs_0_, bf16[64,3584]{1,0:T(8,128)(2,1)S(1)} %collective-permute-done.3.refs_1_, bf16[64,3584]{1,0:T(8,128)(2,1)S(1)} %collective-permute-done.7.refs_2_, ...), custom_call_target="tpu_custom_call" | custom-call | tf_op jit(solution)/shard_map/pallas_call | solution.py:26
  50.2 2.4 %collective-permute-done.12 = f32[64,1024]{1,0:T(8,128)S(1)} collective-permute-done((f32[64,1024]{1,0:T(8,128)S(1)}, f32[64,1024]{1,0:T(8,128)S(1)}, u32[]{:S(2)}, u32[]{:S(2)}) %collective-permute-start.12) | collective-permute-done | bytes 262176 | tf_op jit(solution)/shard_map/ppermute | solution.py:247
  52.6 4.8 %collective-permute-done.10.refs_0_.refs_22_ = bf16[64,4608]{1,0:T(8,128)(2,1)S(1)} collective-permute-done((bf16[64,4608]{1,0:T(8,128)(2,1)S(1)}, bf16[64,4608]{1,0:T(8,128)(2,1)S(1)}, u32[]{:S(2)}, u32[]{:S(2)}) %collective-permute-start.10) | collective-permute-done | bytes 589856 | tf_op jit(solution)/shard_map/ppermute | solution.py:244
  57.4 1.3 collective-permute-done.11.refs_1_.refs_23_
  58.7 1.6 %collective-permute-start.13 = (bf16[64,4608]{1,0:T(8,128)(2,1)S(1)}, bf16[64,4608]{1,0:T(8,128)(2,1)S(1)}, u32[]{:S(2)}, u32[]{:S(2)}) collective-permute-start(bf16[64,4608]{1,0:T(8,128)(2,1)S(1)} %collective-permute-done.10.refs_0_.refs_22_), channel_id=1, source_target_pairs={{0,8},{8,16},{16,24},{24,28},{28,20},{20,12},{12,4},{4,0},{1,9},{9... | collective-permute-start | bytes 1769480 | tf_op jit(solution)/shard_map/ppermute | solution.py:244
  60.8 1.6 %collective-permute-start.15 = (bf16[64,1024]{1,0:T(8,128)(2,1)S(1)}, bf16[64,1024]{1,0:T(8,128)(2,1)S(1)}, u32[]{:S(2)}, u32[]{:S(2)}) collective-permute-start(bf16[64,1024]{1,0:T(8,128)(2,1)S(1)} %add_convert_fusion.2), channel_id=1, source_target_pairs={{0,2},{1,3},{2,0},{3,1},{4,6},{5,7},{6,4},{7,5},{8,10},{9,11},{10,... | collective-permute-start | bytes 393224 | tf_op jit(solution)/shard_map/ppermute | solution.py:247
  62.3 4.4 %collective-permute-done.15 = bf16[64,1024]{1,0:T(8,128)(2,1)S(1)} collective-permute-done((bf16[64,1024]{1,0:T(8,128)(2,1)S(1)}, bf16[64,1024]{1,0:T(8,128)(2,1)S(1)}, u32[]{:S(2)}, u32[]{:S(2)}) %collective-permute-start.15) | collective-permute-done | bytes 131104 | tf_op jit(solution)/shard_map/ppermute | solution.py:247
  66.7 4.9 %collective-permute-done.13.refs_2_.refs_24_ = bf16[64,4608]{1,0:T(8,128)(2,1)S(1)} collective-permute-done((bf16[64,4608]{1,0:T(8,128)(2,1)S(1)}, bf16[64,4608]{1,0:T(8,128)(2,1)S(1)}, u32[]{:S(2)}, u32[]{:S(2)}) %collective-permute-start.13) | collective-permute-done | bytes 589856 | tf_op jit(solution)/shard_map/ppermute | solution.py:244
  71.6 1.3 collective-permute-done.14.refs_3_.refs_25_
  72.9 1.5 collective-permute-start.17
  75.0 2.7 %shard_map.60 = (f32[128,1024]{1,0:T(8,128)S(1)}, f32[128,1024]{1,0:T(8,128)S(1)}) custom-call(s32[2]{0:T(128)S(1)} %pad_add_fusion.me_ref, bf16[64,4608]{1,0:T(8,128)(2,1)S(1)} %collective-permute-done.10.refs_0_.refs_22_, bf16[64,4608]{1,0:T(8,128)(2,1)S(1)} %collective-permute-done.11.refs_1_.refs_23_, ...), custom_call_target="tpu_custom_call" | custom-call | tf_op jit(solution)/shard_map/pallas_call | solution.py:26
  79.0 1.6 %collective-permute-start.20 = (f32[64,1024]{1,0:T(8,128)S(1)}, f32[64,1024]{1,0:T(8,128)S(1)}, u32[]{:S(2)}, u32[]{:S(2)}) collective-permute-start(f32[64,1024]{1,0:T(8,128)S(1)} %get-tuple-element.124), channel_id=1, source_target_pairs={{0,2},{1,3},{2,0},{3,1},{4,6},{5,7},{6,4},{7,5},{8,10},{9,11},{10,... | collective-permute-start | bytes 786440 | tf_op jit(solution)/shard_map/ppermute | solution.py:247
  80.5 6.7 %collective-permute-done.20 = f32[64,1024]{1,0:T(8,128)S(1)} collective-permute-done((f32[64,1024]{1,0:T(8,128)S(1)}, f32[64,1024]{1,0:T(8,128)S(1)}, u32[]{:S(2)}, u32[]{:S(2)}) %collective-permute-start.20) | collective-permute-done | bytes 262176 | tf_op jit(solution)/shard_map/ppermute | solution.py:247
  87.3 1.6 %collective-permute-start.22 = (bf16[64,4608]{1,0:T(8,128)(2,1)S(1)}, bf16[64,4608]{1,0:T(8,128)(2,1)S(1)}, u32[]{:S(2)}, u32[]{:S(2)}) collective-permute-start(bf16[64,4608]{1,0:T(8,128)(2,1)S(1)} %collective-permute-done.17.refs_0_.refs_26_), channel_id=1, source_target_pairs={{0,8},{8,16},{16,24},{24,28},{28,20},{20,12},{12,4},{4,0},{1,9},{9... | collective-permute-start | bytes 1769480 | tf_op jit(solution)/shard_map/ppermute | solution.py:244
  89.3 1.8 %shard_map.62 = (f32[32,1024]{1,0:T(8,128)S(1)}, f32[32,1024]{1,0:T(8,128)S(1)}, f32[32,1024]{1,0:T(8,128)S(1)}, f32[32,1024]{1,0:T(8,128)S(1)}) custom-call(s32[2]{0:T(128)S(1)} %pad_add_fusion.me_ref, bf16[64,4608]{1,0:T(8,128)(2,1)S(1)} %collective-permute-done.17.refs_0_.refs_26_, bf16[64,4608]{1,0:T(8,128)(2,1)S(1)} %collective-permute-done.18.refs_1_.refs_27_, ...), custom_call_target="tpu_custom_call" | custom-call | tf_op jit(solution)/shard_map/pallas_call | solution.py:26
  91.2 1.6 %collective-permute-start.24 = (bf16[64,1024]{1,0:T(8,128)(2,1)S(1)}, bf16[64,1024]{1,0:T(8,128)(2,1)S(1)}, u32[]{:S(2)}, u32[]{:S(2)}) collective-permute-start(bf16[64,1024]{1,0:T(8,128)(2,1)S(1)} %add_convert_fusion.1), channel_id=1, source_target_pairs={{0,2},{1,3},{2,0},{3,1},{4,6},{5,7},{6,4},{7,5},{8,10},{9,11},{10,... | collective-permute-start | bytes 393224 | tf_op jit(solution)/shard_map/ppermute | solution.py:247
  94.0 2.3 %collective-permute-done.24 = bf16[64,1024]{1,0:T(8,128)(2,1)S(1)} collective-permute-done((bf16[64,1024]{1,0:T(8,128)(2,1)S(1)}, bf16[64,1024]{1,0:T(8,128)(2,1)S(1)}, u32[]{:S(2)}, u32[]{:S(2)}) %collective-permute-start.24) | collective-permute-done | bytes 131104 | tf_op jit(solution)/shard_map/ppermute | solution.py:247
  96.2 2.2 %collective-permute-start.27 = (f32[32,1024]{1,0:T(8,128)S(1)}, f32[32,1024]{1,0:T(8,128)S(1)}, u32[]{:S(2)}, u32[]{:S(2)}) collective-permute-start(f32[32,1024]{1,0:T(8,128)S(1)} %get-tuple-element.139), channel_id=1, source_target_pairs={{0,2},{1,3},{2,0},{3,1},{4,6},{5,7},{6,4},{7,5},{8,10},{9,11},{10,... | collective-permute-start | bytes 393224 | tf_op jit(solution)/shard_map/ppermute | solution.py:247
  98.5 6.9 %collective-permute-done.27 = f32[32,1024]{1,0:T(8,128)S(1)} collective-permute-done((f32[32,1024]{1,0:T(8,128)S(1)}, f32[32,1024]{1,0:T(8,128)S(1)}, u32[]{:S(2)}, u32[]{:S(2)}) %collective-permute-start.27) | collective-permute-done | bytes 131104 | tf_op jit(solution)/shard_map/ppermute | solution.py:247
  105.4 2.0 %collective-permute-done.28 = f32[32,1024]{1,0:T(8,128)S(1)} collective-permute-done((f32[32,1024]{1,0:T(8,128)S(1)}, f32[32,1024]{1,0:T(8,128)S(1)}, u32[]{:S(2)}, u32[]{:S(2)}) %collective-permute-start.28) | collective-permute-done | bytes 131104 | tf_op jit(solution)/shard_map/ppermute | solution.py:247
  109.9 1.6 %collective-permute-start.29 = (bf16[64,1024]{1,0:T(8,128)(2,1)S(1)}, bf16[64,1024]{1,0:T(8,128)(2,1)S(1)}, u32[]{:S(2)}, u32[]{:S(2)}) collective-permute-start(bf16[64,1024]{1,0:T(8,128)(2,1)S(1)} %slice.22), channel_id=1, source_target_pairs={{0,8},{8,16},{16,24},{24,28},{28,20},{20,12},{12,4},{4,0},{1,9},{9... | collective-permute-start | bytes 393224 | tf_op jit(solution)/shard_map/ppermute | solution.py:244
  111.6 1.3 collective-permute-start.32
  113.3 1.3 collective-permute-done.33.refs_13_
  115.1 2.5 %collective-permute-done.32 = bf16[64,1024]{1,0:T(8,128)(2,1)S(1)} collective-permute-done((bf16[64,1024]{1,0:T(8,128)(2,1)S(1)}, bf16[64,1024]{1,0:T(8,128)(2,1)S(1)}, u32[]{:S(2)}, u32[]{:S(2)}) %collective-permute-start.32) | collective-permute-done | bytes 131104 | tf_op jit(solution)/shard_map/ppermute | solution.py:247
  117.7 1.5 %collective-permute-start.36 = (bf16[64,1024]{1,0:T(8,128)(2,1)S(1)}, bf16[64,1024]{1,0:T(8,128)(2,1)S(1)}, u32[]{:S(2)}, u32[]{:S(2)}) collective-permute-start(bf16[64,1024]{1,0:T(8,128)(2,1)S(1)} %collective-permute-done.29.refs_30_), channel_id=1, source_target_pairs={{0,8},{8,16},{16,24},{24,28},{28,20},{20,12},{12,4},{4,0},{1,9},{9... | collective-permute-start | bytes 393224 | tf_op jit(solution)/shard_map/ppermute | solution.py:244
  119.8 1.8 %shard_map.63 = (f32[32,1024]{1,0:T(8,128)S(1)}, f32[32,1024]{1,0:T(8,128)S(1)}, f32[32,1024]{1,0:T(8,128)S(1)}, f32[32,1024]{1,0:T(8,128)S(1)}) custom-call(s32[2]{0:T(128)S(1)} %pad_add_fusion.me_ref, bf16[64,4608]{1,0:T(8,128)(2,1)S(1)} %collective-permute-done.22.refs_0_.refs_28_, bf16[64,4608]{1,0:T(8,128)(2,1)S(1)} %collective-permute-done.23.refs_1_.refs_29_, ...), custom_call_target="tpu_custom_call" | custom-call | tf_op jit(solution)/shard_map/pallas_call | solution.py:26
  121.7 1.3 collective-permute-start.40
  124.8 1.6 %collective-permute-start.45 = (bf16[64,1024]{1,0:T(8,128)(2,1)S(1)}, bf16[64,1024]{1,0:T(8,128)(2,1)S(1)}, u32[]{:S(2)}, u32[]{:S(2)}) collective-permute-start(bf16[64,1024]{1,0:T(8,128)(2,1)S(1)} %collective-permute-done.36.refs_32_), channel_id=1, source_target_pairs={{0,8},{8,16},{16,24},{24,28},{28,20},{20,12},{12,4},{4,0},{1,9},{9... | collective-permute-start | bytes 393224 | tf_op jit(solution)/shard_map/ppermute | solution.py:244
  128.0 1.9 %collective-permute-done.41 = f32[32,1024]{1,0:T(8,128)S(1)} collective-permute-done((f32[32,1024]{1,0:T(8,128)S(1)}, f32[32,1024]{1,0:T(8,128)S(1)}, u32[]{:S(2)}, u32[]{:S(2)}) %collective-permute-start.41) | collective-permute-done | bytes 131104 | tf_op jit(solution)/shard_map/ppermute | solution.py:247
  130.0 1.4 collective-permute-start.44
  132.3 1.6 %collective-permute-done.44.refs_19_ = bf16[32,1024]{1,0:T(8,128)(2,1)S(1)} collective-permute-done((bf16[32,1024]{1,0:T(8,128)(2,1)S(1)}, bf16[32,1024]{1,0:T(8,128)(2,1)S(1)}, u32[]{:S(2)}, u32[]{:S(2)}) %collective-permute-start.44) | collective-permute-done | bytes 65568 | tf_op jit(solution)/shard_map/ppermute | solution.py:247
  133.9 2.0 %collective-permute-done.43.refs_18_ = bf16[32,1024]{1,0:T(8,128)(2,1)S(1)} collective-permute-done((bf16[32,1024]{1,0:T(8,128)(2,1)S(1)}, bf16[32,1024]{1,0:T(8,128)(2,1)S(1)}, u32[]{:S(2)}, u32[]{:S(2)}) %collective-permute-start.43) | collective-permute-done | bytes 65568 | tf_op jit(solution)/shard_map/ppermute | solution.py:247
  135.9 16.8 %shard_map.64 = f32[1024,1024]{1,0:T(8,128)} custom-call(s32[8]{0:T(128)S(1)} %copy-done.3, s32[2]{0:T(128)S(1)} %pad_add_fusion.me_ref, bf16[128,1024]{1,0:T(8,128)(2,1)S(1)} %constant_dynamic-update-slice_fusion.refs_0_.refs_1_, bf16[128,1024]{1,0:T(8,128)(2,1)S(1)} %constant_dynamic-update-slice_fusion.refs_0_.refs_1_, ...), custom_call_target="tpu_custom_call" | custom-call | tf_op jit(solution)/shard_map/pallas_call | solution.py:193
  (87 shorter events, 17.5 us)
Async XLA Ops:
  1.3 13.6 %collective-permute-start.1 = (bf16[64,3584]{1,0:T(8,128)(2,1)S(1)}, bf16[64,3584]{1,0:T(8,128)(2,1)S(1)}, u32[]{:S(2)}, u32[]{:S(2)}) collective-permute-start(bf16[64,3584]{1,0:T(8,128)(2,1)S(1)} %get-tuple-element.171.refs_1_), channel_id=1, source_target_pairs={{8,0},{16,8},{24,16},{28,24},{20,28},{12,20},{4,12},{0,4},{9,1},{1... | collective-permute-start | bytes 1376264 | tf_op jit(solution)/shard_map/ppermute | solution.py:244
  4.3 12.0 %collective-permute-start = (bf16[64,3584]{1,0:T(8,128)(2,1)S(1)}, bf16[64,3584]{1,0:T(8,128)(2,1)S(1)}, u32[]{:S(2)}, u32[]{:S(2)}) collective-permute-start(bf16[64,3584]{1,0:T(8,128)(2,1)S(1)} %get-tuple-element.172.refs_0_), channel_id=1, source_target_pairs={{0,8},{8,16},{16,24},{24,28},{28,20},{20,12},{12,4},{4,0},{1,9},{9... | collective-permute-start | bytes 1376264 | tf_op jit(solution)/shard_map/ppermute | solution.py:244
  16.3 13.0 %collective-permute-start.2 = (bf16[64,3584]{1,0:T(8,128)(2,1)S(1)}, bf16[64,3584]{1,0:T(8,128)(2,1)S(1)}, u32[]{:S(2)}, u32[]{:S(2)}) collective-permute-start(bf16[64,3584]{1,0:T(8,128)(2,1)S(1)} %collective-permute-done.refs_2_), channel_id=1, source_target_pairs={{0,8},{8,16},{16,24},{24,28},{28,20},{20,12},{12,4},{4,0},{1,9},{9... | collective-permute-start | bytes 1376264 | tf_op jit(solution)/shard_map/ppermute | solution.py:244
  16.7 12.6 %collective-permute-start.3 = (bf16[64,3584]{1,0:T(8,128)(2,1)S(1)}, bf16[64,3584]{1,0:T(8,128)(2,1)S(1)}, u32[]{:S(2)}, u32[]{:S(2)}) collective-permute-start(bf16[64,3584]{1,0:T(8,128)(2,1)S(1)} %collective-permute-done.1.refs_3_), channel_id=1, source_target_pairs={{8,0},{16,8},{24,16},{28,24},{20,28},{12,20},{4,12},{0,4},{9,1},{1... | collective-permute-start | bytes 1376264 | tf_op jit(solution)/shard_map/ppermute | solution.py:244
  18.3 8.2 %collective-permute-start.5 = (bf16[128,1024]{1,0:T(8,128)(2,1)S(1)}, bf16[128,1024]{1,0:T(8,128)(2,1)S(1)}, u32[]{:S(2)}, u32[]{:S(2)}) collective-permute-start(bf16[128,1024]{1,0:T(8,128)(2,1)S(1)} %copy-done.2), channel_id=1, source_target_pairs={{0,2},{1,3},{2,0},{3,1},{4,6},{5,7},{6,4},{7,5},{8,10},{9,11},{10,... | collective-permute-start | bytes 786440 | tf_op jit(solution)/shard_map/ppermute | solution.py:247
  19.8 6.7 %collective-permute-start.4 = (bf16[128,1024]{1,0:T(8,128)(2,1)S(1)}, bf16[128,1024]{1,0:T(8,128)(2,1)S(1)}, u32[]{:S(2)}, u32[]{:S(2)}) collective-permute-start(bf16[128,1024]{1,0:T(8,128)(2,1)S(1)} %copy-done.2), channel_id=1, source_target_pairs={{0,1},{1,0},{2,3},{3,2},{4,5},{5,4},{6,7},{7,6},{8,9},{9,8},{10,11... | collective-permute-start | bytes 786440 | tf_op jit(solution)/shard_map/ppermute | solution.py:247
  19.8 9.4 %collective-permute-start.6 = (bf16[128,1024]{1,0:T(8,128)(2,1)S(1)}, bf16[128,1024]{1,0:T(8,128)(2,1)S(1)}, u32[]{:S(2)}, u32[]{:S(2)}) collective-permute-start(bf16[128,1024]{1,0:T(8,128)(2,1)S(1)} %copy-done.2), channel_id=1, source_target_pairs={{0,3},{1,2},{2,1},{3,0},{4,7},{5,6},{6,5},{7,4},{8,11},{9,10},{10,... | collective-permute-start | bytes 786440 | tf_op jit(solution)/shard_map/ppermute | solution.py:247
  23.6 23.9 %slice-start = ((s8[7340032]{0:T(1024)(128)(4,1)}), s8[4194304]{0:T(1024)(128)(4,1)S(1)}, s32[]{:S(2)}) async-start(s8[7340032]{0:T(1024)(128)(4,1)} %bitcast.2), calls=%async_computation | async-start | bytes 8388608
  29.3 13.8 %collective-permute-start.9 = (f32[128,1024]{1,0:T(8,128)S(1)}, f32[128,1024]{1,0:T(8,128)S(1)}, u32[]{:S(2)}, u32[]{:S(2)}) collective-permute-start(f32[128,1024]{1,0:T(8,128)S(1)} %get-tuple-element.101), channel_id=1, source_target_pairs={{0,1},{1,0},{2,3},{3,2},{4,5},{5,4},{6,7},{7,6},{8,9},{9,8},{10,11... | collective-permute-start | bytes 1572872 | tf_op jit(solution)/shard_map/ppermute | solution.py:247
  30.2 12.5 %collective-permute-start.7 = (bf16[64,3584]{1,0:T(8,128)(2,1)S(1)}, bf16[64,3584]{1,0:T(8,128)(2,1)S(1)}, u32[]{:S(2)}, u32[]{:S(2)}) collective-permute-start(bf16[64,3584]{1,0:T(8,128)(2,1)S(1)} %collective-permute-done.2.refs_0_), channel_id=1, source_target_pairs={{0,8},{8,16},{16,24},{24,28},{28,20},{20,12},{12,4},{4,0},{1,9},{9... | collective-permute-start | bytes 1376264 | tf_op jit(solution)/shard_map/ppermute | solution.py:244
  30.9 12.2 %collective-permute-start.8 = (bf16[64,3584]{1,0:T(8,128)(2,1)S(1)}, bf16[64,3584]{1,0:T(8,128)(2,1)S(1)}, u32[]{:S(2)}, u32[]{:S(2)}) collective-permute-start(bf16[64,3584]{1,0:T(8,128)(2,1)S(1)} %collective-permute-done.3.refs_1_), channel_id=1, source_target_pairs={{8,0},{16,8},{24,16},{28,24},{20,28},{12,20},{4,12},{0,4},{9,1},{1... | collective-permute-start | bytes 1376264 | tf_op jit(solution)/shard_map/ppermute | solution.py:244
  43.2 14.2 %collective-permute-start.10 = (bf16[64,4608]{1,0:T(8,128)(2,1)S(1)}, bf16[64,4608]{1,0:T(8,128)(2,1)S(1)}, u32[]{:S(2)}, u32[]{:S(2)}) collective-permute-start(bf16[64,4608]{1,0:T(8,128)(2,1)S(1)} %pad_maximum_fusion), channel_id=1, source_target_pairs={{0,8},{8,16},{16,24},{24,28},{28,20},{20,12},{12,4},{4,0},{1,9},{9... | collective-permute-start | bytes 1769480 | tf_op jit(solution)/shard_map/ppermute | solution.py:244
  44.8 13.9 %collective-permute-start.11 = (bf16[64,4608]{1,0:T(8,128)(2,1)S(1)}, bf16[64,4608]{1,0:T(8,128)(2,1)S(1)}, u32[]{:S(2)}, u32[]{:S(2)}) collective-permute-start(bf16[64,4608]{1,0:T(8,128)(2,1)S(1)} %pad_maximum_fusion.1), channel_id=1, source_target_pairs={{8,0},{16,8},{24,16},{28,24},{20,28},{12,20},{4,12},{0,4},{9,1},{1... | collective-permute-start | bytes 1769480 | tf_op jit(solution)/shard_map/ppermute | solution.py:244
  46.0 6.6 %collective-permute-start.12 = (f32[64,1024]{1,0:T(8,128)S(1)}, f32[64,1024]{1,0:T(8,128)S(1)}, u32[]{:S(2)}, u32[]{:S(2)}) collective-permute-start(f32[64,1024]{1,0:T(8,128)S(1)} %get-tuple-element.108), channel_id=1, source_target_pairs={{0,2},{1,3},{2,0},{3,1},{4,6},{5,7},{6,4},{7,5},{8,10},{9,11},{10,... | collective-permute-start | bytes 786440 | tf_op jit(solution)/shard_map/ppermute | solution.py:247
  58.7 12.9 %collective-permute-start.13 = (bf16[64,4608]{1,0:T(8,128)(2,1)S(1)}, bf16[64,4608]{1,0:T(8,128)(2,1)S(1)}, u32[]{:S(2)}, u32[]{:S(2)}) collective-permute-start(bf16[64,4608]{1,0:T(8,128)(2,1)S(1)} %collective-permute-done.10.refs_0_.refs_22_), channel_id=1, source_target_pairs={{0,8},{8,16},{16,24},{24,28},{28,20},{20,12},{12,4},{4,0},{1,9},{9... | collective-permute-start | bytes 1769480 | tf_op jit(solution)/shard_map/ppermute | solution.py:244
  60.3 12.7 %collective-permute-start.14 = (bf16[64,4608]{1,0:T(8,128)(2,1)S(1)}, bf16[64,4608]{1,0:T(8,128)(2,1)S(1)}, u32[]{:S(2)}, u32[]{:S(2)}) collective-permute-start(bf16[64,4608]{1,0:T(8,128)(2,1)S(1)} %collective-permute-done.11.refs_1_.refs_23_), channel_id=1, source_target_pairs={{8,0},{16,8},{24,16},{28,24},{20,28},{12,20},{4,12},{0,4},{9,1},{1... | collective-permute-start | bytes 1769480 | tf_op jit(solution)/shard_map/ppermute | solution.py:244
  60.7 6.0 %collective-permute-start.16 = (f32[128,1024]{1,0:T(8,128)S(1)}, f32[128,1024]{1,0:T(8,128)S(1)}, u32[]{:S(2)}, u32[]{:S(2)}) collective-permute-start(f32[128,1024]{1,0:T(8,128)S(1)} %get-tuple-element.116), channel_id=1, source_target_pairs={{0,1},{1,0},{2,3},{3,2},{4,5},{5,4},{6,7},{7,6},{8,9},{9,8},{10,11... | collective-permute-start | bytes 1572872 | tf_op jit(solution)/shard_map/ppermute | solution.py:247
  60.8 6.0 %collective-permute-start.15 = (bf16[64,1024]{1,0:T(8,128)(2,1)S(1)}, bf16[64,1024]{1,0:T(8,128)(2,1)S(1)}, u32[]{:S(2)}, u32[]{:S(2)}) collective-permute-start(bf16[64,1024]{1,0:T(8,128)(2,1)S(1)} %add_convert_fusion.2), channel_id=1, source_target_pairs={{0,2},{1,3},{2,0},{3,1},{4,6},{5,7},{6,4},{7,5},{8,10},{9,11},{10,... | collective-permute-start | bytes 393224 | tf_op jit(solution)/shard_map/ppermute | solution.py:247
  72.9 14.3 %collective-permute-start.17 = (bf16[64,4608]{1,0:T(8,128)(2,1)S(1)}, bf16[64,4608]{1,0:T(8,128)(2,1)S(1)}, u32[]{:S(2)}, u32[]{:S(2)}) collective-permute-start(bf16[64,4608]{1,0:T(8,128)(2,1)S(1)} %collective-permute-done.13.refs_2_.refs_24_), channel_id=1, source_target_pairs={{0,8},{8,16},{16,24},{24,28},{28,20},{20,12},{12,4},{4,0},{1,9},{9... | collective-permute-start | bytes 1769480 | tf_op jit(solution)/shard_map/ppermute | solution.py:244
  74.4 12.8 %collective-permute-start.18 = (bf16[64,4608]{1,0:T(8,128)(2,1)S(1)}, bf16[64,4608]{1,0:T(8,128)(2,1)S(1)}, u32[]{:S(2)}, u32[]{:S(2)}) collective-permute-start(bf16[64,4608]{1,0:T(8,128)(2,1)S(1)} %collective-permute-done.14.refs_3_.refs_25_), channel_id=1, source_target_pairs={{8,0},{16,8},{24,16},{28,24},{20,28},{12,20},{4,12},{0,4},{9,1},{1... | collective-permute-start | bytes 1769480 | tf_op jit(solution)/shard_map/ppermute | solution.py:244
  77.7 9.6 %collective-permute-start.21 = (f32[128,1024]{1,0:T(8,128)S(1)}, f32[128,1024]{1,0:T(8,128)S(1)}, u32[]{:S(2)}, u32[]{:S(2)}) collective-permute-start(f32[128,1024]{1,0:T(8,128)S(1)} %get-tuple-element.126), channel_id=1, source_target_pairs={{0,1},{1,0},{2,3},{3,2},{4,5},{5,4},{6,7},{7,6},{8,9},{9,8},{10,11... | collective-permute-start | bytes 1572872 | tf_op jit(solution)/shard_map/ppermute | solution.py:247
  77.8 2.8 %collective-permute-start.19 = (bf16[128,1024]{1,0:T(8,128)(2,1)S(1)}, bf16[128,1024]{1,0:T(8,128)(2,1)S(1)}, u32[]{:S(2)}, u32[]{:S(2)}) collective-permute-start(bf16[128,1024]{1,0:T(8,128)(2,1)S(1)} %constant_dynamic-update-slice_fusion.refs_0_.refs_1_), channel_id=1, source_target_pairs={{0,1},{1,0},{2,3},{3,2},{4,5},{5,4},{6,7},{7,6},{8,9},{9,8},{10,11... | collective-permute-start | bytes 786440 | tf_op jit(solution)/shard_map/ppermute | solution.py:247
  79.0 8.3 %collective-permute-start.20 = (f32[64,1024]{1,0:T(8,128)S(1)}, f32[64,1024]{1,0:T(8,128)S(1)}, u32[]{:S(2)}, u32[]{:S(2)}) collective-permute-start(f32[64,1024]{1,0:T(8,128)S(1)} %get-tuple-element.124), channel_id=1, source_target_pairs={{0,2},{1,3},{2,0},{3,1},{4,6},{5,7},{6,4},{7,5},{8,10},{9,11},{10,... | collective-permute-start | bytes 786440 | tf_op jit(solution)/shard_map/ppermute | solution.py:247
  87.3 20.1 %collective-permute-start.22 = (bf16[64,4608]{1,0:T(8,128)(2,1)S(1)}, bf16[64,4608]{1,0:T(8,128)(2,1)S(1)}, u32[]{:S(2)}, u32[]{:S(2)}) collective-permute-start(bf16[64,4608]{1,0:T(8,128)(2,1)S(1)} %collective-permute-done.17.refs_0_.refs_26_), channel_id=1, source_target_pairs={{0,8},{8,16},{16,24},{24,28},{28,20},{20,12},{12,4},{4,0},{1,9},{9... | collective-permute-start | bytes 1769480 | tf_op jit(solution)/shard_map/ppermute | solution.py:244
  88.8 18.6 %collective-permute-start.23 = (bf16[64,4608]{1,0:T(8,128)(2,1)S(1)}, bf16[64,4608]{1,0:T(8,128)(2,1)S(1)}, u32[]{:S(2)}, u32[]{:S(2)}) collective-permute-start(bf16[64,4608]{1,0:T(8,128)(2,1)S(1)} %collective-permute-done.18.refs_1_.refs_27_), channel_id=1, source_target_pairs={{8,0},{16,8},{24,16},{28,24},{20,28},{12,20},{4,12},{0,4},{9,1},{1... | collective-permute-start | bytes 1769480 | tf_op jit(solution)/shard_map/ppermute | solution.py:244
  91.2 5.0 %collective-permute-start.24 = (bf16[64,1024]{1,0:T(8,128)(2,1)S(1)}, bf16[64,1024]{1,0:T(8,128)(2,1)S(1)}, u32[]{:S(2)}, u32[]{:S(2)}) collective-permute-start(bf16[64,1024]{1,0:T(8,128)(2,1)S(1)} %add_convert_fusion.1), channel_id=1, source_target_pairs={{0,2},{1,3},{2,0},{3,1},{4,6},{5,7},{6,4},{7,5},{8,10},{9,11},{10,... | collective-permute-start | bytes 393224 | tf_op jit(solution)/shard_map/ppermute | solution.py:247
  92.8 5.7 %collective-permute-start.26 = (f32[32,1024]{1,0:T(8,128)S(1)}, f32[32,1024]{1,0:T(8,128)S(1)}, u32[]{:S(2)}, u32[]{:S(2)}) collective-permute-start(f32[32,1024]{1,0:T(8,128)S(1)} %get-tuple-element.138), channel_id=1, source_target_pairs={{0,1},{1,0},{2,3},{3,2},{4,5},{5,4},{6,7},{7,6},{8,9},{9,8},{10,11... | collective-permute-start | bytes 393224 | tf_op jit(solution)/shard_map/ppermute | solution.py:247
  93.4 14.0 %collective-permute-start.25 = (f32[64,1024]{1,0:T(8,128)S(1)}, f32[64,1024]{1,0:T(8,128)S(1)}, u32[]{:S(2)}, u32[]{:S(2)}) collective-permute-start(f32[64,1024]{1,0:T(8,128)S(1)} %get-tuple-element.136), channel_id=1, source_target_pairs={{0,2},{1,3},{2,0},{3,1},{4,6},{5,7},{6,4},{7,5},{8,10},{9,11},{10,... | collective-permute-start | bytes 786440 | tf_op jit(solution)/shard_map/ppermute | solution.py:247
  96.2 9.1 %collective-permute-start.27 = (f32[32,1024]{1,0:T(8,128)S(1)}, f32[32,1024]{1,0:T(8,128)S(1)}, u32[]{:S(2)}, u32[]{:S(2)}) collective-permute-start(f32[32,1024]{1,0:T(8,128)S(1)} %get-tuple-element.139), channel_id=1, source_target_pairs={{0,2},{1,3},{2,0},{3,1},{4,6},{5,7},{6,4},{7,5},{8,10},{9,11},{10,... | collective-permute-start | bytes 393224 | tf_op jit(solution)/shard_map/ppermute | solution.py:247
  98.5 8.9 %collective-permute-start.28 = (f32[32,1024]{1,0:T(8,128)S(1)}, f32[32,1024]{1,0:T(8,128)S(1)}, u32[]{:S(2)}, u32[]{:S(2)}) collective-permute-start(f32[32,1024]{1,0:T(8,128)S(1)} %get-tuple-element.140), channel_id=1, source_target_pairs={{0,3},{1,2},{2,1},{3,0},{4,7},{5,6},{6,5},{7,4},{8,11},{9,10},{10,... | collective-permute-start | bytes 393224 | tf_op jit(solution)/shard_map/ppermute | solution.py:247
  107.4 4.2 %collective-permute-start.35 = (bf16[32,1024]{1,0:T(8,128)(2,1)S(1)}, bf16[32,1024]{1,0:T(8,128)(2,1)S(1)}, u32[]{:S(2)}, u32[]{:S(2)}) collective-permute-start(bf16[32,1024]{1,0:T(8,128)(2,1)S(1)} %add_convert_fusion.4.refs_12_), channel_id=1, source_target_pairs={{0,3},{1,2},{2,1},{3,0},{4,7},{5,6},{6,5},{7,4},{8,11},{9,10},{10,... | collective-permute-start | bytes 196616 | tf_op jit(solution)/shard_map/ppermute | solution.py:247
  108.5 4.8 %collective-permute-start.34 = (bf16[32,1024]{1,0:T(8,128)(2,1)S(1)}, bf16[32,1024]{1,0:T(8,128)(2,1)S(1)}, u32[]{:S(2)}, u32[]{:S(2)}) collective-permute-start(bf16[32,1024]{1,0:T(8,128)(2,1)S(1)} %add_convert_fusion.4.refs_12_), channel_id=1, source_target_pairs={{0,2},{1,3},{2,0},{3,1},{4,6},{5,7},{6,4},{7,5},{8,10},{9,11},{10,... | collective-permute-start | bytes 196616 | tf_op jit(solution)/shard_map/ppermute | solution.py:247
  109.4 5.5 %collective-permute-start.30 = (bf16[64,1024]{1,0:T(8,128)(2,1)S(1)}, bf16[64,1024]{1,0:T(8,128)(2,1)S(1)}, u32[]{:S(2)}, u32[]{:S(2)}) collective-permute-start(bf16[64,1024]{1,0:T(8,128)(2,1)S(1)} %slice.23), channel_id=1, source_target_pairs={{8,0},{16,8},{24,16},{28,24},{20,28},{12,20},{4,12},{0,4},{9,1},{1... | collective-permute-start | bytes 393224 | tf_op jit(solution)/shard_map/ppermute | solution.py:244
  109.9 5.1 %collective-permute-start.29 = (bf16[64,1024]{1,0:T(8,128)(2,1)S(1)}, bf16[64,1024]{1,0:T(8,128)(2,1)S(1)}, u32[]{:S(2)}, u32[]{:S(2)}) collective-permute-start(bf16[64,1024]{1,0:T(8,128)(2,1)S(1)} %slice.22), channel_id=1, source_target_pairs={{0,8},{8,16},{16,24},{24,28},{28,20},{20,12},{12,4},{4,0},{1,9},{9... | collective-permute-start | bytes 393224 | tf_op jit(solution)/shard_map/ppermute | solution.py:244
  111.5 6.1 %collective-permute-start.31 = (bf16[128,1024]{1,0:T(8,128)(2,1)S(1)}, bf16[128,1024]{1,0:T(8,128)(2,1)S(1)}, u32[]{:S(2)}, u32[]{:S(2)}) collective-permute-start(bf16[128,1024]{1,0:T(8,128)(2,1)S(1)} %constant_dynamic-update-slice_fusion.2.refs_4_.refs_5_), channel_id=1, source_target_pairs={{0,1},{1,0},{2,3},{3,2},{4,5},{5,4},{6,7},{7,6},{8,9},{9,8},{10,11... | collective-permute-start | bytes 786440 | tf_op jit(solution)/shard_map/ppermute | solution.py:247
  111.6 6.0 %collective-permute-start.32 = (bf16[64,1024]{1,0:T(8,128)(2,1)S(1)}, bf16[64,1024]{1,0:T(8,128)(2,1)S(1)}, u32[]{:S(2)}, u32[]{:S(2)}) collective-permute-start(bf16[64,1024]{1,0:T(8,128)(2,1)S(1)} %add_convert_fusion), channel_id=1, source_target_pairs={{0,2},{1,3},{2,0},{3,1},{4,6},{5,7},{6,4},{7,5},{8,10},{9,11},{10,... | collective-permute-start | bytes 393224 | tf_op jit(solution)/shard_map/ppermute | solution.py:247
  113.3 1.3 collective-permute-start.33
  117.6 7.2 %collective-permute-start.38 = (bf16[128,1024]{1,0:T(8,128)(2,1)S(1)}, bf16[128,1024]{1,0:T(8,128)(2,1)S(1)}, u32[]{:S(2)}, u32[]{:S(2)}) collective-permute-start(bf16[128,1024]{1,0:T(8,128)(2,1)S(1)} %constant_dynamic-update-slice_fusion.4.refs_8_.refs_9_), channel_id=1, source_target_pairs={{0,1},{1,0},{2,3},{3,2},{4,5},{5,4},{6,7},{7,6},{8,9},{9,8},{10,11... | collective-permute-start | bytes 786440 | tf_op jit(solution)/shard_map/ppermute | solution.py:247
  117.7 5.9 %collective-permute-start.36 = (bf16[64,1024]{1,0:T(8,128)(2,1)S(1)}, bf16[64,1024]{1,0:T(8,128)(2,1)S(1)}, u32[]{:S(2)}, u32[]{:S(2)}) collective-permute-start(bf16[64,1024]{1,0:T(8,128)(2,1)S(1)} %collective-permute-done.29.refs_30_), channel_id=1, source_target_pairs={{0,8},{8,16},{16,24},{24,28},{28,20},{20,12},{12,4},{4,0},{1,9},{9... | collective-permute-start | bytes 393224 | tf_op jit(solution)/shard_map/ppermute | solution.py:244
  119.3 5.6 %collective-permute-start.37 = (bf16[64,1024]{1,0:T(8,128)(2,1)S(1)}, bf16[64,1024]{1,0:T(8,128)(2,1)S(1)}, u32[]{:S(2)}, u32[]{:S(2)}) collective-permute-start(bf16[64,1024]{1,0:T(8,128)(2,1)S(1)} %collective-permute-done.30.refs_31_), channel_id=1, source_target_pairs={{8,0},{16,8},{24,16},{28,24},{20,28},{12,20},{4,12},{0,4},{9,1},{1... | collective-permute-start | bytes 393224 | tf_op jit(solution)/shard_map/ppermute | solution.py:244
  121.6 5.3 %collective-permute-start.39 = (f32[32,1024]{1,0:T(8,128)S(1)}, f32[32,1024]{1,0:T(8,128)S(1)}, u32[]{:S(2)}, u32[]{:S(2)}) collective-permute-start(f32[32,1024]{1,0:T(8,128)S(1)} %get-tuple-element.164), channel_id=1, source_target_pairs={{0,1},{1,0},{2,3},{3,2},{4,5},{5,4},{6,7},{7,6},{8,9},{9,8},{10,11... | collective-permute-start | bytes 393224 | tf_op jit(solution)/shard_map/ppermute | solution.py:247
  121.7 6.4 %collective-permute-start.40 = (f32[32,1024]{1,0:T(8,128)S(1)}, f32[32,1024]{1,0:T(8,128)S(1)}, u32[]{:S(2)}, u32[]{:S(2)}) collective-permute-start(f32[32,1024]{1,0:T(8,128)S(1)} %get-tuple-element.165), channel_id=1, source_target_pairs={{0,2},{1,3},{2,0},{3,1},{4,6},{5,7},{6,4},{7,5},{8,10},{9,11},{10,... | collective-permute-start | bytes 393224 | tf_op jit(solution)/shard_map/ppermute | solution.py:247
  123.6 6.3 %collective-permute-start.41 = (f32[32,1024]{1,0:T(8,128)S(1)}, f32[32,1024]{1,0:T(8,128)S(1)}, u32[]{:S(2)}, u32[]{:S(2)}) collective-permute-start(f32[32,1024]{1,0:T(8,128)S(1)} %get-tuple-element.166), channel_id=1, source_target_pairs={{0,3},{1,2},{2,1},{3,0},{4,7},{5,6},{6,5},{7,4},{8,11},{9,10},{10,... | collective-permute-start | bytes 393224 | tf_op jit(solution)/shard_map/ppermute | solution.py:247
  124.8 7.4 %collective-permute-start.45 = (bf16[64,1024]{1,0:T(8,128)(2,1)S(1)}, bf16[64,1024]{1,0:T(8,128)(2,1)S(1)}, u32[]{:S(2)}, u32[]{:S(2)}) collective-permute-start(bf16[64,1024]{1,0:T(8,128)(2,1)S(1)} %collective-permute-done.36.refs_32_), channel_id=1, source_target_pairs={{0,8},{8,16},{16,24},{24,28},{28,20},{20,12},{12,4},{4,0},{1,9},{9... | collective-permute-start | bytes 393224 | tf_op jit(solution)/shard_map/ppermute | solution.py:244
  126.5 5.8 %collective-permute-start.46 = (bf16[64,1024]{1,0:T(8,128)(2,1)S(1)}, bf16[64,1024]{1,0:T(8,128)(2,1)S(1)}, u32[]{:S(2)}, u32[]{:S(2)}) collective-permute-start(bf16[64,1024]{1,0:T(8,128)(2,1)S(1)} %collective-permute-done.37.refs_33_), channel_id=1, source_target_pairs={{8,0},{16,8},{24,16},{28,24},{20,28},{12,20},{4,12},{0,4},{9,1},{1... | collective-permute-start | bytes 393224 | tf_op jit(solution)/shard_map/ppermute | solution.py:244
  130.0 3.9 %collective-permute-start.44 = (bf16[32,1024]{1,0:T(8,128)(2,1)S(1)}, bf16[32,1024]{1,0:T(8,128)(2,1)S(1)}, u32[]{:S(2)}, u32[]{:S(2)}) collective-permute-start(bf16[32,1024]{1,0:T(8,128)(2,1)S(1)} %add_convert_fusion.3.refs_16_), channel_id=1, source_target_pairs={{0,3},{1,2},{2,1},{3,0},{4,7},{5,6},{6,5},{7,4},{8,11},{9,10},{10,... | collective-permute-start | bytes 196616 | tf_op jit(solution)/shard_map/ppermute | solution.py:247
  131.4 4.5 %collective-permute-start.43 = (bf16[32,1024]{1,0:T(8,128)(2,1)S(1)}, bf16[32,1024]{1,0:T(8,128)(2,1)S(1)}, u32[]{:S(2)}, u32[]{:S(2)}) collective-permute-start(bf16[32,1024]{1,0:T(8,128)(2,1)S(1)} %add_convert_fusion.3.refs_16_), channel_id=1, source_target_pairs={{0,2},{1,3},{2,0},{3,1},{4,6},{5,7},{6,4},{7,5},{8,10},{9,11},{10,... | collective-permute-start | bytes 196616 | tf_op jit(solution)/shard_map/ppermute | solution.py:247
  132.2 3.6 %collective-permute-start.42 = (bf16[32,1024]{1,0:T(8,128)(2,1)S(1)}, bf16[32,1024]{1,0:T(8,128)(2,1)S(1)}, u32[]{:S(2)}, u32[]{:S(2)}) collective-permute-start(bf16[32,1024]{1,0:T(8,128)(2,1)S(1)} %add_convert_fusion.3.refs_16_), channel_id=1, source_target_pairs={{0,1},{1,0},{2,3},{3,2},{4,5},{5,4},{6,7},{7,6},{8,9},{9,8},{10,11... | collective-permute-start | bytes 196616 | tf_op jit(solution)/shard_map/ppermute | solution.py:247
  (5 other events, 61.2 us)

commit v4 on v0

v4 whole, which is shorter than its diff:
```python
import functools

import jax
import jax.numpy as jnp
from jax import lax
from jax.experimental import pallas as pl
from jax.experimental.pallas import tpu as pltpu
from jax.sharding import PartitionSpec as P

MAXLEN = 256
GRAIN = 128
TILE = 16
SMALL_VMEM = 8 * 1024 * 1024
DOCUMENT_VMEM = 32 * 1024 * 1024
FREE = pl.CostEstimate(flops=0, bytes_accessed=0, transcendentals=0)
SMEM = pl.BlockSpec(memory_space=pltpu.SMEM)
VMEM = pl.BlockSpec(memory_space=pltpu.VMEM)


def ring_order(count):
    return list(range(0, count, 2)) + list(range(1, count, 2))[::-1]


def call(kernel, shapes, in_specs, *operands, scratch=()):
    return pl.pallas_call(
        kernel,
        out_shape=[jax.ShapeDtypeStruct(*shape) for shape in shapes],
        in_specs=in_specs,
        out_specs=[VMEM] * len(shapes),
        scratch_shapes=list(scratch),
        compiler_params=pltpu.CompilerParams(vmem_limit_bytes=SMALL_VMEM),
        cost_estimate=FREE,
    )(*operands)


def product_of(piece_refs, basis_ref):
    pieces = [ref[...] for ref in piece_refs]
    return jnp.dot(
        jnp.concatenate(pieces, 0), basis_ref[...], preferred_element_type=jnp.float32
    )


def rotate_shares_kernel(count, me_ref, *refs):
    piece_refs, (basis_ref, *share_refs, product_ref) = refs[:-count - 2], refs[-count - 2 :]
    product_ref[...] = product_of(piece_refs, basis_ref)
    rows = share_refs[0].shape[0]
    for d, share_ref in enumerate(share_refs):
        at = pl.multiple_of((me_ref[0] ^ d) * rows, rows)
        share_ref[...] = product_ref[pl.ds(at, rows), :]


def rotate_shares(me, pieces, basis, count):
    rows, width = sum(v.shape[0] for v in pieces), basis.shape[1]
    return call(
        functools.partial(rotate_shares_kernel, count),
        [((rows // count, width), jnp.float32)] * count,
        [SMEM] + [VMEM] * (len(pieces) + 1),
        me,
        *pieces,
        basis,
        scratch=[pltpu.VMEM((rows, width), jnp.float32)],
    )


def own_grads_kernel(me_ref, *refs):
    *feature_refs, basis_ref, out_ref, total_ref = refs
    d, k = pl.program_id(0), pl.program_id(1)
    block = basis_ref.shape[0]

    @pl.when(jnp.logical_and(d == 0, k == 0))
    def _():
        total_ref[...] = jnp.zeros_like(total_ref)

    for i, feature_ref in enumerate(feature_refs):

        @pl.when(d == i)
        def _(feature_ref=feature_ref):
            left = feature_ref[:, pl.ds(pl.multiple_of(k * block, block), block)]
            total_ref[...] += jnp.dot(left, basis_ref[...], preferred_element_type=jnp.float32)

    out_ref[...] = total_ref[...].astype(out_ref.dtype)


def own_grads(me, features, basis):
    rows, depth = features[0].shape
    width = basis.shape[1]
    block = next(n for n in (1024, 512, 256, 128, depth) if depth % n == 0)
    steps = depth // block
    return pl.pallas_call(
        own_grads_kernel,
        out_shape=jax.ShapeDtypeStruct((rows, width), jnp.bfloat16),
        grid_spec=pltpu.PrefetchScalarGridSpec(
            num_scalar_prefetch=1,
            grid=(len(features), steps),
            in_specs=[pl.BlockSpec((rows, depth), lambda d, k, me: (0, 0)) for _ in features]
            + [pl.BlockSpec((block, width), lambda d, k, me: ((me[0] ^ d) * steps + k, 0))],
            out_specs=pl.BlockSpec((rows, width), lambda d, k, me: (0, 0)),
            scratch_shapes=[pltpu.VMEM((rows, width), jnp.float32)],
        ),
        compiler_params=pltpu.CompilerParams(vmem_limit_bytes=SMALL_VMEM),
        cost_estimate=FREE,
    )(me, *features, basis)


def document_kernel(window, places, lengths_ref, me_ref, *refs):
    count = len(places)
    block_refs, (out_ref, *scratch) = refs[:count], refs[count:]
    rotated_ref, grads_ref, turned_ref, total_ref, out_sems = scratch
    tokens, columns = grads_ref.shape
    documents = lengths_ref.shape[0]

    for ref, (is_grads, row, rows, begin) in zip(block_refs, places):
        at = pl.multiple_of(begin(me_ref[0], me_ref[1]), TILE)
        target = grads_ref if is_grads else rotated_ref
        target[pl.ds(at, rows), :] = ref[row : row + rows, :]
    for at in range(0, tokens, window):
        turned_ref[:, at : at + window] = rotated_ref[at : at + window, :].T

    width = out_ref.shape[0]
    strip = min(width, 256)

    def add(s, size, first, last):
        base = jnp.minimum(first // GRAIN * GRAIN, tokens - size)
        base = pl.multiple_of(base, GRAIN)
        row = base + lax.broadcasted_iota(jnp.int32, (size, 1), 0)
        keep = jnp.logical_and(row >= first, row < last)
        right = grads_ref[pl.ds(base, size), :]
        right = jnp.where(keep, right, jnp.zeros_like(right))
        ends = s == documents - 1
        for at in range(0, width, strip if ends else width):
            span = slice(at, at + strip if ends else width)
            left = turned_ref[span, pl.ds(base, size)]
            value = jnp.dot(left, right, preferred_element_type=jnp.float32)
            value = value * value
            if s > 0:
                value = total_ref[span, :] + value
            if ends:
                value = value * jnp.float32(1.0 / tokens)
            total_ref[span, :] = value
            if ends:
                out_copy(at).start()

    def out_copy(at):
        span = pl.ds(at, strip)
        return pltpu.make_async_copy(
            total_ref.at[span, :], out_ref.at[span, :], out_sems.at[at // strip]
        )

    first = jnp.int32(0)
    for s in range(documents):
        last = first + lengths_ref[s]
        fits = last <= jnp.minimum(first // GRAIN * GRAIN, tokens - window) + window
        pl.when(fits)(functools.partial(add, s, window, first, last))
        pl.when(jnp.logical_not(fits))(functools.partial(add, s, window + GRAIN, first, last))
        first = last
    for at in range(0, width, strip):
        out_copy(at).wait()


def document_squares(me, blocks, places, doc_lengths, tokens, width, columns):
    return pl.pallas_call(
        functools.partial(document_kernel, MAXLEN, places),
        out_shape=jax.ShapeDtypeStruct((width, columns), jnp.float32),
        in_specs=[SMEM, SMEM] + [VMEM] * len(blocks),
        out_specs=pl.BlockSpec(memory_space=pltpu.HBM),
        scratch_shapes=[
            pltpu.VMEM((tokens, width), jnp.bfloat16),
            pltpu.VMEM((tokens, columns), jnp.bfloat16),
            pltpu.VMEM((width, tokens), jnp.bfloat16),
            pltpu.VMEM((width, columns), jnp.float32),
            pltpu.SemaphoreType.DMA((max(1, width // 256),)),
        ],
        compiler_params=pltpu.CompilerParams(vmem_limit_bytes=DOCUMENT_VMEM),
        cost_estimate=FREE,
    )(doc_lengths.astype(jnp.int32), me, *blocks)


def solution(mesh):
    n_dp, n_tensor = mesh.shape["dp"], mesh.shape["tensor"]
    order = ring_order(n_dp)
    forward = [(order[i], order[(i + 1) % n_dp]) for i in range(n_dp)]
    backward = [(d, s) for s, d in forward]
    swaps = {d: [(t, t ^ d) for t in range(n_tensor)] for d in range(1, n_tensor)}
    last = n_dp // 2

    def local(activations, in_basis, out_grads, out_basis, doc_lengths):
        shard = activations.shape[0]
        half = shard // 2
        tokens = shard * n_dp
        width, columns = in_basis.shape[1], out_basis.shape[1]
        basis = pltpu.with_memory_space_constraint(in_basis, pltpu.VMEM)
        out_basis = pltpu.with_memory_space_constraint(out_basis, pltpu.HBM)

        mine = lax.axis_index("dp")
        spot = jnp.where(mine % 2 == 0, mine // 2, n_dp - 1 - mine // 2)
        me = jnp.stack([lax.axis_index("tensor"), spot]).astype(jnp.int32)
        activations, me = lax.optimization_barrier((activations, me))

        def start_of(hop, way):
            def start(spot):
                place = lax.rem(spot + (n_dp - hop if way == 0 else hop), jnp.int32(n_dp))
                source = jnp.where(2 * place < n_dp, 2 * place, 2 * (n_dp - 1 - place) + 1)
                return source * shard + (half if hop == last and way == 1 else 0)

            return start

        def share_of(pieces, d, rows):
            def begin(index, spot):
                at, low = (index ^ d) * rows, 0
                token = jnp.int32(0)
                for start, size in pieces:
                    inside = jnp.logical_and(at >= low, at < low + size)
                    token = jnp.where(inside, start(spot) + at - low, token)
                    low += size
                return token

            return begin

        def pass_on(hop, pieces):
            if hop == last:
                pieces = [pieces[0][:half], pieces[1][half:]]
            return [lax.ppermute(v, "dp", p) for v, p in zip(pieces, (forward, backward))]

        def swap(block, d):
            return lax.ppermute(block, "tensor", swaps[d])

        def send_shares(parts):
            return [parts[0]] + [swap(parts[d], d) for d in range(1, n_tensor)]

        def send_total(parts):
            total = functools.reduce(jnp.add, parts).astype(jnp.bfloat16)
            return [total] + [swap(total, d) for d in range(1, n_tensor)]

        groups = {hop: [hop] for hop in range(last + 1)}
        if shard // n_tensor < TILE:
            groups[last] = groups.pop(0) + groups[last]

        act, grads, sums = {0: [activations]}, {}, {}
        flight = {("act", 1): pass_on(1, [activations] * 2)}
        features = [out_grads] + [swap(out_grads, d) for d in range(1, n_tensor)]
        flight["grads", 0] = [own_grads(me, features, out_basis)]

        def rotate(group):
            return rotate_shares(me, [v for h in group for v in act[h]], basis, n_tensor)

        if 0 in groups:
            flight["shares", 0] = send_shares(rotate(groups[0]))
        def settle(flight):
            keys = list(flight)
            return dict(zip(keys, lax.optimization_barrier([flight[key] for key in keys])))

        for hop in range(1, last + 2):
            behind = {}
            if 1 < hop <= last:
                early = {key: flight.pop(key) for key in list(flight) if key[0] != "sums"}
                later = {key: early.pop(key) for key in [("act", hop)]}
                early = settle(early)
                grads[hop - 1] = early.pop(("grads", hop - 1))
                for (_, i), value in early.items():
                    total = send_total(value)
                    (behind if hop == last else flight)["sums", i] = total
                flight.update(later)
            came, flight = settle(flight), behind
            for (kind, i), value in came.items():
                if kind == "shares":
                    flight["sums", i] = send_total(value)
                else:
                    {"act": act, "grads": grads, "sums": sums}[kind][i] = value
            if hop < last:
                flight["act", hop + 1] = pass_on(hop + 1, act[hop])
            if hop <= last:
                shares = rotate(groups[hop])
                gradients = grads[hop - 1]
                if hop == last:
                    shares, gradients = lax.optimization_barrier((list(shares), gradients))
                flight["grads", hop] = pass_on(hop, gradients * (2 if hop == 1 else 1))
                flight["shares", hop] = send_shares(shares)
        for (_, i), value in flight.items():
            sums[i] = value

        blocks, places = [], []
        for i, group in groups.items():
            pieces = [(start_of(h, way), v.shape[0]) for h in group for way, v in enumerate(act[h])]
            rows = sum(size for _, size in pieces) // n_tensor
            for d, block in enumerate(sums[i]):
                blocks.append(block)
                places.append((False, 0, rows, share_of(pieces, d, rows)))
        for h, pieces in grads.items():
            for way, piece in enumerate(pieces):
                start = start_of(h, way)
                blocks.append(piece)
                places.append((True, 0, piece.shape[0], lambda me, spot, start=start: start(spot)))
        return document_squares(me, blocks, places, doc_lengths, tokens, width, columns)

    placed = (P("dp", "tensor"), P("tensor", "dp"), P("dp", "tensor"), P(None, "tensor"), P())
    return jax.shard_map(
        local, mesh=mesh, in_specs=placed, out_specs=P("dp", "tensor"), check_vma=False
    )
```

time: 378 us -> 135 us (0.36)
  waiting for transfers between devices: 182 us -> 59.7 us
  blocking collectives: 76.5 us -> 0 us
  local copies, waits for them, and re-layouts: 54.3 us -> 4.36 us
  starting transfers between devices: 0.08 us -> 43 us
  matrix products: 33.3 us -> 0 us
  Pallas kernels: 0 us -> 26.8 us
  other arithmetic: 17.9 us -> 0.36 us
  between operations: 13.1 us -> 0.41 us
    all_gather x3 -> x0, waiting for transfers between devices: 180 us -> none  [the longest x1 111 us: local(): all_rows = lax.all_gather(activations, 'dp', axis=0, tiled=True)]
    psum x1 -> x0, blocking collectives: 76.5 us -> none  [local(): rotated = lax.psum(partial_value, 'tensor').astype(jnp.bfloat16)]
    ppermute x0 -> x49, waiting for transfers between devices: none -> 59.7 us  [the longest x33 53 us: swap(): return lax.ppermute(block, 'tensor', swaps[d])]
    ppermute x0 -> x49, starting transfers between devices: none -> 43 us  [the longest x33 25.5 us: swap(): return lax.ppermute(block, 'tensor', swaps[d])]
    gather x48 -> x0, local copies, waits for them, and re-layouts: 42.2 us -> none
    dot_general x4 -> x0, matrix products: 33.3 us -> none  [the longest x2 14.2 us: advance(): jnp.einsum('gtj,gtk->gjk', left_rows, right_rows, preferred_element_type=...]
    pallas_call x0 -> x7, Pallas kernels: none -> 26.8 us  [the longest x5 11.4 us: call(): pl.pallas_call(kernel, out_shape=[jax.ShapeDtypeStruct(*shape) for shape...]
    add x2 -> x0, other arithmetic: 12.5 us -> none  [advance(): return (running + jnp.sum(blocks * blocks, axis=0), None)]
  transfers between devices with their start and end apart: 3 -> 49, of which waited for: 3 -> 24; matrix products, arithmetic and copies ran while one was open for 1% -> 0% of each run, Pallas kernels for 0% -> 13%
where the time goes in v4:
time: 135 us
  waiting for transfers between devices  59.7 us (44%)
  starting transfers between devices  43 us (32%)
  Pallas kernels  26.8 us (20%)
  local copies, waits for them, and re-layouts  4.36 us (3%)
    ppermute x33, waiting for transfers between devices, swap(): return lax.ppermute(block, 'tensor', swaps[d])  53 us
    ppermute x33, starting transfers between devices, swap(): return lax.ppermute(block, 'tensor', swaps[d])  25.5 us
    ppermute x16, starting transfers between devices, pass_on(): lax.ppermute(v, 'dp', p)  17.5 us
    pallas_call x5, Pallas kernels, call(): pl.pallas_call(kernel, out_shape=[jax.ShapeDtypeStruct(*shape) for shape...  11.4 us
    pallas_call x1, Pallas kernels, document_squares(): pl.pallas_call(functools.partial(document_kernel, MAXLEN, places), out_sh...  9.88 us
    ppermute x16, waiting for transfers between devices, pass_on(): lax.ppermute(v, 'dp', p)  6.69 us
    pallas_call x1, Pallas kernels, own_grads(): pl.pallas_call(own_grads_kernel, out_shape=jax.ShapeDtypeStruct((rows, wi...  5.55 us
    unnamed x12, local copies, waits for them, and re-layouts  4.28 us
  transfers between devices with their start and end apart: 49, of which 24 were waited for; matrix products, arithmetic and copies ran while one was open for 0% of the time, Pallas kernels for 13%

profile of v4, /device:TPU:0, one launch (start us, length us, event | category | flops | bytes accessed | tf_op | source)
XLA Modules:
  0.0 134.7 jit_solution(13463431494773064741)
XLA Ops:
  0.1 2.9 %collective-permute-start.1 = (bf16[128,3584]{1,0:T(8,128)(2,1)}, bf16[128,3584]{1,0:T(8,128)(2,1)S(1)}, u32[]{:S(2)}, u32[]{:S(2)}) collective-permute-start(bf16[128,3584]{1,0:T(8,128)(2,1)} %refs_0_.2), channel_id=1, source_target_pairs={{8,0},{16,8},{24,16},{28,24},{20,28},{12,20},{4,12},{0,4},{9,1},{1... | collective-permute-start | bytes 2752520 | tf_op jit(solution)/shard_map/ppermute | solution.py:222
  3.2 1.9 %collective-permute-start.3 = (bf16[128,1024]{1,0:T(8,128)(2,1)}, bf16[128,1024]{1,0:T(8,128)(2,1)S(1)}, u32[]{:S(2)}, u32[]{:S(2)}) collective-permute-start(bf16[128,1024]{1,0:T(8,128)(2,1)} %refs_0_.1), channel_id=1, source_target_pairs={{0,2},{1,3},{2,0},{3,1},{4,6},{5,7},{6,4},{7,5},{8,10},{9,11},{10,... | collective-permute-start | bytes 786440 | tf_op jit(solution)/shard_map/ppermute | solution.py:225
  5.3 3.1 %copy-done = bf16[3584,1024]{1,0:T(8,128)(2,1)S(1)} copy-done((bf16[3584,1024]{1,0:T(8,128)(2,1)S(1)}, bf16[3584,1024]{1,0:T(8,128)(2,1)}, u32[]{:S(2)}) %copy-start) | copy-done | bytes 7340056
  8.4 1.2 copy-done.1
  9.6 1.7 %shard_map.56 = (f32[32,1024]{1,0:T(8,128)S(1)}, f32[32,1024]{1,0:T(8,128)S(1)}, f32[32,1024]{1,0:T(8,128)S(1)}, f32[32,1024]{1,0:T(8,128)S(1)}) custom-call(s32[2]{0:T(128)S(1)} %pad_add_fusion.me_ref, bf16[128,3584]{1,0:T(8,128)(2,1)S(1)} %copy-done.1, bf16[3584,1024]{1,0:T(8,128)(2,1)S(1)} %copy-done), custom_call_target="tpu_custom_call" | custom-call | tf_op jit(solution)/shard_map/pallas_call | solution.py:25
  11.3 1.3 collective-permute-done.3.refs_2_
  12.6 1.9 %collective-permute-start.6 = (f32[32,1024]{1,0:T(8,128)S(1)}, f32[32,1024]{1,0:T(8,128)S(1)}, u32[]{:S(2)}, u32[]{:S(2)}) collective-permute-start(f32[32,1024]{1,0:T(8,128)S(1)} %get-tuple-element.90), channel_id=1, source_target_pairs={{0,2},{1,3},{2,0},{3,1},{4,6},{5,7},{6,4},{7,5},{8,10},{9,11},{10,... | collective-permute-start | bytes 393224 | tf_op jit(solution)/shard_map/ppermute | solution.py:225
  14.5 2.2 %collective-permute-done.4.refs_3_ = bf16[128,1024]{1,0:T(8,128)(2,1)S(1)} collective-permute-done((bf16[128,1024]{1,0:T(8,128)(2,1)}, bf16[128,1024]{1,0:T(8,128)(2,1)S(1)}, u32[]{:S(2)}, u32[]{:S(2)}) %collective-permute-start.4) | collective-permute-done | bytes 262176 | tf_op jit(solution)/shard_map/ppermute | solution.py:225
  16.7 2.1 %collective-permute-start.7 = (f32[32,1024]{1,0:T(8,128)S(1)}, f32[32,1024]{1,0:T(8,128)S(1)}, u32[]{:S(2)}, u32[]{:S(2)}) collective-permute-start(f32[32,1024]{1,0:T(8,128)S(1)} %get-tuple-element.91), channel_id=1, source_target_pairs={{0,3},{1,2},{2,1},{3,0},{4,7},{5,6},{6,5},{7,4},{8,11},{9,10},{10,... | collective-permute-start | bytes 393224 | tf_op jit(solution)/shard_map/ppermute | solution.py:225
  18.8 5.6 %shard_map.55.refs_20_ = bf16[128,1024]{1,0:T(8,128)(2,1)S(1)} custom-call(s32[2]{0:T(128)S(1)} %pad_add_fusion.me_ref, bf16[128,1024]{1,0:T(8,128)(2,1)S(1)} %copy-done.2, bf16[128,1024]{1,0:T(8,128)(2,1)S(1)} %collective-permute-done.2.refs_1_, bf16[128,1024]{1,0:T(8,128)(2,1)S(1)} %collective-permute-done.3.refs_2_, ...), custom_call_target="tpu_custom_call" | custom-call | tf_op jit(solution)/shard_map/pallas_call | solution.py:89
  25.0 1.6 %collective-permute-start.12 = (bf16[128,1024]{1,0:T(8,128)(2,1)S(1)}, bf16[128,1024]{1,0:T(8,128)(2,1)S(1)}, u32[]{:S(2)}, u32[]{:S(2)}) collective-permute-start(bf16[128,1024]{1,0:T(8,128)(2,1)S(1)} %shard_map.55.refs_20_), channel_id=1, source_target_pairs={{8,0},{16,8},{24,16},{28,24},{20,28},{12,20},{4,12},{0,4},{9,1},{1... | collective-permute-start | bytes 786440 | tf_op jit(solution)/shard_map/ppermute | solution.py:222
  29.1 2.7 %shard_map.57 = (f32[64,1024]{1,0:T(8,128)S(1)}, f32[64,1024]{1,0:T(8,128)S(1)}, f32[64,1024]{1,0:T(8,128)S(1)}, f32[64,1024]{1,0:T(8,128)S(1)}) custom-call(s32[2]{0:T(128)S(1)} %pad_add_fusion.me_ref, bf16[128,3584]{1,0:T(8,128)(2,1)S(1)} %collective-permute-done.refs_0_, bf16[128,3584]{1,0:T(8,128)(2,1)S(1)} %collective-permute-done.1.refs_1_, ...), custom_call_target="tpu_custom_call" | custom-call | tf_op jit(solution)/shard_map/pallas_call | solution.py:25
  31.8 2.4 %collective-permute-done.12.refs_22_ = bf16[128,1024]{1,0:T(8,128)(2,1)S(1)} collective-permute-done((bf16[128,1024]{1,0:T(8,128)(2,1)S(1)}, bf16[128,1024]{1,0:T(8,128)(2,1)S(1)}, u32[]{:S(2)}, u32[]{:S(2)}) %collective-permute-start.12) | collective-permute-done | bytes 262176 | tf_op jit(solution)/shard_map/ppermute | solution.py:222
  34.3 1.5 %collective-permute-start.14 = (f32[64,1024]{1,0:T(8,128)S(1)}, f32[64,1024]{1,0:T(8,128)S(1)}, u32[]{:S(2)}, u32[]{:S(2)}) collective-permute-start(f32[64,1024]{1,0:T(8,128)S(1)} %get-tuple-element.101), channel_id=1, source_target_pairs={{0,2},{1,3},{2,0},{3,1},{4,6},{5,7},{6,4},{7,5},{8,10},{9,11},{10,... | collective-permute-start | bytes 786440 | tf_op jit(solution)/shard_map/ppermute | solution.py:225
  35.9 1.8 %collective-permute-start.10 = (bf16[32,1024]{1,0:T(8,128)(2,1)S(1)}, bf16[32,1024]{1,0:T(8,128)(2,1)S(1)}, u32[]{:S(2)}, u32[]{:S(2)}) collective-permute-start(bf16[32,1024]{1,0:T(8,128)(2,1)S(1)} %add_convert_fusion.4.refs_0_), channel_id=1, source_target_pairs={{0,3},{1,2},{2,1},{3,0},{4,7},{5,6},{6,5},{7,4},{8,11},{9,10},{10,... | collective-permute-start | bytes 196616 | tf_op jit(solution)/shard_map/ppermute | solution.py:225
  37.7 4.7 %collective-permute-done.14 = f32[64,1024]{1,0:T(8,128)S(1)} collective-permute-done((f32[64,1024]{1,0:T(8,128)S(1)}, f32[64,1024]{1,0:T(8,128)S(1)}, u32[]{:S(2)}, u32[]{:S(2)}) %collective-permute-start.14) | collective-permute-done | bytes 262176 | tf_op jit(solution)/shard_map/ppermute | solution.py:225
  42.5 1.5 %collective-permute-start.9 = (bf16[32,1024]{1,0:T(8,128)(2,1)S(1)}, bf16[32,1024]{1,0:T(8,128)(2,1)S(1)}, u32[]{:S(2)}, u32[]{:S(2)}) collective-permute-start(bf16[32,1024]{1,0:T(8,128)(2,1)S(1)} %add_convert_fusion.4.refs_0_), channel_id=1, source_target_pairs={{0,2},{1,3},{2,0},{3,1},{4,6},{5,7},{6,4},{7,5},{8,10},{9,11},{10,... | collective-permute-start | bytes 196616 | tf_op jit(solution)/shard_map/ppermute | solution.py:225
  44.0 2.7 %collective-permute-done.15 = f32[64,1024]{1,0:T(8,128)S(1)} collective-permute-done((f32[64,1024]{1,0:T(8,128)S(1)}, f32[64,1024]{1,0:T(8,128)S(1)}, u32[]{:S(2)}, u32[]{:S(2)}) %collective-permute-start.15) | collective-permute-done | bytes 262176 | tf_op jit(solution)/shard_map/ppermute | solution.py:225
  46.8 2.3 %collective-permute-start.18 = (bf16[64,1024]{1,0:T(8,128)(2,1)S(1)}, bf16[64,1024]{1,0:T(8,128)(2,1)S(1)}, u32[]{:S(2)}, u32[]{:S(2)}) collective-permute-start(bf16[64,1024]{1,0:T(8,128)(2,1)S(1)} %add_convert_fusion.2.refs_4_), channel_id=1, source_target_pairs={{0,3},{1,2},{2,1},{3,0},{4,7},{5,6},{6,5},{7,4},{8,11},{9,10},{10,... | collective-permute-start | bytes 393224 | tf_op jit(solution)/shard_map/ppermute | solution.py:225
  51.0 2.0 %collective-permute-done.18.refs_7_ = bf16[64,1024]{1,0:T(8,128)(2,1)S(1)} collective-permute-done((bf16[64,1024]{1,0:T(8,128)(2,1)S(1)}, bf16[64,1024]{1,0:T(8,128)(2,1)S(1)}, u32[]{:S(2)}, u32[]{:S(2)}) %collective-permute-start.18) | collective-permute-done | bytes 131104 | tf_op jit(solution)/shard_map/ppermute | solution.py:225
  53.5 2.4 %collective-permute-done.17.refs_6_ = bf16[64,1024]{1,0:T(8,128)(2,1)S(1)} collective-permute-done((bf16[64,1024]{1,0:T(8,128)(2,1)S(1)}, bf16[64,1024]{1,0:T(8,128)(2,1)S(1)}, u32[]{:S(2)}, u32[]{:S(2)}) %collective-permute-start.17) | collective-permute-done | bytes 131104 | tf_op jit(solution)/shard_map/ppermute | solution.py:225
  55.9 1.6 %collective-permute-start.22 = (bf16[128,1024]{1,0:T(8,128)(2,1)S(1)}, bf16[128,1024]{1,0:T(8,128)(2,1)S(1)}, u32[]{:S(2)}, u32[]{:S(2)}) collective-permute-start(bf16[128,1024]{1,0:T(8,128)(2,1)S(1)} %collective-permute-done.12.refs_22_), channel_id=1, source_target_pairs={{8,0},{16,8},{24,16},{28,24},{20,28},{12,20},{4,12},{0,4},{9,1},{1... | collective-permute-start | bytes 786440 | tf_op jit(solution)/shard_map/ppermute | solution.py:222
  58.0 1.6 %collective-permute-start.30 = (bf16[128,3584]{1,0:T(8,128)(2,1)S(1)}, bf16[128,3584]{1,0:T(8,128)(2,1)S(1)}, u32[]{:S(2)}, u32[]{:S(2)}) collective-permute-start(bf16[128,3584]{1,0:T(8,128)(2,1)S(1)} %collective-permute-done.20.refs_1_), channel_id=1, source_target_pairs={{8,0},{16,8},{24,16},{28,24},{20,28},{12,20},{4,12},{0,4},{9,1},{1... | collective-permute-start | bytes 2752520 | tf_op jit(solution)/shard_map/ppermute | solution.py:222
  59.6 2.7 %shard_map.58 = (f32[64,1024]{1,0:T(8,128)S(1)}, f32[64,1024]{1,0:T(8,128)S(1)}, f32[64,1024]{1,0:T(8,128)S(1)}, f32[64,1024]{1,0:T(8,128)S(1)}) custom-call(s32[2]{0:T(128)S(1)} %pad_add_fusion.me_ref, bf16[128,3584]{1,0:T(8,128)(2,1)S(1)} %collective-permute-done.19.refs_0_, bf16[128,3584]{1,0:T(8,128)(2,1)S(1)} %collective-permute-done.20.refs_1_, ...), custom_call_target="tpu_custom_call" | custom-call | tf_op jit(solution)/shard_map/pallas_call | solution.py:25
  63.3 1.9 %collective-permute-done.22.refs_24_ = bf16[128,1024]{1,0:T(8,128)(2,1)S(1)} collective-permute-done((bf16[128,1024]{1,0:T(8,128)(2,1)S(1)}, bf16[128,1024]{1,0:T(8,128)(2,1)S(1)}, u32[]{:S(2)}, u32[]{:S(2)}) %collective-permute-start.22) | collective-permute-done | bytes 262176 | tf_op jit(solution)/shard_map/ppermute | solution.py:222
  65.2 6.4 %collective-permute-done.24 = f32[64,1024]{1,0:T(8,128)S(1)} collective-permute-done((f32[64,1024]{1,0:T(8,128)S(1)}, f32[64,1024]{1,0:T(8,128)S(1)}, u32[]{:S(2)}, u32[]{:S(2)}) %collective-permute-start.24) | collective-permute-done | bytes 262176 | tf_op jit(solution)/shard_map/ppermute | solution.py:225
  71.5 4.7 %collective-permute-done.25 = f32[64,1024]{1,0:T(8,128)S(1)} collective-permute-done((f32[64,1024]{1,0:T(8,128)S(1)}, f32[64,1024]{1,0:T(8,128)S(1)}, u32[]{:S(2)}, u32[]{:S(2)}) %collective-permute-start.25) | collective-permute-done | bytes 262176 | tf_op jit(solution)/shard_map/ppermute | solution.py:225
  76.3 1.1 collective-permute-start.28
  77.4 1.1 collective-permute-start.27
  78.6 2.9 %collective-permute-done.28.refs_11_ = bf16[64,1024]{1,0:T(8,128)(2,1)S(1)} collective-permute-done((bf16[64,1024]{1,0:T(8,128)(2,1)S(1)}, bf16[64,1024]{1,0:T(8,128)(2,1)S(1)}, u32[]{:S(2)}, u32[]{:S(2)}) %collective-permute-start.28) | collective-permute-done | bytes 131104 | tf_op jit(solution)/shard_map/ppermute | solution.py:225
  81.9 3.1 %collective-permute-done.27.refs_10_ = bf16[64,1024]{1,0:T(8,128)(2,1)S(1)} collective-permute-done((bf16[64,1024]{1,0:T(8,128)(2,1)S(1)}, bf16[64,1024]{1,0:T(8,128)(2,1)S(1)}, u32[]{:S(2)}, u32[]{:S(2)}) %collective-permute-start.27) | collective-permute-done | bytes 131104 | tf_op jit(solution)/shard_map/ppermute | solution.py:225
  84.9 1.6 %collective-permute-start.32 = (bf16[128,1024]{1,0:T(8,128)(2,1)S(1)}, bf16[128,1024]{1,0:T(8,128)(2,1)S(1)}, u32[]{:S(2)}, u32[]{:S(2)}) collective-permute-start(bf16[128,1024]{1,0:T(8,128)(2,1)S(1)} %collective-permute-done.22.refs_24_), channel_id=1, source_target_pairs={{8,0},{16,8},{24,16},{28,24},{20,28},{12,20},{4,12},{0,4},{9,1},{1... | collective-permute-start | bytes 786440 | tf_op jit(solution)/shard_map/ppermute | solution.py:222
  86.5 2.7 %shard_map.59 = (f32[64,1024]{1,0:T(8,128)S(1)}, f32[64,1024]{1,0:T(8,128)S(1)}, f32[64,1024]{1,0:T(8,128)S(1)}, f32[64,1024]{1,0:T(8,128)S(1)}) custom-call(s32[2]{0:T(128)S(1)} %pad_add_fusion.me_ref, bf16[128,3584]{1,0:T(8,128)(2,1)S(1)} %collective-permute-done.29.refs_0_, bf16[128,3584]{1,0:T(8,128)(2,1)S(1)} %collective-permute-done.30.refs_1_, ...), custom_call_target="tpu_custom_call" | custom-call | tf_op jit(solution)/shard_map/pallas_call | solution.py:25
  91.2 1.6 %collective-permute-start.40 = (bf16[64,3584]{1,0:T(8,128)(2,1)S(1)}, bf16[64,3584]{1,0:T(8,128)(2,1)S(1)}, u32[]{:S(2)}, u32[]{:S(2)}) collective-permute-start(bf16[64,3584]{1,0:T(8,128)(2,1)S(1)} %slice.13), channel_id=1, source_target_pairs={{8,0},{16,8},{24,16},{28,24},{20,28},{12,20},{4,12},{0,4},{9,1},{1... | collective-permute-start | bytes 1376264 | tf_op jit(solution)/shard_map/ppermute | solution.py:222
  93.3 5.1 %collective-permute-done.34 = f32[64,1024]{1,0:T(8,128)S(1)} collective-permute-done((f32[64,1024]{1,0:T(8,128)S(1)}, f32[64,1024]{1,0:T(8,128)S(1)}, u32[]{:S(2)}, u32[]{:S(2)}) %collective-permute-start.34) | collective-permute-done | bytes 262176 | tf_op jit(solution)/shard_map/ppermute | solution.py:225
  98.5 4.7 %collective-permute-done.35 = f32[64,1024]{1,0:T(8,128)S(1)} collective-permute-done((f32[64,1024]{1,0:T(8,128)S(1)}, f32[64,1024]{1,0:T(8,128)S(1)}, u32[]{:S(2)}, u32[]{:S(2)}) %collective-permute-start.35) | collective-permute-done | bytes 262176 | tf_op jit(solution)/shard_map/ppermute | solution.py:225
  103.3 1.1 collective-permute-start.38
  104.4 1.1 collective-permute-start.37
  105.5 1.7 %shard_map.60 = (f32[32,1024]{1,0:T(8,128)S(1)}, f32[32,1024]{1,0:T(8,128)S(1)}, f32[32,1024]{1,0:T(8,128)S(1)}, f32[32,1024]{1,0:T(8,128)S(1)}) custom-call(s32[2]{0:T(128)S(1)} %pad_add_fusion.me_ref, bf16[64,3584]{1,0:T(8,128)(2,1)S(1)} %collective-permute-done.39.refs_0_, bf16[64,3584]{1,0:T(8,128)(2,1)S(1)} %collective-permute-done.40.refs_1_, ...), custom_call_target="tpu_custom_call" | custom-call | tf_op jit(solution)/shard_map/pallas_call | solution.py:25
  107.3 1.6 %collective-permute-start.42 = (bf16[64,1024]{1,0:T(8,128)(2,1)S(1)}, bf16[64,1024]{1,0:T(8,128)(2,1)S(1)}, u32[]{:S(2)}, u32[]{:S(2)}) collective-permute-start(bf16[64,1024]{1,0:T(8,128)(2,1)S(1)} %slice.15), channel_id=1, source_target_pairs={{8,0},{16,8},{24,16},{28,24},{20,28},{12,20},{4,12},{0,4},{9,1},{1... | collective-permute-start | bytes 393224 | tf_op jit(solution)/shard_map/ppermute | solution.py:222
  109.7 2.3 %collective-permute-done.37.refs_14_ = bf16[64,1024]{1,0:T(8,128)(2,1)S(1)} collective-permute-done((bf16[64,1024]{1,0:T(8,128)(2,1)S(1)}, bf16[64,1024]{1,0:T(8,128)(2,1)S(1)}, u32[]{:S(2)}, u32[]{:S(2)}) %collective-permute-start.37) | collective-permute-done | bytes 131104 | tf_op jit(solution)/shard_map/ppermute | solution.py:225
  113.3 1.2 collective-permute-done.41.refs_27_
  114.5 3.5 %collective-permute-done.44 = f32[32,1024]{1,0:T(8,128)S(1)} collective-permute-done((f32[32,1024]{1,0:T(8,128)S(1)}, f32[32,1024]{1,0:T(8,128)S(1)}, u32[]{:S(2)}, u32[]{:S(2)}) %collective-permute-start.44) | collective-permute-done | bytes 131104 | tf_op jit(solution)/shard_map/ppermute | solution.py:225
  118.7 1.5 %collective-permute-start.48 = (bf16[32,1024]{1,0:T(8,128)(2,1)S(1)}, bf16[32,1024]{1,0:T(8,128)(2,1)S(1)}, u32[]{:S(2)}, u32[]{:S(2)}) collective-permute-start(bf16[32,1024]{1,0:T(8,128)(2,1)S(1)} %add_convert_fusion.3.refs_16_), channel_id=1, source_target_pairs={{0,3},{1,2},{2,1},{3,0},{4,7},{5,6},{6,5},{7,4},{8,11},{9,10},{10,... | collective-permute-start | bytes 196616 | tf_op jit(solution)/shard_map/ppermute | solution.py:225
  120.1 1.1 collective-permute-start.47
  121.3 1.2 collective-permute-done.48.refs_19_
  122.4 2.2 %collective-permute-done.47.refs_18_ = bf16[32,1024]{1,0:T(8,128)(2,1)S(1)} collective-permute-done((bf16[32,1024]{1,0:T(8,128)(2,1)S(1)}, bf16[32,1024]{1,0:T(8,128)(2,1)S(1)}, u32[]{:S(2)}, u32[]{:S(2)}) %collective-permute-start.47) | collective-permute-done | bytes 65568 | tf_op jit(solution)/shard_map/ppermute | solution.py:225
  124.6 9.9 %shard_map.61 = f32[1024,1024]{1,0:T(8,128)} custom-call(s32[8]{0:T(128)S(1)} %copy-done.3, s32[2]{0:T(128)S(1)} %pad_add_fusion.me_ref, bf16[32,1024]{1,0:T(8,128)(2,1)S(1)} %add_convert_fusion.4.refs_0_, bf16[32,1024]{1,0:T(8,128)(2,1)S(1)} %collective-permute-done.8.refs_1_, bf16[32,1024]{1,0:T(8,128)(2,1)S(1)} %collective-permute-done.9.refs_2_, ...), custom_call_target="tpu_custom_call" | custom-call | tf_op jit(solution)/shard_map/pallas_call | solution.py:161
  (80 shorter events, 13.8 us)
Async XLA Ops:
  0.1 24.3 %collective-permute-start.1 = (bf16[128,3584]{1,0:T(8,128)(2,1)}, bf16[128,3584]{1,0:T(8,128)(2,1)S(1)}, u32[]{:S(2)}, u32[]{:S(2)}) collective-permute-start(bf16[128,3584]{1,0:T(8,128)(2,1)} %refs_0_.2), channel_id=1, source_target_pairs={{8,0},{16,8},{24,16},{28,24},{20,28},{12,20},{4,12},{0,4},{9,1},{1... | collective-permute-start | bytes 2752520 | tf_op jit(solution)/shard_map/ppermute | solution.py:222
  3.0 22.0 %collective-permute-start = (bf16[128,3584]{1,0:T(8,128)(2,1)}, bf16[128,3584]{1,0:T(8,128)(2,1)S(1)}, u32[]{:S(2)}, u32[]{:S(2)}) collective-permute-start(bf16[128,3584]{1,0:T(8,128)(2,1)} %refs_0_.2), channel_id=1, source_target_pairs={{0,8},{8,16},{16,24},{24,28},{28,20},{20,12},{12,4},{4,0},{1,9},{9... | collective-permute-start | bytes 2752520 | tf_op jit(solution)/shard_map/ppermute | solution.py:222
  3.2 9.4 %collective-permute-start.3 = (bf16[128,1024]{1,0:T(8,128)(2,1)}, bf16[128,1024]{1,0:T(8,128)(2,1)S(1)}, u32[]{:S(2)}, u32[]{:S(2)}) collective-permute-start(bf16[128,1024]{1,0:T(8,128)(2,1)} %refs_0_.1), channel_id=1, source_target_pairs={{0,2},{1,3},{2,0},{3,1},{4,6},{5,7},{6,4},{7,5},{8,10},{9,11},{10,... | collective-permute-start | bytes 786440 | tf_op jit(solution)/shard_map/ppermute | solution.py:225
  5.1 7.5 %collective-permute-start.2 = (bf16[128,1024]{1,0:T(8,128)(2,1)}, bf16[128,1024]{1,0:T(8,128)(2,1)S(1)}, u32[]{:S(2)}, u32[]{:S(2)}) collective-permute-start(bf16[128,1024]{1,0:T(8,128)(2,1)} %refs_0_.1), channel_id=1, source_target_pairs={{0,1},{1,0},{2,3},{3,2},{4,5},{5,4},{6,7},{7,6},{8,9},{9,8},{10,11... | collective-permute-start | bytes 786440 | tf_op jit(solution)/shard_map/ppermute | solution.py:225
  5.1 11.6 %collective-permute-start.4 = (bf16[128,1024]{1,0:T(8,128)(2,1)}, bf16[128,1024]{1,0:T(8,128)(2,1)S(1)}, u32[]{:S(2)}, u32[]{:S(2)}) collective-permute-start(bf16[128,1024]{1,0:T(8,128)(2,1)} %refs_0_.1), channel_id=1, source_target_pairs={{0,3},{1,2},{2,1},{3,0},{4,7},{5,6},{6,5},{7,4},{8,11},{9,10},{10,... | collective-permute-start | bytes 786440 | tf_op jit(solution)/shard_map/ppermute | solution.py:225
  12.6 11.8 %collective-permute-start.5 = (f32[32,1024]{1,0:T(8,128)S(1)}, f32[32,1024]{1,0:T(8,128)S(1)}, u32[]{:S(2)}, u32[]{:S(2)}) collective-permute-start(f32[32,1024]{1,0:T(8,128)S(1)} %get-tuple-element.89), channel_id=1, source_target_pairs={{0,1},{1,0},{2,3},{3,2},{4,5},{5,4},{6,7},{7,6},{8,9},{9,8},{10,11... | collective-permute-start | bytes 393224 | tf_op jit(solution)/shard_map/ppermute | solution.py:225
  12.6 11.8 %collective-permute-start.6 = (f32[32,1024]{1,0:T(8,128)S(1)}, f32[32,1024]{1,0:T(8,128)S(1)}, u32[]{:S(2)}, u32[]{:S(2)}) collective-permute-start(f32[32,1024]{1,0:T(8,128)S(1)} %get-tuple-element.90), channel_id=1, source_target_pairs={{0,2},{1,3},{2,0},{3,1},{4,6},{5,7},{6,4},{7,5},{8,10},{9,11},{10,... | collective-permute-start | bytes 393224 | tf_op jit(solution)/shard_map/ppermute | solution.py:225
  16.7 7.7 %collective-permute-start.7 = (f32[32,1024]{1,0:T(8,128)S(1)}, f32[32,1024]{1,0:T(8,128)S(1)}, u32[]{:S(2)}, u32[]{:S(2)}) collective-permute-start(f32[32,1024]{1,0:T(8,128)S(1)} %get-tuple-element.91), channel_id=1, source_target_pairs={{0,3},{1,2},{2,1},{3,0},{4,7},{5,6},{6,5},{7,4},{8,11},{9,10},{10,... | collective-permute-start | bytes 393224 | tf_op jit(solution)/shard_map/ppermute | solution.py:225
  25.0 9.2 %collective-permute-start.12 = (bf16[128,1024]{1,0:T(8,128)(2,1)S(1)}, bf16[128,1024]{1,0:T(8,128)(2,1)S(1)}, u32[]{:S(2)}, u32[]{:S(2)}) collective-permute-start(bf16[128,1024]{1,0:T(8,128)(2,1)S(1)} %shard_map.55.refs_20_), channel_id=1, source_target_pairs={{8,0},{16,8},{24,16},{28,24},{20,28},{12,20},{4,12},{0,4},{9,1},{1... | collective-permute-start | bytes 786440 | tf_op jit(solution)/shard_map/ppermute | solution.py:222
  26.6 9.2 %collective-permute-start.11 = (bf16[128,1024]{1,0:T(8,128)(2,1)S(1)}, bf16[128,1024]{1,0:T(8,128)(2,1)S(1)}, u32[]{:S(2)}, u32[]{:S(2)}) collective-permute-start(bf16[128,1024]{1,0:T(8,128)(2,1)S(1)} %shard_map.55.refs_20_), channel_id=1, source_target_pairs={{0,8},{8,16},{16,24},{24,28},{28,20},{20,12},{12,4},{4,0},{1,9},{9... | collective-permute-start | bytes 786440 | tf_op jit(solution)/shard_map/ppermute | solution.py:222
  27.1 30.4 %collective-permute-start.19 = (bf16[128,3584]{1,0:T(8,128)(2,1)S(1)}, bf16[128,3584]{1,0:T(8,128)(2,1)S(1)}, u32[]{:S(2)}, u32[]{:S(2)}) collective-permute-start(bf16[128,3584]{1,0:T(8,128)(2,1)S(1)} %collective-permute-done.refs_0_), channel_id=1, source_target_pairs={{0,8},{8,16},{16,24},{24,28},{28,20},{20,12},{12,4},{4,0},{1,9},{9... | collective-permute-start | bytes 2752520 | tf_op jit(solution)/shard_map/ppermute | solution.py:222
  28.1 29.4 %collective-permute-start.20 = (bf16[128,3584]{1,0:T(8,128)(2,1)S(1)}, bf16[128,3584]{1,0:T(8,128)(2,1)S(1)}, u32[]{:S(2)}, u32[]{:S(2)}) collective-permute-start(bf16[128,3584]{1,0:T(8,128)(2,1)S(1)} %collective-permute-done.1.refs_1_), channel_id=1, source_target_pairs={{8,0},{16,8},{24,16},{28,24},{20,28},{12,20},{4,12},{0,4},{9,1},{1... | collective-permute-start | bytes 2752520 | tf_op jit(solution)/shard_map/ppermute | solution.py:222
  31.8 4.1 %collective-permute-start.13 = (f32[64,1024]{1,0:T(8,128)S(1)}, f32[64,1024]{1,0:T(8,128)S(1)}, u32[]{:S(2)}, u32[]{:S(2)}) collective-permute-start(f32[64,1024]{1,0:T(8,128)S(1)} %get-tuple-element.100), channel_id=1, source_target_pairs={{0,1},{1,0},{2,3},{3,2},{4,5},{5,4},{6,7},{7,6},{8,9},{9,8},{10,11... | collective-permute-start | bytes 786440 | tf_op jit(solution)/shard_map/ppermute | solution.py:225
  34.3 8.2 %collective-permute-start.14 = (f32[64,1024]{1,0:T(8,128)S(1)}, f32[64,1024]{1,0:T(8,128)S(1)}, u32[]{:S(2)}, u32[]{:S(2)}) collective-permute-start(f32[64,1024]{1,0:T(8,128)S(1)} %get-tuple-element.101), channel_id=1, source_target_pairs={{0,2},{1,3},{2,0},{3,1},{4,6},{5,7},{6,4},{7,5},{8,10},{9,11},{10,... | collective-permute-start | bytes 786440 | tf_op jit(solution)/shard_map/ppermute | solution.py:225
  35.9 10.9 %collective-permute-start.15 = (f32[64,1024]{1,0:T(8,128)S(1)}, f32[64,1024]{1,0:T(8,128)S(1)}, u32[]{:S(2)}, u32[]{:S(2)}) collective-permute-start(f32[64,1024]{1,0:T(8,128)S(1)} %get-tuple-element.102), channel_id=1, source_target_pairs={{0,3},{1,2},{2,1},{3,0},{4,7},{5,6},{6,5},{7,4},{8,11},{9,10},{10,... | collective-permute-start | bytes 786440 | tf_op jit(solution)/shard_map/ppermute | solution.py:225
  35.9 13.2 %collective-permute-start.10 = (bf16[32,1024]{1,0:T(8,128)(2,1)S(1)}, bf16[32,1024]{1,0:T(8,128)(2,1)S(1)}, u32[]{:S(2)}, u32[]{:S(2)}) collective-permute-start(bf16[32,1024]{1,0:T(8,128)(2,1)S(1)} %add_convert_fusion.4.refs_0_), channel_id=1, source_target_pairs={{0,3},{1,2},{2,1},{3,0},{4,7},{5,6},{6,5},{7,4},{8,11},{9,10},{10,... | collective-permute-start | bytes 196616 | tf_op jit(solution)/shard_map/ppermute | solution.py:225
  42.5 7.1 %collective-permute-start.9 = (bf16[32,1024]{1,0:T(8,128)(2,1)S(1)}, bf16[32,1024]{1,0:T(8,128)(2,1)S(1)}, u32[]{:S(2)}, u32[]{:S(2)}) collective-permute-start(bf16[32,1024]{1,0:T(8,128)(2,1)S(1)} %add_convert_fusion.4.refs_0_), channel_id=1, source_target_pairs={{0,2},{1,3},{2,0},{3,1},{4,6},{5,7},{6,4},{7,5},{8,10},{9,11},{10,... | collective-permute-start | bytes 196616 | tf_op jit(solution)/shard_map/ppermute | solution.py:225
  46.8 6.2 %collective-permute-start.18 = (bf16[64,1024]{1,0:T(8,128)(2,1)S(1)}, bf16[64,1024]{1,0:T(8,128)(2,1)S(1)}, u32[]{:S(2)}, u32[]{:S(2)}) collective-permute-start(bf16[64,1024]{1,0:T(8,128)(2,1)S(1)} %add_convert_fusion.2.refs_4_), channel_id=1, source_target_pairs={{0,3},{1,2},{2,1},{3,0},{4,7},{5,6},{6,5},{7,4},{8,11},{9,10},{10,... | collective-permute-start | bytes 393224 | tf_op jit(solution)/shard_map/ppermute | solution.py:225
  49.1 6.9 %collective-permute-start.17 = (bf16[64,1024]{1,0:T(8,128)(2,1)S(1)}, bf16[64,1024]{1,0:T(8,128)(2,1)S(1)}, u32[]{:S(2)}, u32[]{:S(2)}) collective-permute-start(bf16[64,1024]{1,0:T(8,128)(2,1)S(1)} %add_convert_fusion.2.refs_4_), channel_id=1, source_target_pairs={{0,2},{1,3},{2,0},{3,1},{4,6},{5,7},{6,4},{7,5},{8,10},{9,11},{10,... | collective-permute-start | bytes 393224 | tf_op jit(solution)/shard_map/ppermute | solution.py:225
  50.8 6.7 %collective-permute-start.16 = (bf16[64,1024]{1,0:T(8,128)(2,1)S(1)}, bf16[64,1024]{1,0:T(8,128)(2,1)S(1)}, u32[]{:S(2)}, u32[]{:S(2)}) collective-permute-start(bf16[64,1024]{1,0:T(8,128)(2,1)S(1)} %add_convert_fusion.2.refs_4_), channel_id=1, source_target_pairs={{0,1},{1,0},{2,3},{3,2},{4,5},{5,4},{6,7},{7,6},{8,9},{9,8},{10,11... | collective-permute-start | bytes 393224 | tf_op jit(solution)/shard_map/ppermute | solution.py:225
  52.9 9.4 %collective-permute-start.21 = (bf16[128,1024]{1,0:T(8,128)(2,1)S(1)}, bf16[128,1024]{1,0:T(8,128)(2,1)S(1)}, u32[]{:S(2)}, u32[]{:S(2)}) collective-permute-start(bf16[128,1024]{1,0:T(8,128)(2,1)S(1)} %collective-permute-done.11.refs_21_), channel_id=1, source_target_pairs={{0,8},{8,16},{16,24},{24,28},{28,20},{20,12},{12,4},{4,0},{1,9},{9... | collective-permute-start | bytes 786440 | tf_op jit(solution)/shard_map/ppermute | solution.py:222
  55.9 9.2 %collective-permute-start.22 = (bf16[128,1024]{1,0:T(8,128)(2,1)S(1)}, bf16[128,1024]{1,0:T(8,128)(2,1)S(1)}, u32[]{:S(2)}, u32[]{:S(2)}) collective-permute-start(bf16[128,1024]{1,0:T(8,128)(2,1)S(1)} %collective-permute-done.12.refs_22_), channel_id=1, source_target_pairs={{8,0},{16,8},{24,16},{28,24},{20,28},{12,20},{4,12},{0,4},{9,1},{1... | collective-permute-start | bytes 786440 | tf_op jit(solution)/shard_map/ppermute | solution.py:222
  57.5 29.0 %collective-permute-start.29 = (bf16[128,3584]{1,0:T(8,128)(2,1)S(1)}, bf16[128,3584]{1,0:T(8,128)(2,1)S(1)}, u32[]{:S(2)}, u32[]{:S(2)}) collective-permute-start(bf16[128,3584]{1,0:T(8,128)(2,1)S(1)} %collective-permute-done.19.refs_0_), channel_id=1, source_target_pairs={{0,8},{8,16},{16,24},{24,28},{28,20},{20,12},{12,4},{4,0},{1,9},{9... | collective-permute-start | bytes 2752520 | tf_op jit(solution)/shard_map/ppermute | solution.py:222
  58.0 28.5 %collective-permute-start.30 = (bf16[128,3584]{1,0:T(8,128)(2,1)S(1)}, bf16[128,3584]{1,0:T(8,128)(2,1)S(1)}, u32[]{:S(2)}, u32[]{:S(2)}) collective-permute-start(bf16[128,3584]{1,0:T(8,128)(2,1)S(1)} %collective-permute-done.20.refs_1_), channel_id=1, source_target_pairs={{8,0},{16,8},{24,16},{28,24},{20,28},{12,20},{4,12},{0,4},{9,1},{1... | collective-permute-start | bytes 2752520 | tf_op jit(solution)/shard_map/ppermute | solution.py:222
  62.3 2.9 %collective-permute-start.23 = (f32[64,1024]{1,0:T(8,128)S(1)}, f32[64,1024]{1,0:T(8,128)S(1)}, u32[]{:S(2)}, u32[]{:S(2)}) collective-permute-start(f32[64,1024]{1,0:T(8,128)S(1)} %get-tuple-element.120), channel_id=1, source_target_pairs={{0,1},{1,0},{2,3},{3,2},{4,5},{5,4},{6,7},{7,6},{8,9},{9,8},{10,11... | collective-permute-start | bytes 786440 | tf_op jit(solution)/shard_map/ppermute | solution.py:225
  62.3 9.2 %collective-permute-start.24 = (f32[64,1024]{1,0:T(8,128)S(1)}, f32[64,1024]{1,0:T(8,128)S(1)}, u32[]{:S(2)}, u32[]{:S(2)}) collective-permute-start(f32[64,1024]{1,0:T(8,128)S(1)} %get-tuple-element.121), channel_id=1, source_target_pairs={{0,2},{1,3},{2,0},{3,1},{4,6},{5,7},{6,4},{7,5},{8,10},{9,11},{10,... | collective-permute-start | bytes 786440 | tf_op jit(solution)/shard_map/ppermute | solution.py:225
  65.2 11.0 %collective-permute-start.25 = (f32[64,1024]{1,0:T(8,128)S(1)}, f32[64,1024]{1,0:T(8,128)S(1)}, u32[]{:S(2)}, u32[]{:S(2)}) collective-permute-start(f32[64,1024]{1,0:T(8,128)S(1)} %get-tuple-element.122), channel_id=1, source_target_pairs={{0,3},{1,2},{2,1},{3,0},{4,7},{5,6},{6,5},{7,4},{8,11},{9,10},{10,... | collective-permute-start | bytes 786440 | tf_op jit(solution)/shard_map/ppermute | solution.py:225
  76.3 5.1 %collective-permute-start.28 = (bf16[64,1024]{1,0:T(8,128)(2,1)S(1)}, bf16[64,1024]{1,0:T(8,128)(2,1)S(1)}, u32[]{:S(2)}, u32[]{:S(2)}) collective-permute-start(bf16[64,1024]{1,0:T(8,128)(2,1)S(1)} %add_convert_fusion.1.refs_8_), channel_id=1, source_target_pairs={{0,3},{1,2},{2,1},{3,0},{4,7},{5,6},{6,5},{7,4},{8,11},{9,10},{10,... | collective-permute-start | bytes 393224 | tf_op jit(solution)/shard_map/ppermute | solution.py:225
  77.4 7.5 %collective-permute-start.27 = (bf16[64,1024]{1,0:T(8,128)(2,1)S(1)}, bf16[64,1024]{1,0:T(8,128)(2,1)S(1)}, u32[]{:S(2)}, u32[]{:S(2)}) collective-permute-start(bf16[64,1024]{1,0:T(8,128)(2,1)S(1)} %add_convert_fusion.1.refs_8_), channel_id=1, source_target_pairs={{0,2},{1,3},{2,0},{3,1},{4,6},{5,7},{6,4},{7,5},{8,10},{9,11},{10,... | collective-permute-start | bytes 393224 | tf_op jit(solution)/shard_map/ppermute | solution.py:225
  78.6 8.0 %collective-permute-start.26 = (bf16[64,1024]{1,0:T(8,128)(2,1)S(1)}, bf16[64,1024]{1,0:T(8,128)(2,1)S(1)}, u32[]{:S(2)}, u32[]{:S(2)}) collective-permute-start(bf16[64,1024]{1,0:T(8,128)(2,1)S(1)} %add_convert_fusion.1.refs_8_), channel_id=1, source_target_pairs={{0,1},{1,0},{2,3},{3,2},{4,5},{5,4},{6,7},{7,6},{8,9},{9,8},{10,11... | collective-permute-start | bytes 393224 | tf_op jit(solution)/shard_map/ppermute | solution.py:225
  81.4 9.8 %collective-permute-start.31 = (bf16[128,1024]{1,0:T(8,128)(2,1)S(1)}, bf16[128,1024]{1,0:T(8,128)(2,1)S(1)}, u32[]{:S(2)}, u32[]{:S(2)}) collective-permute-start(bf16[128,1024]{1,0:T(8,128)(2,1)S(1)} %collective-permute-done.21.refs_23_), channel_id=1, source_target_pairs={{0,8},{8,16},{16,24},{24,28},{28,20},{20,12},{12,4},{4,0},{1,9},{9... | collective-permute-start | bytes 786440 | tf_op jit(solution)/shard_map/ppermute | solution.py:222
  84.9 7.9 %collective-permute-start.32 = (bf16[128,1024]{1,0:T(8,128)(2,1)S(1)}, bf16[128,1024]{1,0:T(8,128)(2,1)S(1)}, u32[]{:S(2)}, u32[]{:S(2)}) collective-permute-start(bf16[128,1024]{1,0:T(8,128)(2,1)S(1)} %collective-permute-done.22.refs_24_), channel_id=1, source_target_pairs={{8,0},{16,8},{24,16},{28,24},{20,28},{12,20},{4,12},{0,4},{9,1},{1... | collective-permute-start | bytes 786440 | tf_op jit(solution)/shard_map/ppermute | solution.py:222
  89.2 4.1 %collective-permute-start.33 = (f32[64,1024]{1,0:T(8,128)S(1)}, f32[64,1024]{1,0:T(8,128)S(1)}, u32[]{:S(2)}, u32[]{:S(2)}) collective-permute-start(f32[64,1024]{1,0:T(8,128)S(1)} %get-tuple-element.136), channel_id=1, source_target_pairs={{0,1},{1,0},{2,3},{3,2},{4,5},{5,4},{6,7},{7,6},{8,9},{9,8},{10,11... | collective-permute-start | bytes 786440 | tf_op jit(solution)/shard_map/ppermute | solution.py:225
  89.3 9.2 %collective-permute-start.34 = (f32[64,1024]{1,0:T(8,128)S(1)}, f32[64,1024]{1,0:T(8,128)S(1)}, u32[]{:S(2)}, u32[]{:S(2)}) collective-permute-start(f32[64,1024]{1,0:T(8,128)S(1)} %get-tuple-element.137), channel_id=1, source_target_pairs={{0,2},{1,3},{2,0},{3,1},{4,6},{5,7},{6,4},{7,5},{8,10},{9,11},{10,... | collective-permute-start | bytes 786440 | tf_op jit(solution)/shard_map/ppermute | solution.py:225
  90.3 12.9 %collective-permute-start.35 = (f32[64,1024]{1,0:T(8,128)S(1)}, f32[64,1024]{1,0:T(8,128)S(1)}, u32[]{:S(2)}, u32[]{:S(2)}) collective-permute-start(f32[64,1024]{1,0:T(8,128)S(1)} %get-tuple-element.138), channel_id=1, source_target_pairs={{0,3},{1,2},{2,1},{3,0},{4,7},{5,6},{6,5},{7,4},{8,11},{9,10},{10,... | collective-permute-start | bytes 786440 | tf_op jit(solution)/shard_map/ppermute | solution.py:225
  91.2 14.3 %collective-permute-start.40 = (bf16[64,3584]{1,0:T(8,128)(2,1)S(1)}, bf16[64,3584]{1,0:T(8,128)(2,1)S(1)}, u32[]{:S(2)}, u32[]{:S(2)}) collective-permute-start(bf16[64,3584]{1,0:T(8,128)(2,1)S(1)} %slice.13), channel_id=1, source_target_pairs={{8,0},{16,8},{24,16},{28,24},{20,28},{12,20},{4,12},{0,4},{9,1},{1... | collective-permute-start | bytes 1376264 | tf_op jit(solution)/shard_map/ppermute | solution.py:222
  92.8 12.7 %collective-permute-start.39 = (bf16[64,3584]{1,0:T(8,128)(2,1)S(1)}, bf16[64,3584]{1,0:T(8,128)(2,1)S(1)}, u32[]{:S(2)}, u32[]{:S(2)}) collective-permute-start(bf16[64,3584]{1,0:T(8,128)(2,1)S(1)} %slice.12), channel_id=1, source_target_pairs={{0,8},{8,16},{16,24},{24,28},{28,20},{20,12},{12,4},{4,0},{1,9},{9... | collective-permute-start | bytes 1376264 | tf_op jit(solution)/shard_map/ppermute | solution.py:222
  103.3 6.1 %collective-permute-start.38 = (bf16[64,1024]{1,0:T(8,128)(2,1)S(1)}, bf16[64,1024]{1,0:T(8,128)(2,1)S(1)}, u32[]{:S(2)}, u32[]{:S(2)}) collective-permute-start(bf16[64,1024]{1,0:T(8,128)(2,1)S(1)} %add_convert_fusion.refs_12_), channel_id=1, source_target_pairs={{0,3},{1,2},{2,1},{3,0},{4,7},{5,6},{6,5},{7,4},{8,11},{9,10},{10,... | collective-permute-start | bytes 393224 | tf_op jit(solution)/shard_map/ppermute | solution.py:225
  104.4 7.5 %collective-permute-start.37 = (bf16[64,1024]{1,0:T(8,128)(2,1)S(1)}, bf16[64,1024]{1,0:T(8,128)(2,1)S(1)}, u32[]{:S(2)}, u32[]{:S(2)}) collective-permute-start(bf16[64,1024]{1,0:T(8,128)(2,1)S(1)} %add_convert_fusion.refs_12_), channel_id=1, source_target_pairs={{0,2},{1,3},{2,0},{3,1},{4,6},{5,7},{6,4},{7,5},{8,10},{9,11},{10,... | collective-permute-start | bytes 393224 | tf_op jit(solution)/shard_map/ppermute | solution.py:225
  105.5 7.3 %collective-permute-start.36 = (bf16[64,1024]{1,0:T(8,128)(2,1)S(1)}, bf16[64,1024]{1,0:T(8,128)(2,1)S(1)}, u32[]{:S(2)}, u32[]{:S(2)}) collective-permute-start(bf16[64,1024]{1,0:T(8,128)(2,1)S(1)} %add_convert_fusion.refs_12_), channel_id=1, source_target_pairs={{0,1},{1,0},{2,3},{3,2},{4,5},{5,4},{6,7},{7,6},{8,9},{9,8},{10,11... | collective-permute-start | bytes 393224 | tf_op jit(solution)/shard_map/ppermute | solution.py:225
  107.3 6.0 %collective-permute-start.42 = (bf16[64,1024]{1,0:T(8,128)(2,1)S(1)}, bf16[64,1024]{1,0:T(8,128)(2,1)S(1)}, u32[]{:S(2)}, u32[]{:S(2)}) collective-permute-start(bf16[64,1024]{1,0:T(8,128)(2,1)S(1)} %slice.15), channel_id=1, source_target_pairs={{8,0},{16,8},{24,16},{28,24},{20,28},{12,20},{4,12},{0,4},{9,1},{1... | collective-permute-start | bytes 393224 | tf_op jit(solution)/shard_map/ppermute | solution.py:222
  108.9 5.6 %collective-permute-start.41 = (bf16[64,1024]{1,0:T(8,128)(2,1)S(1)}, bf16[64,1024]{1,0:T(8,128)(2,1)S(1)}, u32[]{:S(2)}, u32[]{:S(2)}) collective-permute-start(bf16[64,1024]{1,0:T(8,128)(2,1)S(1)} %slice.14), channel_id=1, source_target_pairs={{0,8},{8,16},{16,24},{24,28},{28,20},{20,12},{12,4},{4,0},{1,9},{9... | collective-permute-start | bytes 393224 | tf_op jit(solution)/shard_map/ppermute | solution.py:222
  109.4 5.1 %collective-permute-start.43 = (f32[32,1024]{1,0:T(8,128)S(1)}, f32[32,1024]{1,0:T(8,128)S(1)}, u32[]{:S(2)}, u32[]{:S(2)}) collective-permute-start(f32[32,1024]{1,0:T(8,128)S(1)} %get-tuple-element.154), channel_id=1, source_target_pairs={{0,1},{1,0},{2,3},{3,2},{4,5},{5,4},{6,7},{7,6},{8,9},{9,8},{10,11... | collective-permute-start | bytes 393224 | tf_op jit(solution)/shard_map/ppermute | solution.py:225
  111.9 6.0 %collective-permute-start.44 = (f32[32,1024]{1,0:T(8,128)S(1)}, f32[32,1024]{1,0:T(8,128)S(1)}, u32[]{:S(2)}, u32[]{:S(2)}) collective-permute-start(f32[32,1024]{1,0:T(8,128)S(1)} %get-tuple-element.155), channel_id=1, source_target_pairs={{0,2},{1,3},{2,0},{3,1},{4,6},{5,7},{6,4},{7,5},{8,10},{9,11},{10,... | collective-permute-start | bytes 393224 | tf_op jit(solution)/shard_map/ppermute | solution.py:225
  112.8 5.8 %collective-permute-start.45 = (f32[32,1024]{1,0:T(8,128)S(1)}, f32[32,1024]{1,0:T(8,128)S(1)}, u32[]{:S(2)}, u32[]{:S(2)}) collective-permute-start(f32[32,1024]{1,0:T(8,128)S(1)} %get-tuple-element.156), channel_id=1, source_target_pairs={{0,3},{1,2},{2,1},{3,0},{4,7},{5,6},{6,5},{7,4},{8,11},{9,10},{10,... | collective-permute-start | bytes 393224 | tf_op jit(solution)/shard_map/ppermute | solution.py:225
  118.7 3.8 %collective-permute-start.48 = (bf16[32,1024]{1,0:T(8,128)(2,1)S(1)}, bf16[32,1024]{1,0:T(8,128)(2,1)S(1)}, u32[]{:S(2)}, u32[]{:S(2)}) collective-permute-start(bf16[32,1024]{1,0:T(8,128)(2,1)S(1)} %add_convert_fusion.3.refs_16_), channel_id=1, source_target_pairs={{0,3},{1,2},{2,1},{3,0},{4,7},{5,6},{6,5},{7,4},{8,11},{9,10},{10,... | collective-permute-start | bytes 196616 | tf_op jit(solution)/shard_map/ppermute | solution.py:225
  120.1 4.5 %collective-permute-start.47 = (bf16[32,1024]{1,0:T(8,128)(2,1)S(1)}, bf16[32,1024]{1,0:T(8,128)(2,1)S(1)}, u32[]{:S(2)}, u32[]{:S(2)}) collective-permute-start(bf16[32,1024]{1,0:T(8,128)(2,1)S(1)} %add_convert_fusion.3.refs_16_), channel_id=1, source_target_pairs={{0,2},{1,3},{2,0},{3,1},{4,6},{5,7},{6,4},{7,5},{8,10},{9,11},{10,... | collective-permute-start | bytes 196616 | tf_op jit(solution)/shard_map/ppermute | solution.py:225
  121.3 3.4 %collective-permute-start.46 = (bf16[32,1024]{1,0:T(8,128)(2,1)S(1)}, bf16[32,1024]{1,0:T(8,128)(2,1)S(1)}, u32[]{:S(2)}, u32[]{:S(2)}) collective-permute-start(bf16[32,1024]{1,0:T(8,128)(2,1)S(1)} %add_convert_fusion.3.refs_16_), channel_id=1, source_target_pairs={{0,1},{1,0},{2,3},{3,2},{4,5},{5,4},{6,7},{7,6},{8,9},{9,8},{10,11... | collective-permute-start | bytes 196616 | tf_op jit(solution)/shard_map/ppermute | solution.py:225
  (7 other events, 82.1 us)
